TPU v7x, 32 devices: a whole 2x2x4 slice. The times are simulated.
32 devices in a mesh: line: 8 (over y, x, core), bus: 4 (over z).
Axes of the slice: x: 2, y: 2, z: 4, core: 2. Of those that a mesh axis runs over, the one named last changes fastest.
Arguments:
- ptdf: bfloat16 [2048, 100352], P('line', 'bus')
- base_injection: float32 [100352], P('bus'), may hold values from -6 to 6
- injection_gain: float32 [100352], P('bus'), may hold values from 0.3 to 3
- factor_of_bus: int32 [100352], P('bus'), may hold values from 0 to 511
- line_rating: int32 [2048], P('line'), may hold values from 60 to 300
- directions: int32 [30, 512], replicated, may hold values from 1 to 1073741823, as said below
- shifts: int32 [8, 512], replicated, may hold values from 0 to 1073741823
- chol_factor: float32 [512, 512], replicated
- proposal_mean: float32 [512], replicated, may hold values from -0.3 to 0.3
Outputs:
- flows: float32 [1024, 2048], P('bus', 'line')
- overload: float32 [1024], P('bus')
- weight: float32 [1024], P('bus')
- new_mean: float32 [512], replicated
Inputs may be any that keep to these rules, and one draw needn't show every extreme that they name: directions[b, f] lies in [2^(29 - b), 2^(30 - b)), as Sobol direction numbers do.
All inputs are finite; a program needn't handle non-finite values.
Results may differ from a plain program's by a relative error of at most 0.0029.
Values sent between devices are 32-bit elements; how exact they have to be, the bound alone decides.
No kernel may reach another device: no remote copies, remote signals or barrier semaphores. Data moves between devices by JAX's collectives and lax.ppermute only.
A program may use at most 64 MiB of HBM per device.

v0:
```python
import math

import jax
import jax.numpy as jnp
from jax import lax
from jax.sharding import PartitionSpec as P

POINTS = 128


SHARP = 8.0
HIGH = lax.Precision.HIGHEST


def normals(directions, shifts, start_row, row_count):
    scenario = start_row + jnp.arange(row_count, dtype=jnp.int32)
    sobol_point = scenario % POINTS
    shift_index = scenario // POINTS
    digits = jnp.zeros((row_count, directions.shape[1]), jnp.int32)
    for bit_index in range(max(1, (POINTS - 1).bit_length())):
        picked = sobol_point >> bit_index & 1
        digits = digits ^ picked[:, None] * directions[bit_index][None, :]
    chosen = (shift_index[:, None] == jnp.arange(shifts.shape[0], dtype=jnp.int32)[None, :]).astype(
        jnp.int32
    )
    offset = jnp.sum(chosen[:, :, None] * shifts[None, :, :], axis=1)
    digits = digits ^ offset
    uniform = (2 * (digits >> 7) + 1).astype(jnp.float32) / 16777216.0
    return math.sqrt(2.0) * lax.erf_inv(2.0 * uniform - 1.0)


def per_device(
    ptdf,
    base_injection,
    injection_gain,
    factor_of_bus,
    line_rating,
    directions,
    shifts,
    chol_factor,
    proposal_mean,
):
    bus_devices = lax.axis_size("bus")
    lines_total = ptdf.shape[0] * lax.axis_size("line")
    scenarios = POINTS * shifts.shape[0]
    block_rows = scenarios // bus_devices
    own_start = lax.axis_index("bus") * block_rows
    factors = lax.dot_general(
        normals(directions, shifts, 0, scenarios) + proposal_mean[None, :],
        chol_factor,
        (((1,), (1,)), ((), ())),
        precision=HIGH,
        preferred_element_type=jnp.float32,
    )
    rating = line_rating.astype(jnp.float32) * 0.01
    block_size = min(block_rows * lax.axis_size("bus"), 128)

    def one_block(index):
        rows = lax.dynamic_slice_in_dim(factors, index * block_size, block_size, 0)
        picked = jnp.take(rows, factor_of_bus, axis=1)
        injections = (base_injection[None, :] + injection_gain[None, :] * picked).astype(
            jnp.bfloat16
        )
        return lax.dot_general(
            injections, ptdf, (((1,), (1,)), ((), ())), preferred_element_type=jnp.float32
        )

    pieces = lax.map(
        one_block, jnp.arange(block_rows * lax.axis_size("bus") // block_size, dtype=jnp.int32)
    )
    flows = lax.psum_scatter(
        pieces.reshape(block_rows * lax.axis_size("bus"), ptdf.shape[0]),
        "bus",
        scatter_dimension=0,
        tiled=True,
    )
    own_normals = normals(directions, shifts, own_start, block_rows)
    likelihood = jnp.exp(
        -jnp.dot(own_normals, proposal_mean, precision=HIGH, preferred_element_type=jnp.float32)
    )
    share = (
        jnp.sum(jax.nn.softplus(SHARP * (jnp.abs(flows) / rating[None, :] - 1.0)), axis=1)
        / SHARP
        / lines_total
    )
    overload = lax.psum(share, "line")
    emphasis = likelihood * overload
    moved_part = jnp.dot(emphasis, own_normals, precision=HIGH, preferred_element_type=jnp.float32)
    moved, total = lax.psum((moved_part, jnp.sum(emphasis)), "bus")
    weight = scenarios * likelihood * overload / total
    new_mean = proposal_mean + moved / total
    return (flows, overload, weight, new_mean)


def solution(mesh):
    return jax.shard_map(
        per_device,
        mesh=mesh,
        in_specs=(P("line", "bus"), P("bus"), P("bus"), P("bus"), P("line"), P(), P(), P(), P()),
        out_specs=(P("bus", "line"), P("bus"), P("bus"), P()),
        check_vma=False,
    )
```

profile of v0, /device:TPU:0, one launch (start us, length us, event | category | flops | bytes accessed | tf_op | source)
XLA Modules:
  0.0 719.6 jit_solution(12117348296411109203)
XLA Ops:
  7.5 1.0 fusion.157
  8.6 7.0 multiply_reduce_fusion
  15.6 9.0 %fusion.11 = f32[1024,512]{0,1:T(8,128)S(1)} fusion(f32[512,512]{1,0:T(8,128)S(1)} %copy-done, s32[1024,512]{1,0:T(8,128)S(1)} %multiply_reduce_fusion, f32[512]{0:T(512)S(1)} %copy-done.20, s32[512]{0:T(512)S(1)} %bitcast.44, s32[1024]{0:T(1024)S(1)} %get-tuple-element.98, s32[512]{0:T(512)S(1)} %bitcast.46, s32[1024]{0:T(1024)S(1)} %get-tuple-element.99, ...), kind=kOutput, calls=%fused_computation.21 | convolution fusion | flops 3252158464 | bytes 5287936 | tf_op jit(solution)/shard_map/dot_general | solution.py:48
  24.8 630.2 %while.10 = (s32[]{:T(128)}, f32[8,128,256]{2,1,0:T(8,128)}, f32[25088]{0:T(1024)}, f32[25088]{0:T(1024)}, s32[25088]{0:T(1024)S(1)}, /*index=5*/s32[8]{0:T(128)...) while((s32[]{:T(128)}, f32[8,128,256]{2,1,0:T(8,128)}, ...), condition=%wide.region_2.3_spmd, body=%wide.region_1.2_spmd.sunk | while | flops 1657263616 | bytes 69672496 | solution.py:68
  25.0 0.7 dynamic_slice.11
  26.8 46.6 %gather_fusion = f32[25088,128]{1,0:T(8,128)} fusion(f32[128,512]{0,1:T(8,128)S(1)} %constant_dynamic-slice_fusion.2, s32[25600]{0:T(1024)S(1)} %pad_clamp_fusion.2), kind=kCustom, calls=%fused_computation.clone.1 | custom fusion | bytes 25790464 | tf_op jit(solution)/shard_map/while/body/eval_jaxpr/jit(_take)/gather | solution.py:60
  73.5 30.3 %fusion.172 = f32[8,128,256]{2,1,0:T(8,128)} fusion(f32[8,128,256]{2,1,0:T(8,128)} %get-tuple-element.172, s32[]{:T(128)S(6)} %copy.20, bf16[256,25088]{1,0:T(8,128)(2,1)} %get-tuple-element.190, f32[25088,128]{1,0:T(8,128)} %gather_fusion, f32[25088]{0:T(1024)} %get-tuple-element.185, f32[25088]{0:T(1024)} %get-tuple-element.186, ...), kind=kOutput, calls=%fused_computation.8.clone.2 | convolution fusion | flops 1657012224 | bytes 26051076 | tf_op jit(solution)/shard_map/while/body/eval_jaxpr/dot_general | solution.py:64
  103.8 0.7 dynamic_slice.11
  105.6 46.6 %gather_fusion = f32[25088,128]{1,0:T(8,128)} fusion(f32[128,512]{0,1:T(8,128)S(1)} %constant_dynamic-slice_fusion.2, s32[25600]{0:T(1024)S(1)} %pad_clamp_fusion.2), kind=kCustom, calls=%fused_computation.clone.1 | custom fusion | bytes 25790464 | tf_op jit(solution)/shard_map/while/body/eval_jaxpr/jit(_take)/gather | solution.py:60
  152.2 30.3 %fusion.172 = f32[8,128,256]{2,1,0:T(8,128)} fusion(f32[8,128,256]{2,1,0:T(8,128)} %get-tuple-element.172, s32[]{:T(128)S(6)} %copy.20, bf16[256,25088]{1,0:T(8,128)(2,1)} %get-tuple-element.190, f32[25088,128]{1,0:T(8,128)} %gather_fusion, f32[25088]{0:T(1024)} %get-tuple-element.185, f32[25088]{0:T(1024)} %get-tuple-element.186, ...), kind=kOutput, calls=%fused_computation.8.clone.2 | convolution fusion | flops 1657012224 | bytes 26051076 | tf_op jit(solution)/shard_map/while/body/eval_jaxpr/dot_general | solution.py:64
  184.3 46.6 %gather_fusion = f32[25088,128]{1,0:T(8,128)} fusion(f32[128,512]{0,1:T(8,128)S(1)} %constant_dynamic-slice_fusion.2, s32[25600]{0:T(1024)S(1)} %pad_clamp_fusion.2), kind=kCustom, calls=%fused_computation.clone.1 | custom fusion | bytes 25790464 | tf_op jit(solution)/shard_map/while/body/eval_jaxpr/jit(_take)/gather | solution.py:60
  231.0 30.3 %fusion.172 = f32[8,128,256]{2,1,0:T(8,128)} fusion(f32[8,128,256]{2,1,0:T(8,128)} %get-tuple-element.172, s32[]{:T(128)S(6)} %copy.20, bf16[256,25088]{1,0:T(8,128)(2,1)} %get-tuple-element.190, f32[25088,128]{1,0:T(8,128)} %gather_fusion, f32[25088]{0:T(1024)} %get-tuple-element.185, f32[25088]{0:T(1024)} %get-tuple-element.186, ...), kind=kOutput, calls=%fused_computation.8.clone.2 | convolution fusion | flops 1657012224 | bytes 26051076 | tf_op jit(solution)/shard_map/while/body/eval_jaxpr/dot_general | solution.py:64
  261.3 0.7 dynamic_slice.11
  263.1 46.6 %gather_fusion = f32[25088,128]{1,0:T(8,128)} fusion(f32[128,512]{0,1:T(8,128)S(1)} %constant_dynamic-slice_fusion.2, s32[25600]{0:T(1024)S(1)} %pad_clamp_fusion.2), kind=kCustom, calls=%fused_computation.clone.1 | custom fusion | bytes 25790464 | tf_op jit(solution)/shard_map/while/body/eval_jaxpr/jit(_take)/gather | solution.py:60
  309.7 30.3 %fusion.172 = f32[8,128,256]{2,1,0:T(8,128)} fusion(f32[8,128,256]{2,1,0:T(8,128)} %get-tuple-element.172, s32[]{:T(128)S(6)} %copy.20, bf16[256,25088]{1,0:T(8,128)(2,1)} %get-tuple-element.190, f32[25088,128]{1,0:T(8,128)} %gather_fusion, f32[25088]{0:T(1024)} %get-tuple-element.185, f32[25088]{0:T(1024)} %get-tuple-element.186, ...), kind=kOutput, calls=%fused_computation.8.clone.2 | convolution fusion | flops 1657012224 | bytes 26051076 | tf_op jit(solution)/shard_map/while/body/eval_jaxpr/dot_general | solution.py:64
  341.8 46.6 %gather_fusion = f32[25088,128]{1,0:T(8,128)} fusion(f32[128,512]{0,1:T(8,128)S(1)} %constant_dynamic-slice_fusion.2, s32[25600]{0:T(1024)S(1)} %pad_clamp_fusion.2), kind=kCustom, calls=%fused_computation.clone.1 | custom fusion | bytes 25790464 | tf_op jit(solution)/shard_map/while/body/eval_jaxpr/jit(_take)/gather | solution.py:60
  388.5 30.3 %fusion.172 = f32[8,128,256]{2,1,0:T(8,128)} fusion(f32[8,128,256]{2,1,0:T(8,128)} %get-tuple-element.172, s32[]{:T(128)S(6)} %copy.20, bf16[256,25088]{1,0:T(8,128)(2,1)} %get-tuple-element.190, f32[25088,128]{1,0:T(8,128)} %gather_fusion, f32[25088]{0:T(1024)} %get-tuple-element.185, f32[25088]{0:T(1024)} %get-tuple-element.186, ...), kind=kOutput, calls=%fused_computation.8.clone.2 | convolution fusion | flops 1657012224 | bytes 26051076 | tf_op jit(solution)/shard_map/while/body/eval_jaxpr/dot_general | solution.py:64
  420.6 46.6 %gather_fusion = f32[25088,128]{1,0:T(8,128)} fusion(f32[128,512]{0,1:T(8,128)S(1)} %constant_dynamic-slice_fusion.2, s32[25600]{0:T(1024)S(1)} %pad_clamp_fusion.2), kind=kCustom, calls=%fused_computation.clone.1 | custom fusion | bytes 25790464 | tf_op jit(solution)/shard_map/while/body/eval_jaxpr/jit(_take)/gather | solution.py:60
  467.2 30.3 %fusion.172 = f32[8,128,256]{2,1,0:T(8,128)} fusion(f32[8,128,256]{2,1,0:T(8,128)} %get-tuple-element.172, s32[]{:T(128)S(6)} %copy.20, bf16[256,25088]{1,0:T(8,128)(2,1)} %get-tuple-element.190, f32[25088,128]{1,0:T(8,128)} %gather_fusion, f32[25088]{0:T(1024)} %get-tuple-element.185, f32[25088]{0:T(1024)} %get-tuple-element.186, ...), kind=kOutput, calls=%fused_computation.8.clone.2 | convolution fusion | flops 1657012224 | bytes 26051076 | tf_op jit(solution)/shard_map/while/body/eval_jaxpr/dot_general | solution.py:64
  499.3 46.6 %gather_fusion = f32[25088,128]{1,0:T(8,128)} fusion(f32[128,512]{0,1:T(8,128)S(1)} %constant_dynamic-slice_fusion.2, s32[25600]{0:T(1024)S(1)} %pad_clamp_fusion.2), kind=kCustom, calls=%fused_computation.clone.1 | custom fusion | bytes 25790464 | tf_op jit(solution)/shard_map/while/body/eval_jaxpr/jit(_take)/gather | solution.py:60
  546.0 30.3 %fusion.172 = f32[8,128,256]{2,1,0:T(8,128)} fusion(f32[8,128,256]{2,1,0:T(8,128)} %get-tuple-element.172, s32[]{:T(128)S(6)} %copy.20, bf16[256,25088]{1,0:T(8,128)(2,1)} %get-tuple-element.190, f32[25088,128]{1,0:T(8,128)} %gather_fusion, f32[25088]{0:T(1024)} %get-tuple-element.185, f32[25088]{0:T(1024)} %get-tuple-element.186, ...), kind=kOutput, calls=%fused_computation.8.clone.2 | convolution fusion | flops 1657012224 | bytes 26051076 | tf_op jit(solution)/shard_map/while/body/eval_jaxpr/dot_general | solution.py:64
  578.1 46.6 %gather_fusion = f32[25088,128]{1,0:T(8,128)} fusion(f32[128,512]{0,1:T(8,128)S(1)} %constant_dynamic-slice_fusion.2, s32[25600]{0:T(1024)S(1)} %pad_clamp_fusion.2), kind=kCustom, calls=%fused_computation.clone.1 | custom fusion | bytes 25790464 | tf_op jit(solution)/shard_map/while/body/eval_jaxpr/jit(_take)/gather | solution.py:60
  624.7 30.3 %fusion.172 = f32[8,128,256]{2,1,0:T(8,128)} fusion(f32[8,128,256]{2,1,0:T(8,128)} %get-tuple-element.172, s32[]{:T(128)S(6)} %copy.20, bf16[256,25088]{1,0:T(8,128)(2,1)} %get-tuple-element.190, f32[25088,128]{1,0:T(8,128)} %gather_fusion, f32[25088]{0:T(1024)} %get-tuple-element.185, f32[25088]{0:T(1024)} %get-tuple-element.186, ...), kind=kOutput, calls=%fused_computation.8.clone.2 | convolution fusion | flops 1657012224 | bytes 26051076 | tf_op jit(solution)/shard_map/while/body/eval_jaxpr/dot_general | solution.py:64
  655.2 1.6 multiply_reduce_fusion.1
  656.9 0.7 convert_multiply_fusion
  657.6 1.5 select_multiply_fusion
  659.6 25.4 %reduce-scatter.2.cloned.1.call-done = f32[256,256]{1,0:T(8,128)} async-done(((f32[1024,256]{1,0:T(8,128)}), f32[256,256]{1,0:T(8,128)}) %reduce-scatter.2.cloned.1.call-update) | async-done | bytes 262160 | tf_op jit(solution)/shard_map/reduce_scatter | solution.py:71
  685.0 1.2 fusion.117
  686.2 13.4 %psum.21 = f32[256]{0:T(256)S(1)} all-reduce(f32[256]{0:T(256)S(1)} %broadcast_multiply_fusion), channel_id=1, replica_groups=mesh['line'=8,'bus'=4] {'line'}, use_global_device_ids=true, to_apply=%region_5.6 | all-reduce | flops 256 | bytes 2048 | tf_op jit(solution)/shard_map/psum | solution.py:86
  700.6 9.8 %all-reduce = (f32[]{:T(128)}, f32[512]{0:T(512)S(1)}) all-reduce(f32[]{:T(128)} %get-tuple-element.89, f32[512]{0:T(512)S(1)} %bitcast.48), channel_id=1, replica_groups=mesh['line'=8,'bus'=4] {'bus'}, use_global_device_ids=true, to_apply=%region_8.9 | all-reduce | flops 513 | bytes 4104 | tf_op jit(solution)/shard_map/psum | solution.py:89
  710.5 1.1 multiply_divide_fusion
  711.6 1.1 divide_add_fusion
  (161 shorter events, 8.8 us)
Async XLA Ops:
  7.2 677.8 %reduce-scatter.2.cloned.1.call-start = ((), (), s32[]{:S(2)}) async-start(), calls=%async_computation.1 | async-start | bytes 1310720 | tf_op jit(solution)/shard_map/reduce_scatter | solution.py:71
  8.5 16.2 %copy-start.6 = (s32[1,512]{1,0:T(1,128)}, s32[1,512]{1,0:T(1,128)S(1)}, u32[]{:S(2)}) copy-start(s32[1,512]{1,0:T(1,128)S(1)} %get-tuple-element.91) | copy-start | bytes 6148
  8.5 16.2 %copy-start.8 = (s32[1,512]{1,0:T(1,128)}, s32[1,512]{1,0:T(1,128)S(1)}, u32[]{:S(2)}) copy-start(s32[1,512]{1,0:T(1,128)S(1)} %get-tuple-element.92) | copy-start | bytes 6148
  8.5 16.2 %copy-start.10 = (s32[1,512]{1,0:T(1,128)}, s32[1,512]{1,0:T(1,128)S(1)}, u32[]{:S(2)}) copy-start(s32[1,512]{1,0:T(1,128)S(1)} %get-tuple-element.93) | copy-start | bytes 6148
  8.5 16.2 %copy-start.12 = (s32[1,512]{1,0:T(1,128)}, s32[1,512]{1,0:T(1,128)S(1)}, u32[]{:S(2)}) copy-start(s32[1,512]{1,0:T(1,128)S(1)} %get-tuple-element.94) | copy-start | bytes 6148
  8.5 16.2 %copy-start.14 = (s32[1,512]{1,0:T(1,128)}, s32[1,512]{1,0:T(1,128)S(1)}, u32[]{:S(2)}) copy-start(s32[1,512]{1,0:T(1,128)S(1)} %get-tuple-element.95) | copy-start | bytes 6148
  8.6 16.2 %copy-start.16 = (s32[1,512]{1,0:T(1,128)}, s32[1,512]{1,0:T(1,128)S(1)}, u32[]{:S(2)}) copy-start(s32[1,512]{1,0:T(1,128)S(1)} %get-tuple-element.96) | copy-start | bytes 6148
  8.6 16.2 %copy-start.18 = (s32[1,512]{1,0:T(1,128)}, s32[1,512]{1,0:T(1,128)S(1)}, u32[]{:S(2)}) copy-start(s32[1,512]{1,0:T(1,128)S(1)} %get-tuple-element.97) | copy-start | bytes 6148
  24.7 630.5 %copy-start.4 = (s32[8,512]{1,0:T(8,128)S(1)}, s32[8,512]{1,0:T(8,128)}, u32[]{:S(2)}) copy-start(s32[8,512]{1,0:T(8,128)} %param.17) | copy-start | bytes 49156
  24.8 632.8 %copy-start.7 = (s32[1,512]{1,0:T(1,128)S(1)}, s32[1,512]{1,0:T(1,128)}, u32[]{:S(2)}) copy-start(s32[1,512]{1,0:T(1,128)} %copy-done.6) | copy-start | bytes 6148
  24.8 632.8 %copy-start.9 = (s32[1,512]{1,0:T(1,128)S(1)}, s32[1,512]{1,0:T(1,128)}, u32[]{:S(2)}) copy-start(s32[1,512]{1,0:T(1,128)} %copy-done.8) | copy-start | bytes 6148
  24.8 632.8 %copy-start.11 = (s32[1,512]{1,0:T(1,128)S(1)}, s32[1,512]{1,0:T(1,128)}, u32[]{:S(2)}) copy-start(s32[1,512]{1,0:T(1,128)} %copy-done.10) | copy-start | bytes 6148
  24.8 632.8 %copy-start.13 = (s32[1,512]{1,0:T(1,128)S(1)}, s32[1,512]{1,0:T(1,128)}, u32[]{:S(2)}) copy-start(s32[1,512]{1,0:T(1,128)} %copy-done.12) | copy-start | bytes 6148
  24.8 632.8 %copy-start.15 = (s32[1,512]{1,0:T(1,128)S(1)}, s32[1,512]{1,0:T(1,128)}, u32[]{:S(2)}) copy-start(s32[1,512]{1,0:T(1,128)} %copy-done.14) | copy-start | bytes 6148
  24.8 632.8 %copy-start.17 = (s32[1,512]{1,0:T(1,128)S(1)}, s32[1,512]{1,0:T(1,128)}, u32[]{:S(2)}) copy-start(s32[1,512]{1,0:T(1,128)} %copy-done.16) | copy-start | bytes 6148
  24.8 632.8 %copy-start.19 = (s32[1,512]{1,0:T(1,128)S(1)}, s32[1,512]{1,0:T(1,128)}, u32[]{:S(2)}) copy-start(s32[1,512]{1,0:T(1,128)} %copy-done.18) | copy-start | bytes 6148
  73.5 30.3 %copy-start.3 = (f32[1024,512]{0,1:T(8,128)S(1)}, f32[1024,512]{0,1:T(8,128)}, u32[]{:S(2)}) copy-start(f32[1024,512]{0,1:T(8,128)} %copy-done.2) | copy-start | bytes 6291460 | tf_op jit(solution)/shard_map/while
  73.5 30.3 %copy-start.23 = (s32[8]{0:T(128)S(1)}, s32[8]{0:T(128)}, u32[]{:S(2)}) copy-start(s32[8]{0:T(128)} %copy-done.22) | copy-start | bytes 100 | tf_op jit(solution)/shard_map/while
  152.2 30.3 %copy-start.3 = (f32[1024,512]{0,1:T(8,128)S(1)}, f32[1024,512]{0,1:T(8,128)}, u32[]{:S(2)}) copy-start(f32[1024,512]{0,1:T(8,128)} %copy-done.2) | copy-start | bytes 6291460 | tf_op jit(solution)/shard_map/while
  152.2 30.3 %copy-start.23 = (s32[8]{0:T(128)S(1)}, s32[8]{0:T(128)}, u32[]{:S(2)}) copy-start(s32[8]{0:T(128)} %copy-done.22) | copy-start | bytes 100 | tf_op jit(solution)/shard_map/while
  231.0 30.3 %copy-start.3 = (f32[1024,512]{0,1:T(8,128)S(1)}, f32[1024,512]{0,1:T(8,128)}, u32[]{:S(2)}) copy-start(f32[1024,512]{0,1:T(8,128)} %copy-done.2) | copy-start | bytes 6291460 | tf_op jit(solution)/shard_map/while
  231.0 30.3 %copy-start.23 = (s32[8]{0:T(128)S(1)}, s32[8]{0:T(128)}, u32[]{:S(2)}) copy-start(s32[8]{0:T(128)} %copy-done.22) | copy-start | bytes 100 | tf_op jit(solution)/shard_map/while
  309.7 30.3 %copy-start.3 = (f32[1024,512]{0,1:T(8,128)S(1)}, f32[1024,512]{0,1:T(8,128)}, u32[]{:S(2)}) copy-start(f32[1024,512]{0,1:T(8,128)} %copy-done.2) | copy-start | bytes 6291460 | tf_op jit(solution)/shard_map/while
  309.7 30.3 %copy-start.23 = (s32[8]{0:T(128)S(1)}, s32[8]{0:T(128)}, u32[]{:S(2)}) copy-start(s32[8]{0:T(128)} %copy-done.22) | copy-start | bytes 100 | tf_op jit(solution)/shard_map/while
  388.4 30.3 %copy-start.3 = (f32[1024,512]{0,1:T(8,128)S(1)}, f32[1024,512]{0,1:T(8,128)}, u32[]{:S(2)}) copy-start(f32[1024,512]{0,1:T(8,128)} %copy-done.2) | copy-start | bytes 6291460 | tf_op jit(solution)/shard_map/while
  388.5 30.3 %copy-start.23 = (s32[8]{0:T(128)S(1)}, s32[8]{0:T(128)}, u32[]{:S(2)}) copy-start(s32[8]{0:T(128)} %copy-done.22) | copy-start | bytes 100 | tf_op jit(solution)/shard_map/while
  467.2 30.3 %copy-start.3 = (f32[1024,512]{0,1:T(8,128)S(1)}, f32[1024,512]{0,1:T(8,128)}, u32[]{:S(2)}) copy-start(f32[1024,512]{0,1:T(8,128)} %copy-done.2) | copy-start | bytes 6291460 | tf_op jit(solution)/shard_map/while
  467.2 30.3 %copy-start.23 = (s32[8]{0:T(128)S(1)}, s32[8]{0:T(128)}, u32[]{:S(2)}) copy-start(s32[8]{0:T(128)} %copy-done.22) | copy-start | bytes 100 | tf_op jit(solution)/shard_map/while
  546.0 30.3 %copy-start.3 = (f32[1024,512]{0,1:T(8,128)S(1)}, f32[1024,512]{0,1:T(8,128)}, u32[]{:S(2)}) copy-start(f32[1024,512]{0,1:T(8,128)} %copy-done.2) | copy-start | bytes 6291460 | tf_op jit(solution)/shard_map/while
  546.0 30.3 %copy-start.23 = (s32[8]{0:T(128)S(1)}, s32[8]{0:T(128)}, u32[]{:S(2)}) copy-start(s32[8]{0:T(128)} %copy-done.22) | copy-start | bytes 100 | tf_op jit(solution)/shard_map/while
  624.7 30.3 %copy-start.3 = (f32[1024,512]{0,1:T(8,128)S(1)}, f32[1024,512]{0,1:T(8,128)}, u32[]{:S(2)}) copy-start(f32[1024,512]{0,1:T(8,128)} %copy-done.2) | copy-start | bytes 6291460 | tf_op jit(solution)/shard_map/while
  624.7 30.3 %copy-start.23 = (s32[8]{0:T(128)S(1)}, s32[8]{0:T(128)}, u32[]{:S(2)}) copy-start(s32[8]{0:T(128)} %copy-done.22) | copy-start | bytes 100 | tf_op jit(solution)/shard_map/while
  (21 other events, 65.8 us)
Sparse Core Ops, SparseCore 0:
  655.2 29.8 reduce-scatter.1
where the time goes:
time: 720 us
  local copies, waits for them, and re-layouts  380 us (53%)
  matrix products  252 us (35%)
  waiting for transfers between devices  25.4 us (4%)
  blocking collectives  23.3 us (3%)
  other arithmetic  18.2 us (3%)
  between operations  14.4 us (2%)
    gather x8, local copies, waits for them, and re-layouts, one_block(): picked = jnp.take(rows, factor_of_bus, axis=1)  373 us
    dot_general x8, matrix products, one_block(): lax.dot_general(injections, ptdf, (((1,), (1,)), ((), ())), preferred_ele...  242 us
    reduce_scatter x1, waiting for transfers between devices, per_device(): lax.psum_scatter(pieces.reshape(block_rows * lax.axis_size('bus'), ptdf.s...  25.4 us
  transfers between devices with their start and end apart: 1, of which 1 were waited for; matrix products, arithmetic and copies ran while one was open for 1% of the time, Pallas kernels for 0%

commit v1 on v0

v1 whole, which is shorter than its diff:
```python
import math

import jax
import jax.numpy as jnp
from jax import lax
from jax.experimental import pallas as pl
from jax.experimental.pallas import tpu as pltpu
from jax.sharding import PartitionSpec as P

POINTS = 128
SHARP = 8.0
HIGH = lax.Precision.HIGHEST
NT = (((1,), (1,)), ((), ()))
LANES = 128
EXTRA = 16


def normals(directions, shifts, start_row, row_count):
    scenario = start_row + jnp.arange(row_count, dtype=jnp.int32)
    sobol_point = scenario % POINTS
    shift_index = scenario // POINTS
    digits = jnp.zeros((row_count, directions.shape[1]), jnp.int32)
    for bit_index in range(max(1, (POINTS - 1).bit_length())):
        picked = sobol_point >> bit_index & 1
        digits = digits ^ picked[:, None] * directions[bit_index][None, :]
    chosen = (shift_index[:, None] == jnp.arange(shifts.shape[0], dtype=jnp.int32)[None, :]).astype(
        jnp.int32
    )
    offset = jnp.sum(chosen[:, :, None] * shifts[None, :, :], axis=1)
    digits = digits ^ offset
    uniform = (2 * (digits >> 7) + 1).astype(jnp.float32) / 16777216.0
    return math.sqrt(2.0) * lax.erf_inv(2.0 * uniform - 1.0)


def block_width(buses):
    for width in (3584, 1792, 896, 512, 256):
        if buses % width == 0:
            return width
    return LANES


def segment_sums(ptdf, base, gain, factor, n_factors):
    lines, buses = ptdf.shape
    width = block_width(buses)
    blocks, rows, per = buses // width, buses // LANES, width // LANES

    def body(p_hbm, b_hbm, g_hbm, f_hbm, out, p_v, b_v, g_v, f_v, p_sem, v_sem):
        vectors = [
            pltpu.make_async_copy(h, v, v_sem.at[i])
            for i, (h, v) in enumerate(((f_hbm, f_v), (g_hbm, g_v), (b_hbm, b_v)))
        ]
        for copy in vectors:
            copy.start()

        def block_copy(k):
            at = pl.ds(pl.multiple_of(k * width, width), width)
            return pltpu.make_async_copy(p_hbm.at[:, at], p_v.at[:, at], p_sem.at[k])

        def start(k, _):
            block_copy(k).start()
            return 0

        lax.fori_loop(0, blocks, start, 0)
        out[...] = jnp.zeros_like(out)
        for copy in vectors:
            copy.wait()

        def step(k, _):
            block_copy(k).wait()

            def row(v):
                return jnp.concatenate([v[pl.ds(k * per + j, 1), :] for j in range(per)], 1)

            g = row(g_v)
            p = p_v[:, pl.ds(pl.multiple_of(k * width, width), width)]
            scaled = (p.astype(jnp.float32) * g).astype(jnp.bfloat16)
            own = lax.broadcasted_iota(jnp.int16, (n_factors, width), 0) == row(f_v).astype(jnp.int16)
            hot = jnp.where(own, jnp.bfloat16(1), jnp.bfloat16(0))
            ratio = row(b_v) / g
            high = ratio.astype(jnp.bfloat16)
            low = (ratio - high.astype(jnp.float32)).astype(jnp.bfloat16)
            rest = jnp.zeros((EXTRA - 2, width), jnp.bfloat16)
            left = jnp.concatenate([hot, high, low, rest], 0)
            out[...] += lax.dot_general(left, scaled, NT, preferred_element_type=jnp.float32)
            return 0

        lax.fori_loop(0, blocks, step, 0)

    hbm = pl.BlockSpec(memory_space=pl.ANY)
    return pl.pallas_call(
        body,
        in_specs=[hbm] * 4,
        out_specs=pl.BlockSpec(memory_space=pltpu.VMEM),
        out_shape=jax.ShapeDtypeStruct((n_factors + EXTRA, lines), jnp.float32),
        scratch_shapes=[
            pltpu.VMEM((lines, buses), jnp.bfloat16),
            pltpu.VMEM((rows, LANES), jnp.float32),
            pltpu.VMEM((rows, LANES), jnp.float32),
            pltpu.VMEM((rows, LANES), jnp.int32),
            pltpu.SemaphoreType.DMA((blocks,)),
            pltpu.SemaphoreType.DMA((3,)),
        ],
        compiler_params=pltpu.CompilerParams(vmem_limit_bytes=48 * 2**20),
        cost_estimate=pl.CostEstimate(
            flops=2 * lines * buses * n_factors, bytes_accessed=2 * lines * buses, transcendentals=0
        ),
        name="segment_sums",
    )(ptdf, base.reshape(rows, LANES), gain.reshape(rows, LANES), factor.reshape(rows, LANES))


def xor_sum(value, axis):
    size = lax.axis_size(axis)
    if size & (size - 1):
        return lax.psum(value, axis)
    bit = 1
    while bit < size:
        value = value + lax.ppermute(value, axis, [(i, i ^ bit) for i in range(size)])
        bit *= 2
    return value


def per_device(
    ptdf,
    base_injection,
    injection_gain,
    factor_of_bus,
    line_rating,
    directions,
    shifts,
    chol_factor,
    proposal_mean,
):
    bus_devices = lax.axis_size("bus")
    lines_total = ptdf.shape[0] * lax.axis_size("line")
    n_factors = directions.shape[1]
    scenarios = POINTS * shifts.shape[0]
    block_rows = scenarios // bus_devices
    z = lax.axis_index("bus")

    sums = segment_sums(ptdf, base_injection, injection_gain, factor_of_bus, n_factors)
    per_factor, base_flow = sums[:n_factors], sums[n_factors] + sums[n_factors + 1]

    def draws(block, count=block_rows):
        return normals(directions, shifts, block * block_rows, count)

    def part(normal):
        factors = lax.dot_general(
            normal + proposal_mean[None, :],
            chol_factor,
            NT,
            precision=lax.Precision.HIGH,
            preferred_element_type=jnp.float32,
        )
        return base_flow[None, :] + jnp.dot(
            factors, per_factor, precision=lax.Precision.HIGH, preferred_element_type=jnp.float32
        )

    own_normals = draws(z)
    if bus_devices == 4:
        near = [(0, 1), (1, 0), (2, 3), (3, 2)]
        across = [(0, 3), (3, 0), (1, 2), (2, 1)]
        pair = part(draws(z ^ 3)) + lax.ppermute(part(draws(z ^ 2)), "bus", near)
        far = lax.ppermute(pair, "bus", across)
        beside = lax.ppermute(part(draws(z ^ 1)), "bus", near)
        flows = part(own_normals) + far + beside
    else:
        flows = lax.psum_scatter(part(draws(0, scenarios)), "bus", scatter_dimension=0, tiled=True)

    rating = line_rating.astype(jnp.float32) * 0.01
    likelihood = jnp.exp(
        -jnp.dot(own_normals, proposal_mean, precision=HIGH, preferred_element_type=jnp.float32)
    )
    share = jnp.sum(jax.nn.softplus(SHARP * (jnp.abs(flows) / rating[None, :] - 1.0)), axis=1)
    overload = xor_sum(share, "line") / SHARP / lines_total
    emphasis = likelihood * overload
    moved_part = jnp.dot(emphasis, own_normals, precision=HIGH, preferred_element_type=jnp.float32)
    sent = jnp.concatenate([moved_part, jnp.full((LANES,), jnp.sum(emphasis))])
    got = xor_sum(sent, "bus")
    moved, total = got[:n_factors], got[n_factors]
    weight = scenarios * likelihood * overload / total
    new_mean = proposal_mean + moved / total
    return (flows, overload, weight, new_mean)


def solution(mesh):
    return jax.shard_map(
        per_device,
        mesh=mesh,
        in_specs=(P("line", "bus"), P("bus"), P("bus"), P("bus"), P("line"), P(), P(), P(), P()),
        out_specs=(P("bus", "line"), P("bus"), P("bus"), P()),
        check_vma=False,
    )
```

time: 720 us -> 69.1 us (0.10)
  local copies, waits for them, and re-layouts: 380 us -> 5.67 us
  matrix products: 252 us -> 9.76 us
  blocking collectives: 23.3 us -> 0 us
  starting transfers between devices: 0.04 us -> 16.4 us
  between operations: 14.4 us -> 0.93 us
  waiting for transfers between devices: 25.4 us -> 14.7 us
  Pallas kernels: 0 us -> 10.3 us
    gather x8 -> x0, local copies, waits for them, and re-layouts: 373 us -> none  [one_block(): picked = jnp.take(rows, factor_of_bus, axis=1)]
    dot_general x9 -> x8, matrix products: 251 us -> 8.9 us  [the longest x4 6.53 us: part(): lax.dot_general(normal + proposal_mean[None, :], chol_factor, NT, precisi...]
    reduce_scatter x1 -> x0, waiting for transfers between devices: 25.4 us -> none  [per_device(): lax.psum_scatter(pieces.reshape(block_rows * lax.axis_size('bus'), ptdf.s...]
    psum x2 -> x0, blocking collectives: 23.3 us -> none  [the longest x1 13.4 us: per_device(): overload = lax.psum(share, 'line')]
    ppermute x0 -> x8, starting transfers between devices: none -> 16.4 us  [the longest x5 9.08 us: xor_sum(): lax.ppermute(value, axis, [(i, i ^ bit) for i in range(size)])]
    ppermute x0 -> x8, waiting for transfers between devices: none -> 14.7 us  [the longest x1 7.35 us: per_device(): far = lax.ppermute(pair, 'bus', across)]
    pallas_call x0 -> x1, Pallas kernels: none -> 10.3 us  [segment_sums(): pl.pallas_call(body, in_specs=[hbm] * 4, out_specs=pl.BlockSpec(memory_sp...]
  transfers between devices with their start and end apart: 1 -> 8, of which waited for: 1 -> 7; matrix products, arithmetic and copies ran while one was open for 1% -> 13% of each run, Pallas kernels for 0% -> 0%
where the time goes in v1:
time: 69.1 us; the launch traced here: 68.8 us
  starting transfers between devices  16.4 us (24%)
  waiting for transfers between devices  14.7 us (21%)
  other arithmetic  11.1 us (16%)
  Pallas kernels  10.3 us (15%)
  matrix products  9.76 us (14%)
  local copies, waits for them, and re-layouts  5.67 us (8%)
  between operations  0.93 us (1%)
    pallas_call x1, Pallas kernels, segment_sums(): pl.pallas_call(body, in_specs=[hbm] * 4, out_specs=pl.BlockSpec(memory_sp...  10.3 us
    ppermute x5, starting transfers between devices, xor_sum(): lax.ppermute(value, axis, [(i, i ^ bit) for i in range(size)])  9.08 us
    ppermute x1, waiting for transfers between devices, per_device(): far = lax.ppermute(pair, 'bus', across)  7.35 us
    ppermute x5, waiting for transfers between devices, xor_sum(): lax.ppermute(value, axis, [(i, i ^ bit) for i in range(size)])  7.1 us
    dot_general x4, matrix products, part(): lax.dot_general(normal + proposal_mean[None, :], chol_factor, NT, precisi...  6.53 us
    reduce_sum x1, other arithmetic, normals(): offset = jnp.sum(chosen[:, :, None] * shifts[None, :, :], axis=1)  5.2 us
    ppermute x1, starting transfers between devices, per_device(): far = lax.ppermute(pair, 'bus', across)  4.15 us
    unnamed x17, local copies, waits for them, and re-layouts  3.54 us
  transfers between devices with their start and end apart: 8, of which 7 were waited for; matrix products, arithmetic and copies ran while one was open for 13% of the time, Pallas kernels for 0%

profile of v1, /device:TPU:0, one launch (start us, length us, event | category | flops | bytes accessed | tf_op | source)
XLA Modules:
  0.0 68.8 jit_solution(16782359939715480639)
XLA Ops:
  1.2 1.0 %fusion.422 = (s32[1,512]{1,0:T(1,128)S(1)}, s32[1,512]{1,0:T(1,128)S(1)}, s32[1,512]{1,0:T(1,128)S(1)}, s32[1,512]{1,0:T(1,128)S(1)}, s32[1,512]{1,0:T(1,128)S(...) fusion(s32[30,512]{1,0:T(8,128)} %param.14), kind=kLoop, calls=%fused_computation.501 | loop fusion | bytes 28672 | tf_op jit(solution)/shard_map/slice | solution.py:25
  2.2 0.9 %copy-done.1 = f32[25088]{0:T(1024)S(1)} copy-done((f32[25088]{0:T(1024)S(1)}, f32[25088]{0:T(1024)}, u32[]{:S(2)}) %copy-start.1) | copy-done | bytes 100376
  3.1 0.9 %copy-done.2 = f32[25088]{0:T(1024)S(1)} copy-done((f32[25088]{0:T(1024)S(1)}, f32[25088]{0:T(1024)}, u32[]{:S(2)}) %copy-start.2) | copy-done | bytes 100376
  4.0 0.9 %copy-done.3 = s32[25088]{0:T(1024)S(1)} copy-done((s32[25088]{0:T(1024)S(1)}, s32[25088]{0:T(1024)}, u32[]{:S(2)}) %copy-start.3) | copy-done | bytes 100376
  4.9 10.3 %segment_sums.1 = f32[528,256]{1,0:T(8,128)S(1)} custom-call(bf16[256,25088]{1,0:T(8,128)(2,1)} %p_hbm.1, f32[196,128]{1,0:T(8,128)S(1)} %bitcast.28, f32[196,128]{1,0:T(8,128)S(1)} %bitcast.29, s32[196,128]{1,0:T(8,128)S(1)} %bitcast.30), custom_call_target="tpu_custom_call" | custom-call | flops 6576668672 | bytes 12845056 | tf_op jit(solution)/shard_map/segment_sums/pallas_call | solution.py:90
  15.2 5.2 %multiply_reduce_fusion.2 = (s32[256,512]{1,0:T(8,128)S(1)}, s32[256,512]{1,0:T(8,128)S(1)}, s32[256,512]{1,0:T(8,128)S(1)}, s32[256,512]{1,0:T(8,128)S(1)}) fusion(s32[256,8]{1,0:T(8,128)S(1)} %fusion.325, s32[8,512]{1,0:T(8,128)S(1)} %copy-done.5, s32[256,8]{1,0:T(8,128)S(1)} %fusion.326, s32[256,8]{1,0:T(8,128)S(1)} %fusion.327, s32[256,8]{1,0:T(8,128)S(1)} %fusion.324), kind=kLoop, calls=%fused_computation.2 | loop fusion | flops 7864320 | bytes 2146304 | tf_op jit(solution)/shard_map/reduce_sum | solution.py:29
  20.4 2.0 %fusion.67 = f32[256,512]{1,0:T(8,128)S(1)} fusion(f32[512,512]{1,0:T(8,128)S(1)} %copy-done, s32[256,512]{1,0:T(8,128)S(1)} %get-tuple-element.13, s32[256]{0:T(256)S(1)} %get-tuple-element.35, s32[256]{0:T(256)S(1)} %get-tuple-element.36, s32[256]{0:T(256)S(1)} %get-tuple-element.37, s32[256]{0:T(256)S(1)} %get-tuple-element.38, ...), kind=kOutput, calls=%fused_computation.79 | convolution fusion | flops 410386432 | bytes 2120704 | tf_op jit(solution)/shard_map/dot_general | solution.py:147
  22.4 0.6 convolution_add_fusion.1
  23.0 3.1 %collective-permute-start = (f32[256,256]{0,1:T(8,128)S(1)}, f32[256,256]{0,1:T(8,128)S(1)}, u32[]{:S(2)}, u32[]{:S(2)}) collective-permute-start(f32[256,256]{0,1:T(8,128)S(1)} %convolution_add_fusion.1), channel_id=1, source_target_pairs={{0,1},{1,0},{2,3},{3,2},{4,5},{5,4},{6,7},{7,6},{8,9},{9,8},{10,11... | collective-permute-start | bytes 786440 | tf_op jit(solution)/shard_map/ppermute | solution.py:162
  26.1 2.0 %fusion.9 = f32[256,512]{1,0:T(8,128)S(1)} fusion(f32[512,512]{1,0:T(8,128)S(1)} %copy-done, s32[256,512]{1,0:T(8,128)S(1)} %get-tuple-element.14, s32[256]{0:T(256)S(1)} %get-tuple-element.43, s32[256]{0:T(256)S(1)} %get-tuple-element.44, s32[256]{0:T(256)S(1)} %get-tuple-element.45, s32[256]{0:T(256)S(1)} %get-tuple-element.46, ...), kind=kOutput, calls=%fused_computation.22 | convolution fusion | flops 410386432 | bytes 2120704 | tf_op jit(solution)/shard_map/dot_general | solution.py:147
  28.1 0.6 convolution_add_fusion
  28.9 2.0 %fusion.125 = f32[256,512]{1,0:T(8,128)S(1)} fusion(f32[512,512]{1,0:T(8,128)S(1)} %copy-done, s32[256,512]{1,0:T(8,128)S(1)} %get-tuple-element.12, s32[256]{0:T(256)S(1)} %get-tuple-element.28, s32[256]{0:T(256)S(1)} %get-tuple-element.29, s32[256]{0:T(256)S(1)} %get-tuple-element.30, s32[256]{0:T(256)S(1)} %get-tuple-element.31, ...), kind=kOutput, calls=%fused_computation.136 | convolution fusion | flops 410386432 | bytes 2120704 | tf_op jit(solution)/shard_map/dot_general | solution.py:147
  30.9 1.5 %select_multiply_fusion = f32[256,512]{1,0:T(8,128)S(1)} fusion(s32[256,512]{1,0:T(8,128)S(1)} %get-tuple-element.15, s32[512]{0:T(512)S(1)} %bitcast.63, s32[256]{0:T(256)S(1)} %get-tuple-element.51, s32[512]{0:T(512)S(1)} %bitcast.67, s32[256]{0:T(256)S(1)} %get-tuple-element.52, s32[512]{0:T(512)S(1)} %bitcast.47, s32[256]{0:T(256)S(1)} %get-tuple-element.53, ...), kind=kLoop, calls=%fused_computation.195 | loop fusion | flops 7602176 | bytes 1070080 | tf_op jit(solution)/shard_map/mul | solution.py:32
  32.3 0.6 fusion.183
  33.2 0.6 fusion
  33.8 4.2 %collective-permute-start.1 = (f32[256,256]{0,1:T(8,128)S(1)}, f32[256,256]{0,1:T(8,128)S(1)}, u32[]{:S(2)}, u32[]{:S(2)}) collective-permute-start(f32[256,256]{0,1:T(8,128)S(1)} %fusion), channel_id=1, source_target_pairs={{0,3},{3,0},{1,2},{2,1},{4,7},{7,4},{5,6},{6,5},{8,11},{11,8},{9,1... | collective-permute-start | bytes 786440 | tf_op jit(solution)/shard_map/ppermute | solution.py:163
  38.6 7.4 %collective-permute-done.1 = f32[256,256]{0,1:T(8,128)S(1)} collective-permute-done((f32[256,256]{0,1:T(8,128)S(1)}, f32[256,256]{0,1:T(8,128)S(1)}, u32[]{:S(2)}, u32[]{:S(2)}) %collective-permute-start.1) | collective-permute-done | bytes 262176 | tf_op jit(solution)/shard_map/ppermute | solution.py:163
  46.3 1.1 %collective-permute-done.3 = f32[256]{0:T(256)S(1)} collective-permute-done((f32[256]{0:T(256)S(1)}, f32[256]{0:T(256)S(1)}, u32[]{:S(2)}, u32[]{:S(2)}) %collective-permute-start.3) | collective-permute-done | bytes 1056 | tf_op jit(solution)/shard_map/ppermute | solution.py:117
  47.4 1.5 %collective-permute-start.4 = (f32[256]{0:T(256)S(1)}, f32[256]{0:T(256)S(1)}, u32[]{:S(2)}, u32[]{:S(2)}) collective-permute-start(f32[256]{0:T(256)S(1)} %add.398), channel_id=1, source_target_pairs={{0,8},{4,12},{8,0},{12,4},{16,24},{20,28},{24,16},{28,20},{1,9},{5... | collective-permute-start | bytes 3080 | tf_op jit(solution)/shard_map/ppermute | solution.py:117
  48.9 2.1 %collective-permute-done.4 = f32[256]{0:T(256)S(1)} collective-permute-done((f32[256]{0:T(256)S(1)}, f32[256]{0:T(256)S(1)}, u32[]{:S(2)}, u32[]{:S(2)}) %collective-permute-start.4) | collective-permute-done | bytes 1056 | tf_op jit(solution)/shard_map/ppermute | solution.py:117
  51.0 1.5 %collective-permute-start.5 = (f32[256]{0:T(256)S(1)}, f32[256]{0:T(256)S(1)}, u32[]{:S(2)}, u32[]{:S(2)}) collective-permute-start(f32[256]{0:T(256)S(1)} %add.399), channel_id=1, source_target_pairs={{0,16},{4,20},{8,24},{12,28},{16,0},{20,4},{24,8},{28,12},{1,17},{... | collective-permute-start | bytes 3080 | tf_op jit(solution)/shard_map/ppermute | solution.py:117
  53.0 1.6 %collective-permute-done.5 = f32[256]{0:T(256)S(1)} collective-permute-done((f32[256]{0:T(256)S(1)}, f32[256]{0:T(256)S(1)}, u32[]{:S(2)}, u32[]{:S(2)}) %collective-permute-start.5) | collective-permute-done | bytes 1056 | tf_op jit(solution)/shard_map/ppermute | solution.py:117
  54.6 0.6 fusion.420
  55.5 0.7 concatenate.3
  56.2 2.9 %collective-permute-start.6 = (f32[640]{0:T(1024)S(1)}, f32[640]{0:T(1024)S(1)}, u32[]{:S(2)}, u32[]{:S(2)}) collective-permute-start(f32[640]{0:T(1024)S(1)} %concatenate.3), channel_id=1, source_target_pairs={{0,1},{1,0},{2,3},{3,2},{4,5},{5,4},{6,7},{7,6},{8,9},{9,8},{10,11... | collective-permute-start | bytes 7688 | tf_op jit(solution)/shard_map/ppermute | solution.py:117
  59.1 1.6 %collective-permute-done.6 = f32[640]{0:T(1024)S(1)} collective-permute-done((f32[640]{0:T(1024)S(1)}, f32[640]{0:T(1024)S(1)}, u32[]{:S(2)}, u32[]{:S(2)}) %collective-permute-start.6) | collective-permute-done | bytes 2592 | tf_op jit(solution)/shard_map/ppermute | solution.py:117
  60.7 0.6 pad_add_fusion
  61.3 3.1 %collective-permute-start.7 = (f32[640]{0:T(1024)S(1)}, f32[640]{0:T(1024)S(1)}, u32[]{:S(2)}, u32[]{:S(2)}) collective-permute-start(f32[640]{0:T(1024)S(1)} %pad_add_fusion), channel_id=1, source_target_pairs={{0,2},{1,3},{2,0},{3,1},{4,6},{5,7},{6,4},{7,5},{8,10},{9,11},{10,... | collective-permute-start | bytes 7688 | tf_op jit(solution)/shard_map/ppermute | solution.py:117
  64.5 0.8 %copy.20 = f32[256,256]{1,0:T(8,128)} copy(f32[256,256]{0,1:T(8,128)S(1)} %get-tuple-element.20) | data formatting | bytes 524288
  65.3 0.8 %collective-permute-done.7 = f32[640]{0:T(1024)S(1)} collective-permute-done((f32[640]{0:T(1024)S(1)}, f32[640]{0:T(1024)S(1)}, u32[]{:S(2)}, u32[]{:S(2)}) %collective-permute-start.7) | collective-permute-done | bytes 2592 | tf_op jit(solution)/shard_map/ppermute | solution.py:117
  66.5 1.1 %divide_add_fusion = f32[512]{0:T(512)} fusion(f32[512]{0:T(512)S(1)} %copy-done.4, f32[640]{0:T(1024)S(1)} %add.402, f32[]{:T(128)} %bitcast.15), kind=kLoop, calls=%fused_computation.345 | loop fusion | flops 1024 | bytes 6148 | tf_op jit(solution)/shard_map/add | solution.py:181
  67.7 1.1 %multiply_divide_fusion = f32[256]{0:T(256)} fusion(f32[256]{0:T(256)S(1)} %get-tuple-element.18, f32[256]{0:T(256)S(1)} %bitcast.39, f32[]{:T(128)} %bitcast.15), kind=kLoop, calls=%fused_computation.367 | loop fusion | flops 1024 | bytes 3076 | tf_op jit(solution)/shard_map/div | solution.py:180
  (48 shorter events, 3.3 us)
Async XLA Ops:
  0.6 19.8 %copy-start = (f32[512,512]{1,0:T(8,128)S(1)}, f32[512,512]{1,0:T(8,128)}, u32[]{:S(2)}) copy-start(f32[512,512]{1,0:T(8,128)} %param.16) | copy-start | bytes 3145732
  2.2 0.9 %copy-start.1 = (f32[25088]{0:T(1024)S(1)}, f32[25088]{0:T(1024)}, u32[]{:S(2)}) copy-start(f32[25088]{0:T(1024)} %param.10) | copy-start | bytes 301060
  3.1 0.9 %copy-start.2 = (f32[25088]{0:T(1024)S(1)}, f32[25088]{0:T(1024)}, u32[]{:S(2)}) copy-start(f32[25088]{0:T(1024)} %param.11) | copy-start | bytes 301060
  4.0 0.9 %copy-start.3 = (s32[25088]{0:T(1024)S(1)}, s32[25088]{0:T(1024)}, u32[]{:S(2)}) copy-start(s32[25088]{0:T(1024)} %param.12) | copy-start | bytes 301060
  4.9 10.3 %copy-start.5 = (s32[8,512]{1,0:T(8,128)S(1)}, s32[8,512]{1,0:T(8,128)}, u32[]{:S(2)}) copy-start(s32[8,512]{1,0:T(8,128)} %param.15) | copy-start | bytes 49156
  4.9 15.5 %copy-start.4 = (f32[512]{0:T(512)S(1)}, f32[512]{0:T(512)}, u32[]{:S(2)}) copy-start(f32[512]{0:T(512)} %param.17) | copy-start | bytes 6148
  23.0 10.2 %collective-permute-start = (f32[256,256]{0,1:T(8,128)S(1)}, f32[256,256]{0,1:T(8,128)S(1)}, u32[]{:S(2)}, u32[]{:S(2)}) collective-permute-start(f32[256,256]{0,1:T(8,128)S(1)} %convolution_add_fusion.1), channel_id=1, source_target_pairs={{0,1},{1,0},{2,3},{3,2},{4,5},{5,4},{6,7},{7,6},{8,9},{9,8},{10,11... | collective-permute-start | bytes 786440 | tf_op jit(solution)/shard_map/ppermute | solution.py:162
  28.7 9.9 %collective-permute-start.2 = (f32[256,256]{0,1:T(8,128)S(1)}, f32[256,256]{0,1:T(8,128)S(1)}, u32[]{:S(2)}, u32[]{:S(2)}) collective-permute-start(f32[256,256]{0,1:T(8,128)S(1)} %convolution_add_fusion), channel_id=1, source_target_pairs={{0,1},{1,0},{2,3},{3,2},{4,5},{5,4},{6,7},{7,6},{8,9},{9,8},{10,11... | collective-permute-start | bytes 786440 | tf_op jit(solution)/shard_map/ppermute | solution.py:164
  30.9 7.1 %copy-start.7 = (s32[256]{0:T(256)S(1)}, s32[256]{0:T(256)}, u32[]{:S(2)}) copy-start(s32[256]{0:T(256)} %param.13) | copy-start | bytes 3076
  33.8 12.1 %collective-permute-start.1 = (f32[256,256]{0,1:T(8,128)S(1)}, f32[256,256]{0,1:T(8,128)S(1)}, u32[]{:S(2)}, u32[]{:S(2)}) collective-permute-start(f32[256,256]{0,1:T(8,128)S(1)} %fusion), channel_id=1, source_target_pairs={{0,3},{3,0},{1,2},{2,1},{4,7},{7,4},{5,6},{6,5},{8,11},{11,8},{9,1... | collective-permute-start | bytes 786440 | tf_op jit(solution)/shard_map/ppermute | solution.py:163
  46.2 1.2 %collective-permute-start.3 = (f32[256]{0:T(256)S(1)}, f32[256]{0:T(256)S(1)}, u32[]{:S(2)}, u32[]{:S(2)}) collective-permute-start(f32[256]{0:T(256)S(1)} %get-tuple-element.19), channel_id=1, source_target_pairs={{0,4},{4,0},{8,12},{12,8},{16,20},{20,16},{24,28},{28,24},{1,5},{5... | collective-permute-start | bytes 3080 | tf_op jit(solution)/shard_map/ppermute | solution.py:117
  47.4 3.6 %collective-permute-start.4 = (f32[256]{0:T(256)S(1)}, f32[256]{0:T(256)S(1)}, u32[]{:S(2)}, u32[]{:S(2)}) collective-permute-start(f32[256]{0:T(256)S(1)} %add.398), channel_id=1, source_target_pairs={{0,8},{4,12},{8,0},{12,4},{16,24},{20,28},{24,16},{28,20},{1,9},{5... | collective-permute-start | bytes 3080 | tf_op jit(solution)/shard_map/ppermute | solution.py:117
  51.0 3.6 %collective-permute-start.5 = (f32[256]{0:T(256)S(1)}, f32[256]{0:T(256)S(1)}, u32[]{:S(2)}, u32[]{:S(2)}) collective-permute-start(f32[256]{0:T(256)S(1)} %add.399), channel_id=1, source_target_pairs={{0,16},{4,20},{8,24},{12,28},{16,0},{20,4},{24,8},{28,12},{1,17},{... | collective-permute-start | bytes 3080 | tf_op jit(solution)/shard_map/ppermute | solution.py:117
  55.2 13.6 %copy-start.6 = (f32[256]{0:T(256)}, f32[256]{0:T(256)S(1)}, u32[]{:S(2)}) copy-start(f32[256]{0:T(256)S(1)} %get-tuple-element.18) | copy-start | bytes 3076
  56.2 4.5 %collective-permute-start.6 = (f32[640]{0:T(1024)S(1)}, f32[640]{0:T(1024)S(1)}, u32[]{:S(2)}, u32[]{:S(2)}) collective-permute-start(f32[640]{0:T(1024)S(1)} %concatenate.3), channel_id=1, source_target_pairs={{0,1},{1,0},{2,3},{3,2},{4,5},{5,4},{6,7},{7,6},{8,9},{9,8},{10,11... | collective-permute-start | bytes 7688 | tf_op jit(solution)/shard_map/ppermute | solution.py:117
  61.3 4.7 %collective-permute-start.7 = (f32[640]{0:T(1024)S(1)}, f32[640]{0:T(1024)S(1)}, u32[]{:S(2)}, u32[]{:S(2)}) collective-permute-start(f32[640]{0:T(1024)S(1)} %pad_add_fusion), channel_id=1, source_target_pairs={{0,2},{1,3},{2,0},{3,1},{4,6},{5,7},{6,4},{7,5},{8,10},{9,11},{10,... | collective-permute-start | bytes 7688 | tf_op jit(solution)/shard_map/ppermute | solution.py:117

commit v2 on v1

v2 whole, which is shorter than its diff:
```python
import math

import jax
import jax.numpy as jnp
from jax import lax
from jax.experimental import pallas as pl
from jax.experimental.pallas import tpu as pltpu
from jax.sharding import PartitionSpec as P

POINTS = 128
SHARP = 8.0
HIGH = lax.Precision.HIGH
HIGHEST = lax.Precision.HIGHEST
NT = (((1,), (1,)), ((), ()))
NN = (((1,), (0,)), ((), ()))
LANES = 128
EXTRA = 16
MIB = 2**20
CENTRAL = (
    2.81022636e-08, 3.43273939e-07, -3.5233877e-06, -4.39150654e-06, 0.00021858087,
    -0.00125372503, -0.00417768164, 0.246640727, 1.50140941,
)
TAIL = (
    -0.000200214257, 0.000100950558, 0.00134934322, -0.00367342844, 0.00573950773,
    -0.0076224613, 0.00943887047, 1.00167406, 2.83297682,
)


def dot(a, b, dims, precision):
    return lax.dot_general(a, b, dims, precision=precision, preferred_element_type=jnp.float32)


def normal_of(digits):
    x = (2 * (digits >> 7) + 1).astype(jnp.float32) * (2.0 / 16777216.0) - 1.0
    w = -jnp.log((1.0 - x) * (1.0 + x))
    central = w < 5.0
    w = jnp.where(central, w - 2.5, jnp.sqrt(w) - 3.0)
    p = jnp.where(central, CENTRAL[0], TAIL[0])
    for a, b in zip(CENTRAL[1:], TAIL[1:]):
        p = jnp.where(central, a, b) + p * w
    return math.sqrt(2.0) * (p * x)


def block_normals(directions, shifts, start, rows):
    group = min(rows, POINTS)
    n = directions.shape[1]
    digits = jnp.zeros((1, n), jnp.int32)
    bits = group.bit_length() - 1
    lead = min(bits, 3)
    at = lax.broadcasted_iota(jnp.int32, (2**lead, n), 0)
    digits = jnp.zeros((2**lead, n), jnp.int32)
    for b in range(lead):
        digits = digits ^ jnp.where((at >> b & 1) == 1, directions[b : b + 1, :], 0)
    for b in range(lead, bits):
        digits = jnp.concatenate([digits, digits ^ directions[b : b + 1, :]], 0)
    pieces = []
    for j in range(rows // group):
        first = start + j * group
        point = lax.rem(first, POINTS)
        flip = shifts[pl.ds(lax.div(first, POINTS), 1), :]
        for b in range(bits, POINTS.bit_length() - 1):
            flip = flip ^ (directions[b : b + 1, :] * (point >> b & 1))
        pieces.append(normal_of(digits ^ flip))
    return jnp.concatenate(pieces, 0) if len(pieces) > 1 else pieces[0]


def block_width(buses):
    for width in (3584, 1792, 896, 512, 256):
        if buses % width == 0:
            return width
    return LANES


def head(blocks, ptdf, base, gain, factor, directions, shifts, chol, mean, block_rows):
    lines, buses = ptdf.shape
    n = directions.shape[1]
    width = block_width(buses)
    steps, rows, per = buses // width, buses // LANES, width // LANES

    def body(
        blocks_s, p_h, b_h, g_h, f_h, d_h, s_h, c_h, m_h,
        sums, part, p_v, b_v, g_v, f_v, d_v, s_v, c_v, m_v, p_sem, v_sem,
    ):
        pairs = ((d_h, d_v), (s_h, s_v), (c_h, c_v), (m_h, m_v), (f_h, f_v), (g_h, g_v), (b_h, b_v))
        small = [pltpu.make_async_copy(h, v, v_sem.at[i]) for i, (h, v) in enumerate(pairs)]
        for copy in small:
            copy.start()

        def block_copy(k):
            at = pl.ds(pl.multiple_of(k * width, width), width)
            return pltpu.make_async_copy(p_h.at[:, at], p_v.at[:, at], p_sem.at[k])

        def start(k, _):
            block_copy(k).start()
            return 0

        lax.fori_loop(0, steps, start, 0)
        sums[...] = jnp.zeros_like(sums)
        for copy in small:
            copy.wait()
        draws = block_normals(d_v, s_v, blocks_s[0] * block_rows, block_rows)
        factors = dot(draws + m_v[...], c_v[...], NT, HIGH)

        def step(k, _):
            block_copy(k).wait()

            def row(v):
                return jnp.concatenate([v[pl.ds(k * per + j, 1), :] for j in range(per)], 1)

            g = row(g_v)
            p = p_v[:, pl.ds(pl.multiple_of(k * width, width), width)]
            scaled = (p.astype(jnp.float32) * g).astype(jnp.bfloat16)
            own = lax.broadcasted_iota(jnp.int16, (n, width), 0) == row(f_v).astype(jnp.int16)
            hot = jnp.where(own, jnp.bfloat16(1), jnp.bfloat16(0))
            ratio = row(b_v) / g
            high = ratio.astype(jnp.bfloat16)
            low = (ratio - high.astype(jnp.float32)).astype(jnp.bfloat16)
            rest = jnp.zeros((EXTRA - 2, width), jnp.bfloat16)
            left = jnp.concatenate([hot, high, low, rest], 0)
            sums[...] += lax.dot_general(left, scaled, NT, preferred_element_type=jnp.float32)
            return 0

        lax.fori_loop(0, steps, step, 0)
        base_row = sums[n : n + 1, :] + sums[n + 1 : n + 2, :]
        part[...] = dot(factors, sums[:n, :], NN, HIGH) + base_row

    hbm = pl.BlockSpec(memory_space=pltpu.HBM)
    vmem = pl.BlockSpec(memory_space=pltpu.VMEM)
    return pl.pallas_call(
        body,
        in_specs=[pl.BlockSpec(memory_space=pltpu.SMEM)] + [hbm] * 8,
        out_specs=[vmem, vmem],
        out_shape=[
            jax.ShapeDtypeStruct((n + EXTRA, lines), jnp.float32),
            jax.ShapeDtypeStruct((block_rows, lines), jnp.float32),
        ],
        scratch_shapes=[
            pltpu.VMEM((lines, buses), jnp.bfloat16),
            pltpu.VMEM((rows, LANES), jnp.float32),
            pltpu.VMEM((rows, LANES), jnp.float32),
            pltpu.VMEM((rows, LANES), jnp.int32),
            pltpu.VMEM(directions.shape, jnp.int32),
            pltpu.VMEM(shifts.shape, jnp.int32),
            pltpu.VMEM(chol.shape, jnp.float32),
            pltpu.VMEM((1, n), jnp.float32),
            pltpu.SemaphoreType.DMA((steps,)),
            pltpu.SemaphoreType.DMA((7,)),
        ],
        compiler_params=pltpu.CompilerParams(vmem_limit_bytes=48 * MIB),
        cost_estimate=pl.CostEstimate(
            flops=2 * lines * buses * n, bytes_accessed=2 * lines * buses, transcendentals=0
        ),
        name="segment_sums",
    )(
        blocks,
        *(
            pltpu.with_memory_space_constraint(x, pltpu.HBM)
            for x in (
                ptdf, base.reshape(rows, LANES), gain.reshape(rows, LANES), factor.reshape(rows, LANES),
                directions, shifts, chol, mean.reshape(1, n),
            )
        ),
    )


def other_parts(blocks, sums, directions, shifts, chol, mean, block_rows):
    n = directions.shape[1]
    lines = sums.shape[1]

    def body(blocks_s, sums_v, d_v, s_v, c_v, m_v, part_1, part_2, part_3, draws, likelihood):
        base_row = sums_v[n : n + 1, :] + sums_v[n + 1 : n + 2, :]
        for i, part in enumerate((part_1, part_2, part_3)):
            draws[...] = block_normals(d_v, s_v, blocks_s[i + 1] * block_rows, block_rows)
            factors = dot(draws[...] + m_v[...], c_v[...], NT, HIGH)
            part[...] = dot(factors, sums_v[:n, :], NN, HIGH) + base_row
        tilt = dot(jnp.broadcast_to(m_v[...], (8, n)), draws[...], NT, HIGHEST)
        likelihood[...] = jnp.exp(-tilt)

    vmem = pl.BlockSpec(memory_space=pltpu.VMEM)
    shapes = [(block_rows, lines)] * 3 + [(block_rows, n), (8, block_rows)]
    return pl.pallas_call(
        body,
        in_specs=[pl.BlockSpec(memory_space=pltpu.SMEM)] + [vmem] * 5,
        out_specs=[vmem] * 5,
        out_shape=[jax.ShapeDtypeStruct(s, jnp.float32) for s in shapes],
        compiler_params=pltpu.CompilerParams(vmem_limit_bytes=32 * MIB),
        cost_estimate=pl.CostEstimate(
            flops=18 * block_rows * n * (n + lines), bytes_accessed=4 * MIB, transcendentals=6 * block_rows * n
        ),
        name="other_parts",
    )(blocks, sums, directions, shifts, chol, mean.reshape(1, n))


def finish_flows(mine, far, beside, rating, draws, likelihood, lines_total):
    rows, lines = mine.shape
    n = draws.shape[1]
    packed_rows = -(-(rows // LANES + n // LANES + 1) // 8) * 8

    def body(mine_v, far_v, beside_v, rating_v, draws_v, like_v, flows, packed):
        value = mine_v[...] + far_v[...] + beside_v[...]
        flows[...] = value
        limit = jnp.concatenate([rating_v[j : j + 1, :] for j in range(lines // LANES)], 1)
        limit = limit.astype(jnp.float32) * 0.01
        over = SHARP * (jnp.abs(value) / limit - 1.0)
        soft = jnp.maximum(over, 0.0) + jnp.log1p(jnp.exp(-jnp.abs(over)))
        share = dot(jnp.ones((8, lines), jnp.float32), soft, NT, HIGHEST) * (1.0 / SHARP / lines_total)
        emphasis = like_v[...] * share
        moved = dot(emphasis, draws_v[...], NN, HIGHEST)
        total = jnp.sum(emphasis[:1, :], axis=1, keepdims=True)
        parts = [share[:1, j * LANES : (j + 1) * LANES] for j in range(rows // LANES)]
        parts += [moved[:1, j * LANES : (j + 1) * LANES] for j in range(n // LANES)]
        parts += [jnp.broadcast_to(total, (1, LANES))]
        parts += [jnp.zeros((1, LANES), jnp.float32)] * (packed_rows - len(parts))
        packed[...] = jnp.concatenate(parts, 0)

    vmem = pl.BlockSpec(memory_space=pltpu.VMEM)
    return pl.pallas_call(
        body,
        in_specs=[vmem] * 6,
        out_specs=[vmem] * 2,
        out_shape=[
            jax.ShapeDtypeStruct((rows, lines), jnp.float32),
            jax.ShapeDtypeStruct((packed_rows, LANES), jnp.float32),
        ],
        compiler_params=pltpu.CompilerParams(vmem_limit_bytes=32 * MIB),
        name="finish_flows",
    )(mine, far, beside, rating.reshape(lines // LANES, LANES), draws, likelihood)


def last_outputs(own, others, likelihood, mean, scenarios):
    rows, n = likelihood.shape[1], mean.shape[0]
    a, b = rows // LANES, n // LANES

    def body(own_v, *refs):
        others_v, (like_v, mean_v, overload, weight, new_mean) = refs[:-5], refs[-5:]
        mine = own_v[...]
        everyone = mine
        for other in others_v:
            everyone = everyone + other[...]
        total = everyone[a + b : a + b + 1, :]
        like = jnp.concatenate([like_v[:1, j * LANES : (j + 1) * LANES] for j in range(a)], 0)
        overload[...] = mine[:a, :]
        weight[...] = scenarios * like * mine[:a, :] / total
        new_mean[...] = mean_v[...] + everyone[a : a + b, :] / total

    vmem = pl.BlockSpec(memory_space=pltpu.VMEM)
    shapes = [(a, LANES), (a, LANES), (b, LANES)]
    out = pl.pallas_call(
        body,
        in_specs=[vmem] * (3 + len(others)),
        out_specs=[vmem] * 3,
        out_shape=[jax.ShapeDtypeStruct(s, jnp.float32) for s in shapes],
        name="last_outputs",
    )(own, *others, likelihood, mean.reshape(b, LANES))
    return [x.reshape(-1) for x in out]


def xor_sum(value, axis):
    size = lax.axis_size(axis)
    if size & (size - 1):
        return lax.psum(value, axis)
    bit = 1
    while bit < size:
        value = value + lax.ppermute(value, axis, [(i, i ^ bit) for i in range(size)])
        bit *= 2
    return value


def normals(directions, shifts):
    point = jnp.arange(POINTS, dtype=jnp.int32)
    digits = jnp.zeros((POINTS, directions.shape[1]), jnp.int32)
    for b in range(POINTS.bit_length() - 1):
        digits = digits ^ (point >> b & 1)[:, None] * directions[b][None, :]
    return normal_of(digits[None, :, :] ^ shifts[:, None, :]).reshape(-1, directions.shape[1])


def per_device(
    ptdf,
    base_injection,
    injection_gain,
    factor_of_bus,
    line_rating,
    directions,
    shifts,
    chol_factor,
    proposal_mean,
):
    bus_devices = lax.axis_size("bus")
    lines_total = ptdf.shape[0] * lax.axis_size("line")
    n = directions.shape[1]
    scenarios = POINTS * shifts.shape[0]
    block_rows = scenarios // bus_devices
    z = lax.axis_index("bus").astype(jnp.int32)
    blocks = jnp.stack([z ^ 2, z ^ 3, z ^ 1, z]) if bus_devices == 4 else jnp.stack([z] * 4)
    drawn = (directions, shifts, chol_factor, proposal_mean)
    sums, first = head(
        blocks, ptdf, base_injection, injection_gain, factor_of_bus, *drawn, block_rows
    )

    if bus_devices == 4:
        near = [(0, 1), (1, 0), (2, 3), (3, 2)]
        across = [(0, 3), (3, 0), (1, 2), (2, 1)]
        from_near = lax.ppermute(first, "bus", near)
        second, third, mine, own_normals, likelihood = other_parts(blocks, sums, *drawn, block_rows)
        far = lax.ppermute(second + from_near, "bus", across)
        beside = lax.ppermute(third, "bus", near)
        flows, packed = finish_flows(
            mine, far, beside, line_rating, own_normals, likelihood, lines_total
        )
        packed = xor_sum(packed, "line")
        others = [
            lax.ppermute(packed, "bus", [(i, i ^ k) for i in range(bus_devices)])
            for k in range(1, bus_devices)
        ]
        overload, weight, new_mean = last_outputs(
            packed, others, likelihood, proposal_mean, scenarios
        )
        return (flows, overload, weight, new_mean)

    draws = normals(directions, shifts)
    factors = dot(draws + proposal_mean[None, :], chol_factor, NT, HIGH)
    part = dot(factors, sums[:n], NN, HIGH) + (sums[n] + sums[n + 1])[None, :]
    flows = lax.psum_scatter(part, "bus", scatter_dimension=0, tiled=True)
    rating = line_rating.astype(jnp.float32) * 0.01
    own_normals = lax.dynamic_slice_in_dim(draws, z * block_rows, block_rows, 0)
    likelihood = jnp.exp(-jnp.dot(own_normals, proposal_mean, precision=HIGHEST))
    share = jnp.sum(jax.nn.softplus(SHARP * (jnp.abs(flows) / rating[None, :] - 1.0)), axis=1)
    overload = lax.psum(share, "line") / SHARP / lines_total
    emphasis = likelihood * overload
    moved_part = jnp.dot(emphasis, own_normals, precision=HIGHEST)
    moved, total = lax.psum((moved_part, jnp.sum(emphasis)), "bus")
    return (flows, overload, scenarios * emphasis / total, proposal_mean + moved / total)


def solution(mesh):
    return jax.shard_map(
        per_device,
        mesh=mesh,
        in_specs=(P("line", "bus"), P("bus"), P("bus"), P("bus"), P("line"), P(), P(), P(), P()),
        out_specs=(P("bus", "line"), P("bus"), P("bus"), P()),
        check_vma=False,
    )
```

time: 69.1 us -> 55.8 us (0.81)
  Pallas kernels: 10.3 us -> 21.3 us
  other arithmetic: 11.1 us -> 0.12 us
  matrix products: 9.76 us -> 0 us
  local copies, waits for them, and re-layouts: 5.67 us -> 0.62 us
  waiting for transfers between devices: 14.7 us -> 18.3 us
  starting transfers between devices: 16.4 us -> 14.6 us
    pallas_call x1 -> x4, Pallas kernels: 10.3 us -> 21.3 us  [the longest x1 12.3 us: head(): pl.pallas_call(body, in_specs=[pl.BlockSpec(memory_space=pltpu.SMEM)] + [...]
    dot_general x10 -> x0, matrix products: 9.76 us -> none  [the longest x4 6.53 us: part(): lax.dot_general(normal + proposal_mean[None, :], chol_factor, NT, precisi...]
    reduce_sum x3 -> x0, other arithmetic: 6.09 us -> none  [the longest x1 5.2 us: normals(): offset = jnp.sum(chosen[:, :, None] * shifts[None, :, :], axis=1)]
    ppermute x5 -> x3, starting transfers between devices: 9.08 us -> 3 us  [xor_sum(): lax.ppermute(value, axis, [(i, i ^ bit) for i in range(size)])]
    ppermute x3 -> x6, waiting for transfers between devices: 7.59 us -> 12.9 us  [the longest x1 7.67 us: per_device(): far = lax.ppermute(second + from_near, 'bus', across)]
    ppermute x3 -> x6, starting transfers between devices: 7.29 us -> 11.6 us  [the longest x3 4.39 us: per_device(): lax.ppermute(packed, 'bus', [(i, i ^ k) for i in range(bus_devices)])]
    unnamed x17 -> x20, local copies, waits for them, and re-layouts: 3.54 us -> 0.62 us
    ppermute x5 -> x3, waiting for transfers between devices: 7.1 us -> 5.38 us  [xor_sum(): lax.ppermute(value, axis, [(i, i ^ bit) for i in range(size)])]
  transfers between devices with their start and end apart: 8 -> 9, of which waited for: 7 -> 8; matrix products, arithmetic and copies ran while one was open for 13% -> 0% of each run, Pallas kernels for 0% -> 11%
where the time goes in v2:
time: 55.8 us; the launch traced here: 55.6 us
  Pallas kernels  21.3 us (38%)
  waiting for transfers between devices  18.3 us (33%)
  starting transfers between devices  14.6 us (26%)
  between operations  0.7 us (1%)
  local copies, waits for them, and re-layouts  0.62 us (1%)
    pallas_call x1, Pallas kernels, head(): pl.pallas_call(body, in_specs=[pl.BlockSpec(memory_space=pltpu.SMEM)] + [...  12.3 us
    ppermute x1, waiting for transfers between devices, per_device(): far = lax.ppermute(second + from_near, 'bus', across)  7.67 us
    pallas_call x1, Pallas kernels, other_parts(): pl.pallas_call(body, in_specs=[pl.BlockSpec(memory_space=pltpu.SMEM)] + [...  6.09 us
    ppermute x3, waiting for transfers between devices, xor_sum(): lax.ppermute(value, axis, [(i, i ^ bit) for i in range(size)])  5.38 us
    ppermute x3, starting transfers between devices, per_device(): lax.ppermute(packed, 'bus', [(i, i ^ k) for i in range(bus_devices)])  4.39 us
    ppermute x1, starting transfers between devices, per_device(): far = lax.ppermute(second + from_near, 'bus', across)  4 us
    ppermute x1, waiting for transfers between devices, per_device(): beside = lax.ppermute(third, 'bus', near)  3.61 us
    ppermute x1, starting transfers between devices, per_device(): from_near = lax.ppermute(first, 'bus', near)  3.07 us
  transfers between devices with their start and end apart: 9, of which 8 were waited for; matrix products, arithmetic and copies ran while one was open for 0% of the time, Pallas kernels for 11%

profile of v2, /device:TPU:0, one launch (start us, length us, event | category | flops | bytes accessed | tf_op | source)
XLA Modules:
  0.0 55.6 jit_solution(9900771022572697507)
XLA Ops:
  0.6 0.0 copy-start.1
  0.6 0.0 copy-start.3
  0.7 0.0 copy-start.5
  0.7 0.0 copy-start.4
  0.7 0.1 pad_add_fusion.blocks_s
  0.8 12.3 %segment_sums.1 = (f32[528,256]{1,0:T(8,128)S(1)}, f32[256,256]{1,0:T(8,128)S(1)}) custom-call(s32[4]{0:T(128)S(1)} %pad_add_fusion.blocks_s, bf16[256,25088]{1,0:T(8,128)(2,1)} %p_h.1, f32[196,128]{1,0:T(8,128)} %bitcast.17, f32[196,128]{1,0:T(8,128)} %bitcast.18, s32[196,128]{1,0:T(8,128)} %bitcast.19, s32[30,512]{1,0:T(8,128)} %d_v.1, s32[8,512]{1,0:T(8,128)} %s_v.1, ...), custom_call_target="tpu_custom_call" | custom-call | flops 6576668672 | bytes 12845056 | tf_op jit(solution)/shard_map/segment_sums/pallas_call | solution.py:129
  13.0 3.1 %collective-permute-start = (f32[256,256]{1,0:T(8,128)S(1)}, f32[256,256]{1,0:T(8,128)S(1)}, u32[]{:S(2)}, u32[]{:S(2)}) collective-permute-start(f32[256,256]{1,0:T(8,128)S(1)} %get-tuple-element.19), channel_id=1, source_target_pairs={{0,1},{1,0},{2,3},{3,2},{4,5},{5,4},{6,7},{7,6},{8,9},{9,8},{10,11... | collective-permute-start | bytes 786440 | tf_op jit(solution)/shard_map/ppermute | solution.py:303
  16.1 0.0 copy-done.3
  16.1 6.1 %other_parts.1 = (f32[256,256]{1,0:T(8,128)S(1)}, f32[256,256]{1,0:T(8,128)S(1)}, f32[256,256]{1,0:T(8,128)S(1)}, f32[256,512]{1,0:T(8,128)S(1)}, f32[8,256]{1,0:T(8,128)S(1)}) custom-call(s32[4]{0:T(128)S(1)} %pad_add_fusion.blocks_s, f32[528,256]{1,0:T(8,128)S(1)} %get-tuple-element.16.sums_v, s32[30,512]{1,0:T(8,128)S(1)} %copy-done.4, ...), custom_call_target="tpu_custom_call" | custom-call | flops 1811939328 | bytes 4194304 | tf_op jit(solution)/shard_map/other_parts/pallas_call | solution.py:181
  22.2 0.1 collective-permute-start.2
  22.3 0.1 collective-permute-done
  22.5 4.0 %collective-permute-start.1 = (f32[256,256]{1,0:T(8,128)S(1)}, f32[256,256]{1,0:T(8,128)S(1)}, u32[]{:S(2)}, u32[]{:S(2)}) collective-permute-start(f32[256,256]{1,0:T(8,128)S(1)} %add.12), channel_id=1, source_target_pairs={{0,3},{3,0},{1,2},{2,1},{4,7},{7,4},{5,6},{6,5},{8,11},{11,8},{9,1... | collective-permute-start | bytes 786440 | tf_op jit(solution)/shard_map/ppermute | solution.py:305
  26.5 3.6 %collective-permute-done.2.beside_v = f32[256,256]{1,0:T(8,128)S(1)} collective-permute-done((f32[256,256]{1,0:T(8,128)S(1)}, f32[256,256]{1,0:T(8,128)S(1)}, u32[]{:S(2)}, u32[]{:S(2)}) %collective-permute-start.2) | collective-permute-done | bytes 262176 | tf_op jit(solution)/shard_map/ppermute | solution.py:306
  30.1 7.7 %collective-permute-done.1.far_v = f32[256,256]{1,0:T(8,128)S(1)} collective-permute-done((f32[256,256]{1,0:T(8,128)S(1)}, f32[256,256]{1,0:T(8,128)S(1)}, u32[]{:S(2)}, u32[]{:S(2)}) %collective-permute-start.1) | collective-permute-done | bytes 262176 | tf_op jit(solution)/shard_map/ppermute | solution.py:305
  37.8 1.6 %finish_flows.1 = (f32[256,256]{1,0:T(8,128)}, f32[8,128]{1,0:T(8,128)S(1)}) custom-call(f32[256,256]{1,0:T(8,128)S(1)} %get-tuple-element.17.mine_v, f32[256,256]{1,0:T(8,128)S(1)} %collective-permute-done.1.far_v, f32[256,256]{1,0:T(8,128)S(1)} %collective-permute-done.2.beside_v, s32[2,128]{1,0:T(2,128)S(1)} %bitcast.16, ...), custom_call_target="tpu_custom_call" | custom-call | tf_op jit(solution)/shard_map/finish_flows/pallas_call | solution.py:217
  39.3 0.0 collective-permute-start.3
  39.3 1.2 %collective-permute-done.3 = f32[8,128]{1,0:T(8,128)S(1)} collective-permute-done((f32[8,128]{1,0:T(8,128)S(1)}, f32[8,128]{1,0:T(8,128)S(1)}, u32[]{:S(2)}, u32[]{:S(2)}) %collective-permute-start.3) | collective-permute-done | bytes 4128 | tf_op jit(solution)/shard_map/ppermute | solution.py:264
  40.5 1.5 %collective-permute-start.4 = (f32[8,128]{1,0:T(8,128)S(1)}, f32[8,128]{1,0:T(8,128)S(1)}, u32[]{:S(2)}, u32[]{:S(2)}) collective-permute-start(f32[8,128]{1,0:T(8,128)S(1)} %add.13), channel_id=1, source_target_pairs={{0,8},{4,12},{8,0},{12,4},{16,24},{20,28},{24,16},{28,20},{1,9},{5... | collective-permute-start | bytes 12296 | tf_op jit(solution)/shard_map/ppermute | solution.py:264
  42.0 2.1 %collective-permute-done.4 = f32[8,128]{1,0:T(8,128)S(1)} collective-permute-done((f32[8,128]{1,0:T(8,128)S(1)}, f32[8,128]{1,0:T(8,128)S(1)}, u32[]{:S(2)}, u32[]{:S(2)}) %collective-permute-start.4) | collective-permute-done | bytes 4128 | tf_op jit(solution)/shard_map/ppermute | solution.py:264
  44.1 1.5 %collective-permute-start.5 = (f32[8,128]{1,0:T(8,128)S(1)}, f32[8,128]{1,0:T(8,128)S(1)}, u32[]{:S(2)}, u32[]{:S(2)}) collective-permute-start(f32[8,128]{1,0:T(8,128)S(1)} %add.14), channel_id=1, source_target_pairs={{0,16},{4,20},{8,24},{12,28},{16,0},{20,4},{24,8},{28,12},{1,17},{... | collective-permute-start | bytes 12296 | tf_op jit(solution)/shard_map/ppermute | solution.py:264
  45.6 2.1 %collective-permute-done.5 = f32[8,128]{1,0:T(8,128)S(1)} collective-permute-done((f32[8,128]{1,0:T(8,128)S(1)}, f32[8,128]{1,0:T(8,128)S(1)}, u32[]{:S(2)}, u32[]{:S(2)}) %collective-permute-start.5) | collective-permute-done | bytes 4128 | tf_op jit(solution)/shard_map/ppermute | solution.py:264
  47.7 0.5 collective-permute-start.8
  48.2 0.5 collective-permute-start.7
  48.6 3.5 %collective-permute-start.6 = (f32[8,128]{1,0:T(8,128)S(1)}, f32[8,128]{1,0:T(8,128)S(1)}, u32[]{:S(2)}, u32[]{:S(2)}) collective-permute-start(f32[8,128]{1,0:T(8,128)S(1)} %add.15.own_v), channel_id=1, source_target_pairs={{0,1},{1,0},{2,3},{3,2},{4,5},{5,4},{6,7},{7,6},{8,9},{9,8},{10,11... | collective-permute-start | bytes 12296 | tf_op jit(solution)/shard_map/ppermute | solution.py:312
  52.1 1.0 %collective-permute-done.8.refs_2_ = f32[8,128]{1,0:T(8,128)S(1)} collective-permute-done((f32[8,128]{1,0:T(8,128)S(1)}, f32[8,128]{1,0:T(8,128)S(1)}, u32[]{:S(2)}, u32[]{:S(2)}) %collective-permute-start.8) | collective-permute-done | bytes 4128 | tf_op jit(solution)/shard_map/ppermute | solution.py:312
  53.1 0.0 collective-permute-done.7.refs_1_
  53.1 0.6 %collective-permute-done.6.refs_0_ = f32[8,128]{1,0:T(8,128)S(1)} collective-permute-done((f32[8,128]{1,0:T(8,128)S(1)}, f32[8,128]{1,0:T(8,128)S(1)}, u32[]{:S(2)}, u32[]{:S(2)}) %collective-permute-start.6) | collective-permute-done | bytes 4128 | tf_op jit(solution)/shard_map/ppermute | solution.py:312
  53.7 0.0 copy-done.6
  53.7 0.0 copy-done.7
  53.7 0.0 copy-done.8
  53.7 0.6 copy-done.9
  54.3 1.3 %last_outputs.1 = (f32[2,128]{1,0:T(2,128)}, f32[2,128]{1,0:T(2,128)}, f32[4,128]{1,0:T(4,128)}) custom-call(f32[8,128]{1,0:T(8,128)} %copy-done.6, f32[8,128]{1,0:T(8,128)} %copy-done.9, f32[8,128]{1,0:T(8,128)} %copy-done.8, f32[8,128]{1,0:T(8,128)} %copy-done.7, f32[8,256]{1,0:T(8,128)} %copy-done, f32[4,128]{1,0:T(4,128)} %bitcast.14), custom_call_target="tpu_custom_call" | custom-call | tf_op jit(solution)/shard_map/last_outputs/pallas_call | solution.py:248
  (15 shorter events, 0.1 us)
Async XLA Ops:
  0.6 15.5 %copy-start.1 = (f32[512]{0:T(512)S(1)}, f32[512]{0:T(512)}, u32[]{:S(2)}) copy-start(f32[512]{0:T(512)} %param.17) | copy-start | bytes 6148
  0.6 15.5 %copy-start.3 = (f32[512,512]{1,0:T(8,128)S(1)}, f32[512,512]{1,0:T(8,128)}, u32[]{:S(2)}) copy-start(f32[512,512]{1,0:T(8,128)} %c_v.1) | copy-start | bytes 3145732
  0.7 15.5 %copy-start.5 = (s32[8,512]{1,0:T(8,128)S(1)}, s32[8,512]{1,0:T(8,128)}, u32[]{:S(2)}) copy-start(s32[8,512]{1,0:T(8,128)} %s_v.1) | copy-start | bytes 49156
  0.7 15.5 %copy-start.4 = (s32[30,512]{1,0:T(8,128)S(1)}, s32[30,512]{1,0:T(8,128)}, u32[]{:S(2)}) copy-start(s32[30,512]{1,0:T(8,128)} %d_v.1) | copy-start | bytes 184324
  0.8 37.0 %copy-start.2 = (s32[256]{0:T(256)S(1)}, s32[256]{0:T(256)}, u32[]{:S(2)}) copy-start(s32[256]{0:T(256)} %param.13) | copy-start | bytes 3076
  13.0 9.4 %collective-permute-start = (f32[256,256]{1,0:T(8,128)S(1)}, f32[256,256]{1,0:T(8,128)S(1)}, u32[]{:S(2)}, u32[]{:S(2)}) collective-permute-start(f32[256,256]{1,0:T(8,128)S(1)} %get-tuple-element.19), channel_id=1, source_target_pairs={{0,1},{1,0},{2,3},{3,2},{4,5},{5,4},{6,7},{7,6},{8,9},{9,8},{10,11... | collective-permute-start | bytes 786440 | tf_op jit(solution)/shard_map/ppermute | solution.py:303
  22.2 31.5 %copy-start = (f32[8,256]{1,0:T(8,128)}, f32[8,256]{1,0:T(8,128)S(1)}, u32[]{:S(2)}) copy-start(f32[8,256]{1,0:T(8,128)S(1)} %get-tuple-element.22.like_v.refs_3_) | copy-start | bytes 24580
  22.2 7.8 %collective-permute-start.2 = (f32[256,256]{1,0:T(8,128)S(1)}, f32[256,256]{1,0:T(8,128)S(1)}, u32[]{:S(2)}, u32[]{:S(2)}) collective-permute-start(f32[256,256]{1,0:T(8,128)S(1)} %get-tuple-element.20), channel_id=1, source_target_pairs={{0,1},{1,0},{2,3},{3,2},{4,5},{5,4},{6,7},{7,6},{8,9},{9,8},{10,11... | collective-permute-start | bytes 786440 | tf_op jit(solution)/shard_map/ppermute | solution.py:306
  22.5 15.3 %collective-permute-start.1 = (f32[256,256]{1,0:T(8,128)S(1)}, f32[256,256]{1,0:T(8,128)S(1)}, u32[]{:S(2)}, u32[]{:S(2)}) collective-permute-start(f32[256,256]{1,0:T(8,128)S(1)} %add.12), channel_id=1, source_target_pairs={{0,3},{3,0},{1,2},{2,1},{4,7},{7,4},{5,6},{6,5},{8,11},{11,8},{9,1... | collective-permute-start | bytes 786440 | tf_op jit(solution)/shard_map/ppermute | solution.py:305
  39.3 1.2 %collective-permute-start.3 = (f32[8,128]{1,0:T(8,128)S(1)}, f32[8,128]{1,0:T(8,128)S(1)}, u32[]{:S(2)}, u32[]{:S(2)}) collective-permute-start(f32[8,128]{1,0:T(8,128)S(1)} %get-tuple-element.24), channel_id=1, source_target_pairs={{0,4},{4,0},{8,12},{12,8},{16,20},{20,16},{24,28},{28,24},{1,5},{5... | collective-permute-start | bytes 12296 | tf_op jit(solution)/shard_map/ppermute | solution.py:264
  40.5 3.6 %collective-permute-start.4 = (f32[8,128]{1,0:T(8,128)S(1)}, f32[8,128]{1,0:T(8,128)S(1)}, u32[]{:S(2)}, u32[]{:S(2)}) collective-permute-start(f32[8,128]{1,0:T(8,128)S(1)} %add.13), channel_id=1, source_target_pairs={{0,8},{4,12},{8,0},{12,4},{16,24},{20,28},{24,16},{28,20},{1,9},{5... | collective-permute-start | bytes 12296 | tf_op jit(solution)/shard_map/ppermute | solution.py:264
  44.1 3.6 %collective-permute-start.5 = (f32[8,128]{1,0:T(8,128)S(1)}, f32[8,128]{1,0:T(8,128)S(1)}, u32[]{:S(2)}, u32[]{:S(2)}) collective-permute-start(f32[8,128]{1,0:T(8,128)S(1)} %add.14), channel_id=1, source_target_pairs={{0,16},{4,20},{8,24},{12,28},{16,0},{20,4},{24,8},{28,12},{1,17},{... | collective-permute-start | bytes 12296 | tf_op jit(solution)/shard_map/ppermute | solution.py:264
  47.7 6.0 %copy-start.6 = (f32[8,128]{1,0:T(8,128)}, f32[8,128]{1,0:T(8,128)S(1)}, u32[]{:S(2)}) copy-start(f32[8,128]{1,0:T(8,128)S(1)} %add.15.own_v) | copy-start | bytes 12292
  47.7 5.4 %collective-permute-start.8 = (f32[8,128]{1,0:T(8,128)S(1)}, f32[8,128]{1,0:T(8,128)S(1)}, u32[]{:S(2)}, u32[]{:S(2)}) collective-permute-start(f32[8,128]{1,0:T(8,128)S(1)} %add.15.own_v), channel_id=1, source_target_pairs={{0,3},{1,2},{2,1},{3,0},{4,7},{5,6},{6,5},{7,4},{8,11},{9,10},{10,... | collective-permute-start | bytes 12296 | tf_op jit(solution)/shard_map/ppermute | solution.py:312
  48.2 5.0 %collective-permute-start.7 = (f32[8,128]{1,0:T(8,128)S(1)}, f32[8,128]{1,0:T(8,128)S(1)}, u32[]{:S(2)}, u32[]{:S(2)}) collective-permute-start(f32[8,128]{1,0:T(8,128)S(1)} %add.15.own_v), channel_id=1, source_target_pairs={{0,2},{1,3},{2,0},{3,1},{4,6},{5,7},{6,4},{7,5},{8,10},{9,11},{10,... | collective-permute-start | bytes 12296 | tf_op jit(solution)/shard_map/ppermute | solution.py:312
  48.6 5.1 %collective-permute-start.6 = (f32[8,128]{1,0:T(8,128)S(1)}, f32[8,128]{1,0:T(8,128)S(1)}, u32[]{:S(2)}, u32[]{:S(2)}) collective-permute-start(f32[8,128]{1,0:T(8,128)S(1)} %add.15.own_v), channel_id=1, source_target_pairs={{0,1},{1,0},{2,3},{3,2},{4,5},{5,4},{6,7},{7,6},{8,9},{9,8},{10,11... | collective-permute-start | bytes 12296 | tf_op jit(solution)/shard_map/ppermute | solution.py:312
  53.1 0.6 %copy-start.7 = (f32[8,128]{1,0:T(8,128)}, f32[8,128]{1,0:T(8,128)S(1)}, u32[]{:S(2)}) copy-start(f32[8,128]{1,0:T(8,128)S(1)} %collective-permute-done.8.refs_2_) | copy-start | bytes 12292
  53.1 0.6 %copy-start.8 = (f32[8,128]{1,0:T(8,128)}, f32[8,128]{1,0:T(8,128)S(1)}, u32[]{:S(2)}) copy-start(f32[8,128]{1,0:T(8,128)S(1)} %collective-permute-done.7.refs_1_) | copy-start | bytes 12292
  53.7 0.6 %copy-start.9 = (f32[8,128]{1,0:T(8,128)}, f32[8,128]{1,0:T(8,128)S(1)}, u32[]{:S(2)}) copy-start(f32[8,128]{1,0:T(8,128)S(1)} %collective-permute-done.6.refs_0_) | copy-start | bytes 12292

commit v3 on v2

--- a/solution.py
+++ b/solution.py
@@ -65,7 +65,7 @@
 
 
 def block_width(buses):
-    for width in (3584, 1792, 896, 512, 256):
+    for width in (6272, 3584, 1792, 896, 512, 256):
         if buses % width == 0:
             return width
     return LANES
@@ -96,9 +96,11 @@
 
         lax.fori_loop(0, steps, start, 0)
         sums[...] = jnp.zeros_like(sums)
-        for copy in small:
+        for copy in small[:2]:
             copy.wait()
         draws = block_normals(d_v, s_v, blocks_s[0] * block_rows, block_rows)
+        for copy in small[2:]:
+            copy.wait()
         factors = dot(draws + m_v[...], c_v[...], NT, HIGH)
 
         def step(k, _):
@@ -163,32 +165,56 @@
     )
 
 
-def other_parts(blocks, sums, directions, shifts, chol, mean, block_rows):
+def middle_parts(blocks, sums, directions, shifts, chol, mean, block_rows):
     n = directions.shape[1]
     lines = sums.shape[1]
 
-    def body(blocks_s, sums_v, d_v, s_v, c_v, m_v, part_1, part_2, part_3, draws, likelihood):
+    def body(blocks_s, sums_v, d_v, s_v, c_v, m_v, part_2, part_1):
         base_row = sums_v[n : n + 1, :] + sums_v[n + 1 : n + 2, :]
-        for i, part in enumerate((part_1, part_2, part_3)):
-            draws[...] = block_normals(d_v, s_v, blocks_s[i + 1] * block_rows, block_rows)
-            factors = dot(draws[...] + m_v[...], c_v[...], NT, HIGH)
+        for i, part in ((2, part_2), (1, part_1)):
+            draws = block_normals(d_v, s_v, blocks_s[i] * block_rows, block_rows)
+            factors = dot(draws + m_v[...], c_v[...], NT, HIGH)
             part[...] = dot(factors, sums_v[:n, :], NN, HIGH) + base_row
+
+    vmem = pl.BlockSpec(memory_space=pltpu.VMEM)
+    return pl.pallas_call(
+        body,
+        in_specs=[pl.BlockSpec(memory_space=pltpu.SMEM)] + [vmem] * 5,
+        out_specs=[vmem] * 2,
+        out_shape=[jax.ShapeDtypeStruct((block_rows, lines), jnp.float32)] * 2,
+        compiler_params=pltpu.CompilerParams(vmem_limit_bytes=32 * MIB),
+        cost_estimate=pl.CostEstimate(
+            flops=12 * block_rows * n * (n + lines), bytes_accessed=3 * MIB, transcendentals=4 * block_rows * n
+        ),
+        name="middle_parts",
+    )(blocks, sums, directions, shifts, chol, mean.reshape(1, n))
+
+
+def own_part(third, blocks, sums, directions, shifts, chol, mean, block_rows):
+    n = directions.shape[1]
+    lines = sums.shape[1]
+
+    def body(third_h, blocks_s, sums_v, d_v, s_v, c_v, m_v, part, draws, likelihood):
+        base_row = sums_v[n : n + 1, :] + sums_v[n + 1 : n + 2, :]
+        draws[...] = block_normals(d_v, s_v, blocks_s[3] * block_rows, block_rows)
+        factors = dot(draws[...] + m_v[...], c_v[...], NT, HIGH)
+        part[...] = dot(factors, sums_v[:n, :], NN, HIGH) + base_row
         tilt = dot(jnp.broadcast_to(m_v[...], (8, n)), draws[...], NT, HIGHEST)
         likelihood[...] = jnp.exp(-tilt)
 
     vmem = pl.BlockSpec(memory_space=pltpu.VMEM)
-    shapes = [(block_rows, lines)] * 3 + [(block_rows, n), (8, block_rows)]
+    shapes = [(block_rows, lines), (block_rows, n), (8, block_rows)]
     return pl.pallas_call(
         body,
-        in_specs=[pl.BlockSpec(memory_space=pltpu.SMEM)] + [vmem] * 5,
-        out_specs=[vmem] * 5,
+        in_specs=[pl.BlockSpec(memory_space=pl.ANY), pl.BlockSpec(memory_space=pltpu.SMEM)] + [vmem] * 5,
+        out_specs=[vmem] * 3,
         out_shape=[jax.ShapeDtypeStruct(s, jnp.float32) for s in shapes],
         compiler_params=pltpu.CompilerParams(vmem_limit_bytes=32 * MIB),
         cost_estimate=pl.CostEstimate(
-            flops=18 * block_rows * n * (n + lines), bytes_accessed=4 * MIB, transcendentals=6 * block_rows * n
+            flops=6 * block_rows * n * (n + lines), bytes_accessed=2 * MIB, transcendentals=2 * block_rows * n
         ),
-        name="other_parts",
-    )(blocks, sums, directions, shifts, chol, mean.reshape(1, n))
+        name="own_part",
+    )(third, blocks, sums, directions, shifts, chol, mean.reshape(1, n))
 
 
 def finish_flows(mine, far, beside, rating, draws, likelihood, lines_total):
@@ -200,12 +226,11 @@
         value = mine_v[...] + far_v[...] + beside_v[...]
         flows[...] = value
         limit = jnp.concatenate([rating_v[j : j + 1, :] for j in range(lines // LANES)], 1)
-        limit = limit.astype(jnp.float32) * 0.01
-        over = SHARP * (jnp.abs(value) / limit - 1.0)
-        soft = jnp.maximum(over, 0.0) + jnp.log1p(jnp.exp(-jnp.abs(over)))
-        share = dot(jnp.ones((8, lines), jnp.float32), soft, NT, HIGHEST) * (1.0 / SHARP / lines_total)
+        over = jnp.abs(value) * (SHARP / (limit.astype(jnp.float32) * 0.01)) - SHARP
+        soft = jnp.maximum(over, 0.0) + jnp.log(1.0 + jnp.exp(-jnp.abs(over)))
+        share = dot(jnp.ones((8, lines), jnp.float32), soft, NT, HIGH) * (1.0 / SHARP / lines_total)
         emphasis = like_v[...] * share
-        moved = dot(emphasis, draws_v[...], NN, HIGHEST)
+        moved = dot(emphasis, draws_v[...], NN, HIGH)
         total = jnp.sum(emphasis[:1, :], axis=1, keepdims=True)
         parts = [share[:1, j * LANES : (j + 1) * LANES] for j in range(rows // LANES)]
         parts += [moved[:1, j * LANES : (j + 1) * LANES] for j in range(n // LANES)]
@@ -227,43 +252,39 @@
     )(mine, far, beside, rating.reshape(lines // LANES, LANES), draws, likelihood)
 
 
-def last_outputs(own, others, likelihood, mean, scenarios):
+def last_outputs(own, half, other, likelihood, mean, scenarios):
     rows, n = likelihood.shape[1], mean.shape[0]
     a, b = rows // LANES, n // LANES
 
-    def body(own_v, *refs):
-        others_v, (like_v, mean_v, overload, weight, new_mean) = refs[:-5], refs[-5:]
-        mine = own_v[...]
-        everyone = mine
-        for other in others_v:
-            everyone = everyone + other[...]
+    def body(own_v, half_v, other_v, like_v, mean_v, overload, weight, new_mean):
+        mine = own_v[:a, :]
+        everyone = half_v[...] + other_v[...]
         total = everyone[a + b : a + b + 1, :]
         like = jnp.concatenate([like_v[:1, j * LANES : (j + 1) * LANES] for j in range(a)], 0)
-        overload[...] = mine[:a, :]
-        weight[...] = scenarios * like * mine[:a, :] / total
+        overload[...] = mine
+        weight[...] = scenarios * like * mine / total
         new_mean[...] = mean_v[...] + everyone[a : a + b, :] / total
 
     vmem = pl.BlockSpec(memory_space=pltpu.VMEM)
     shapes = [(a, LANES), (a, LANES), (b, LANES)]
     out = pl.pallas_call(
         body,
-        in_specs=[vmem] * (3 + len(others)),
+        in_specs=[vmem] * 5,
         out_specs=[vmem] * 3,
         out_shape=[jax.ShapeDtypeStruct(s, jnp.float32) for s in shapes],
         name="last_outputs",
-    )(own, *others, likelihood, mean.reshape(b, LANES))
+    )(own, half, other, likelihood, mean.reshape(b, LANES))
     return [x.reshape(-1) for x in out]
 
 
-def xor_sum(value, axis):
-    size = lax.axis_size(axis)
-    if size & (size - 1):
-        return lax.psum(value, axis)
-    bit = 1
-    while bit < size:
-        value = value + lax.ppermute(value, axis, [(i, i ^ bit) for i in range(size)])
-        bit *= 2
-    return value
+def exchange(value, line_flip, bus_flip):
+    lines, buses = lax.axis_size("line"), lax.axis_size("bus")
+    pairs = [
+        (i * buses + j, (i ^ line_flip) * buses + (j ^ bus_flip))
+        for i in range(lines)
+        for j in range(buses)
+    ]
+    return lax.ppermute(value, ("line", "bus"), pairs)
 
 
 def normals(directions, shifts):
@@ -298,22 +319,22 @@
     )
 
     if bus_devices == 4:
-        near = [(0, 1), (1, 0), (2, 3), (3, 2)]
-        across = [(0, 3), (3, 0), (1, 2), (2, 1)]
-        from_near = lax.ppermute(first, "bus", near)
-        second, third, mine, own_normals, likelihood = other_parts(blocks, sums, *drawn, block_rows)
-        far = lax.ppermute(second + from_near, "bus", across)
-        beside = lax.ppermute(third, "bus", near)
+        from_near = exchange(first, 0, 1)
+        third, second = middle_parts(blocks, sums, *drawn, block_rows)
+        beside = exchange(third, 0, 1)
+        mine, own_normals, likelihood = own_part(third, blocks, sums, *drawn, block_rows)
+        far = exchange(second + from_near, 0, 3)
         flows, packed = finish_flows(
             mine, far, beside, line_rating, own_normals, likelihood, lines_total
         )
-        packed = xor_sum(packed, "line")
-        others = [
-            lax.ppermute(packed, "bus", [(i, i ^ k) for i in range(bus_devices)])
-            for k in range(1, bus_devices)
-        ]
+        packed = packed + exchange(packed, 1, 0)
+        flip = 2
+        while flip < lax.axis_size("line"):
+            packed = packed + exchange(packed, flip + 1, 0)
+            flip *= 2
+        half = packed + exchange(packed, 1, 1)
         overload, weight, new_mean = last_outputs(
-            packed, others, likelihood, proposal_mean, scenarios
+            packed, half, exchange(half, 1, 2), likelihood, proposal_mean, scenarios
         )
         return (flows, overload, weight, new_mean)
 

time: 55.8 us -> 52.9 us (0.948)
  waiting for transfers between devices: 18.3 us -> 17.1 us
  starting transfers between devices: 14.6 us -> 13.5 us
    ppermute x9 -> x8, waiting for transfers between devices: 18.3 us -> 17.1 us  [exchange(): return lax.ppermute(value, ('line', 'bus'), pairs)]
    ppermute x9 -> x8, starting transfers between devices: 14.6 us -> 13.5 us  [exchange(): return lax.ppermute(value, ('line', 'bus'), pairs)]
    pallas_call x2 -> x3, Pallas kernels: 7.4 us -> 7.82 us  [the longest x1 3.93 us: middle_parts(): pl.pallas_call(body, in_specs=[pl.BlockSpec(memory_space=pltpu.SMEM)] + [...]
  transfers between devices with their start and end apart: 9 -> 8, of which waited for: 8 -> 7; matrix products, arithmetic and copies ran while one was open for 0% -> 0% of each run, Pallas kernels for 11% -> 12%
where the time goes in v3:
time: 52.9 us; the launch traced here: 52.8 us
  Pallas kernels  20.8 us (39%)
  waiting for transfers between devices  17.1 us (32%)
  starting transfers between devices  13.5 us (26%)
  between operations  0.72 us (1%)
  local copies, waits for them, and re-layouts  0.62 us (1%)
    ppermute x8, waiting for transfers between devices, exchange(): return lax.ppermute(value, ('line', 'bus'), pairs)  17.1 us
    ppermute x8, starting transfers between devices, exchange(): return lax.ppermute(value, ('line', 'bus'), pairs)  13.5 us
    pallas_call x1, Pallas kernels, head(): pl.pallas_call(body, in_specs=[pl.BlockSpec(memory_space=pltpu.SMEM)] + [...  11.8 us
    pallas_call x1, Pallas kernels, middle_parts(): pl.pallas_call(body, in_specs=[pl.BlockSpec(memory_space=pltpu.SMEM)] + [...  3.93 us
    pallas_call x1, Pallas kernels, own_part(): pl.pallas_call(body, in_specs=[pl.BlockSpec(memory_space=pl.ANY), pl.Bloc...  2.59 us
    pallas_call x1, Pallas kernels, last_outputs(): pl.pallas_call(body, in_specs=[vmem] * 5, out_specs=[vmem] * 3, out_shape...  1.3 us
    pallas_call x1, Pallas kernels, finish_flows(): pl.pallas_call(body, in_specs=[vmem] * 6, out_specs=[vmem] * 2, out_shape...  1.19 us
  transfers between devices with their start and end apart: 8, of which 7 were waited for; matrix products, arithmetic and copies ran while one was open for 0% of the time, Pallas kernels for 12%

profile of v3, /device:TPU:0, one launch (start us, length us, event | category | flops | bytes accessed | tf_op | source)
XLA Modules:
  0.0 52.8 jit_solution(11802482459527300407)
XLA Ops:
  0.6 0.0 copy-start.3
  0.6 0.0 copy-start.5
  0.7 0.0 copy-start.4
  0.7 0.0 copy-start.1
  0.7 0.1 pad_add_fusion.blocks_s
  0.8 11.8 %segment_sums.1 = (f32[528,256]{1,0:T(8,128)S(1)}, f32[256,256]{1,0:T(8,128)S(1)}) custom-call(s32[4]{0:T(128)S(1)} %pad_add_fusion.blocks_s, bf16[256,25088]{1,0:T(8,128)(2,1)} %p_h.1, f32[196,128]{1,0:T(8,128)} %bitcast.18, f32[196,128]{1,0:T(8,128)} %bitcast.19, s32[196,128]{1,0:T(8,128)} %bitcast.20, s32[30,512]{1,0:T(8,128)} %d_v.3, s32[8,512]{1,0:T(8,128)} %s_v.3, ...), custom_call_target="tpu_custom_call" | custom-call | flops 6576668672 | bytes 12845056 | tf_op jit(solution)/shard_map/segment_sums/pallas_call | solution.py:131
  12.5 3.1 %collective-permute-start = (f32[256,256]{1,0:T(8,128)S(1)}, f32[256,256]{1,0:T(8,128)S(1)}, u32[]{:S(2)}, u32[]{:S(2)}) collective-permute-start(f32[256,256]{1,0:T(8,128)S(1)} %get-tuple-element.20), channel_id=1, source_target_pairs={{0,1},{1,0},{2,3},{3,2},{4,5},{5,4},{6,7},{7,6},{8,9},{9,8},{10,11... | collective-permute-start | bytes 786440 | tf_op jit(solution)/shard_map/ppermute | solution.py:287
  15.6 0.0 copy-done.3
  15.6 0.0 copy-done.5
  15.6 0.0 copy-done.4
  15.6 0.0 copy-done.1
  15.6 3.9 %middle_parts.1 = (f32[256,256]{1,0:T(8,128)S(1)}, f32[256,256]{1,0:T(8,128)S(1)}) custom-call(s32[4]{0:T(128)S(1)} %pad_add_fusion.blocks_s, f32[528,256]{1,0:T(8,128)S(1)} %get-tuple-element.16.sums_v, s32[30,512]{1,0:T(8,128)S(1)} %copy-done.4, s32[8,512]{1,0:T(8,128)S(1)} %copy-done.5, f32[512,512]{1,0:T(8,128)S(1)} %copy-done.3, f32[1,512]{1,0:T(1,128)S(1)} %bitcast.15), custom_call_target="tpu_custom_call" | custom-call | flops 1207959552 | bytes 3145728 | tf_op jit(solution)/shard_map/middle_parts/pallas_call | solution.py:180
  19.6 0.1 collective-permute-start.2
  19.7 2.6 %collective-permute-done = f32[256,256]{1,0:T(8,128)S(1)} collective-permute-done((f32[256,256]{1,0:T(8,128)S(1)}, f32[256,256]{1,0:T(8,128)S(1)}, u32[]{:S(2)}, u32[]{:S(2)}) %collective-permute-start) | collective-permute-done | bytes 262176 | tf_op jit(solution)/shard_map/ppermute | solution.py:287
  22.4 4.6 %collective-permute-start.1 = (f32[256,256]{1,0:T(8,128)S(1)}, f32[256,256]{1,0:T(8,128)S(1)}, u32[]{:S(2)}, u32[]{:S(2)}) collective-permute-start(f32[256,256]{1,0:T(8,128)S(1)} %add.15), channel_id=1, source_target_pairs={{0,3},{1,2},{2,1},{3,0},{4,7},{5,6},{6,5},{7,4},{8,11},{9,10},{10,... | collective-permute-start | bytes 786440 | tf_op jit(solution)/shard_map/ppermute | solution.py:287
  27.0 2.6 %own_part.1 = (f32[256,256]{1,0:T(8,128)S(1)}, f32[256,512]{1,0:T(8,128)S(1)}, f32[8,256]{1,0:T(8,128)S(1)}) custom-call(f32[256,256]{1,0:T(8,128)S(1)} %get-tuple-element.17.third_h, s32[4]{0:T(128)S(1)} %pad_add_fusion.blocks_s, f32[528,256]{1,0:T(8,128)S(1)} %get-tuple-element.16.sums_v, s32[30,512]{1,0:T(8,128)S(1)} %copy-done.4, ...), custom_call_target="tpu_custom_call" | custom-call | flops 603979776 | bytes 2097152 | tf_op jit(solution)/shard_map/own_part/pallas_call | solution.py:207
  29.5 0.0 collective-permute-done.2.beside_v
  29.6 5.9 %collective-permute-done.1.far_v = f32[256,256]{1,0:T(8,128)S(1)} collective-permute-done((f32[256,256]{1,0:T(8,128)S(1)}, f32[256,256]{1,0:T(8,128)S(1)}, u32[]{:S(2)}, u32[]{:S(2)}) %collective-permute-start.1) | collective-permute-done | bytes 262176 | tf_op jit(solution)/shard_map/ppermute | solution.py:287
  35.5 0.0 copy-done.2
  35.5 1.2 %finish_flows.1 = (f32[256,256]{1,0:T(8,128)}, f32[8,128]{1,0:T(8,128)S(1)}) custom-call(f32[256,256]{1,0:T(8,128)S(1)} %get-tuple-element.18.mine_v, f32[256,256]{1,0:T(8,128)S(1)} %collective-permute-done.1.far_v, f32[256,256]{1,0:T(8,128)S(1)} %collective-permute-done.2.beside_v, s32[2,128]{1,0:T(2,128)S(1)} %bitcast.17, ...), custom_call_target="tpu_custom_call" | custom-call | tf_op jit(solution)/shard_map/finish_flows/pallas_call | solution.py:242
  36.7 0.0 collective-permute-start.3
  36.7 1.2 %collective-permute-done.3 = f32[8,128]{1,0:T(8,128)S(1)} collective-permute-done((f32[8,128]{1,0:T(8,128)S(1)}, f32[8,128]{1,0:T(8,128)S(1)}, u32[]{:S(2)}, u32[]{:S(2)}) %collective-permute-start.3) | collective-permute-done | bytes 4128 | tf_op jit(solution)/shard_map/ppermute | solution.py:287
  37.8 1.3 %collective-permute-start.4 = (f32[8,128]{1,0:T(8,128)S(1)}, f32[8,128]{1,0:T(8,128)S(1)}, u32[]{:S(2)}, u32[]{:S(2)}) collective-permute-start(f32[8,128]{1,0:T(8,128)S(1)} %add.16), channel_id=1, source_target_pairs={{0,12},{1,13},{2,14},{3,15},{4,8},{5,9},{6,10},{7,11},{8,4},{9,5},... | collective-permute-start | bytes 12296 | tf_op jit(solution)/shard_map/ppermute | solution.py:287
  39.1 1.8 %collective-permute-done.4 = f32[8,128]{1,0:T(8,128)S(1)} collective-permute-done((f32[8,128]{1,0:T(8,128)S(1)}, f32[8,128]{1,0:T(8,128)S(1)}, u32[]{:S(2)}, u32[]{:S(2)}) %collective-permute-start.4) | collective-permute-done | bytes 4128 | tf_op jit(solution)/shard_map/ppermute | solution.py:287
  40.9 1.3 %collective-permute-start.5 = (f32[8,128]{1,0:T(8,128)S(1)}, f32[8,128]{1,0:T(8,128)S(1)}, u32[]{:S(2)}, u32[]{:S(2)}) collective-permute-start(f32[8,128]{1,0:T(8,128)S(1)} %add.17), channel_id=1, source_target_pairs={{0,20},{1,21},{2,22},{3,23},{4,16},{5,17},{6,18},{7,19},{8,28},{9,... | collective-permute-start | bytes 12296 | tf_op jit(solution)/shard_map/ppermute | solution.py:287
  42.2 1.7 %collective-permute-done.5 = f32[8,128]{1,0:T(8,128)S(1)} collective-permute-done((f32[8,128]{1,0:T(8,128)S(1)}, f32[8,128]{1,0:T(8,128)S(1)}, u32[]{:S(2)}, u32[]{:S(2)}) %collective-permute-start.5) | collective-permute-done | bytes 4128 | tf_op jit(solution)/shard_map/ppermute | solution.py:287
  43.9 1.2 %collective-permute-start.6 = (f32[8,128]{1,0:T(8,128)S(1)}, f32[8,128]{1,0:T(8,128)S(1)}, u32[]{:S(2)}, u32[]{:S(2)}) collective-permute-start(f32[8,128]{1,0:T(8,128)S(1)} %add.18.own_v), channel_id=1, source_target_pairs={{0,5},{1,4},{2,7},{3,6},{4,1},{5,0},{6,3},{7,2},{8,13},{9,12},{10,... | collective-permute-start | bytes 12296 | tf_op jit(solution)/shard_map/ppermute | solution.py:287
  45.1 1.8 %collective-permute-done.6 = f32[8,128]{1,0:T(8,128)S(1)} collective-permute-done((f32[8,128]{1,0:T(8,128)S(1)}, f32[8,128]{1,0:T(8,128)S(1)}, u32[]{:S(2)}, u32[]{:S(2)}) %collective-permute-start.6) | collective-permute-done | bytes 4128 | tf_op jit(solution)/shard_map/ppermute | solution.py:287
  46.9 1.9 %collective-permute-start.7 = (f32[8,128]{1,0:T(8,128)S(1)}, f32[8,128]{1,0:T(8,128)S(1)}, u32[]{:S(2)}, u32[]{:S(2)}) collective-permute-start(f32[8,128]{1,0:T(8,128)S(1)} %add.19.half_v), channel_id=1, source_target_pairs={{0,6},{1,7},{2,4},{3,5},{4,2},{5,3},{6,0},{7,1},{8,14},{9,15},{10,... | collective-permute-start | bytes 12296 | tf_op jit(solution)/shard_map/ppermute | solution.py:287
  48.8 2.0 %collective-permute-done.7.other_v = f32[8,128]{1,0:T(8,128)S(1)} collective-permute-done((f32[8,128]{1,0:T(8,128)S(1)}, f32[8,128]{1,0:T(8,128)S(1)}, u32[]{:S(2)}, u32[]{:S(2)}) %collective-permute-start.7) | collective-permute-done | bytes 4128 | tf_op jit(solution)/shard_map/ppermute | solution.py:287
  50.9 0.6 %copy-done.8 = f32[8,128]{1,0:T(8,128)} copy-done((f32[8,128]{1,0:T(8,128)}, f32[8,128]{1,0:T(8,128)S(1)}, u32[]{:S(2)}) %copy-start.8) | copy-done | bytes 4120
  51.5 1.3 %last_outputs.1 = (f32[2,128]{1,0:T(2,128)}, f32[2,128]{1,0:T(2,128)}, f32[4,128]{1,0:T(4,128)}) custom-call(f32[8,128]{1,0:T(8,128)} %copy-done.6, f32[8,128]{1,0:T(8,128)} %copy-done.7, f32[8,128]{1,0:T(8,128)} %copy-done.8, f32[8,256]{1,0:T(8,128)} %copy-done, f32[4,128]{1,0:T(4,128)} %bitcast.14), custom_call_target="tpu_custom_call" | custom-call | tf_op jit(solution)/shard_map/last_outputs/pallas_call | solution.py:270
  (13 shorter events, 0.1 us)
Async XLA Ops:
  0.6 15.0 %copy-start.3 = (f32[512,512]{1,0:T(8,128)S(1)}, f32[512,512]{1,0:T(8,128)}, u32[]{:S(2)}) copy-start(f32[512,512]{1,0:T(8,128)} %c_v.3) | copy-start | bytes 3145732
  0.6 15.0 %copy-start.5 = (s32[8,512]{1,0:T(8,128)S(1)}, s32[8,512]{1,0:T(8,128)}, u32[]{:S(2)}) copy-start(s32[8,512]{1,0:T(8,128)} %s_v.3) | copy-start | bytes 49156
  0.7 15.0 %copy-start.4 = (s32[30,512]{1,0:T(8,128)S(1)}, s32[30,512]{1,0:T(8,128)}, u32[]{:S(2)}) copy-start(s32[30,512]{1,0:T(8,128)} %d_v.3) | copy-start | bytes 184324
  0.7 15.0 %copy-start.1 = (f32[512]{0:T(512)S(1)}, f32[512]{0:T(512)}, u32[]{:S(2)}) copy-start(f32[512]{0:T(512)} %param.17) | copy-start | bytes 6148
  0.8 34.7 %copy-start.2 = (s32[256]{0:T(256)S(1)}, s32[256]{0:T(256)}, u32[]{:S(2)}) copy-start(s32[256]{0:T(256)} %param.13) | copy-start | bytes 3076
  12.5 9.8 %collective-permute-start = (f32[256,256]{1,0:T(8,128)S(1)}, f32[256,256]{1,0:T(8,128)S(1)}, u32[]{:S(2)}, u32[]{:S(2)}) collective-permute-start(f32[256,256]{1,0:T(8,128)S(1)} %get-tuple-element.20), channel_id=1, source_target_pairs={{0,1},{1,0},{2,3},{3,2},{4,5},{5,4},{6,7},{7,6},{8,9},{9,8},{10,11... | collective-permute-start | bytes 786440 | tf_op jit(solution)/shard_map/ppermute | solution.py:287
  19.6 10.0 %collective-permute-start.2 = (f32[256,256]{1,0:T(8,128)S(1)}, f32[256,256]{1,0:T(8,128)S(1)}, u32[]{:S(2)}, u32[]{:S(2)}) collective-permute-start(f32[256,256]{1,0:T(8,128)S(1)} %get-tuple-element.17.third_h), channel_id=1, source_target_pairs={{0,1},{1,0},{2,3},{3,2},{4,5},{5,4},{6,7},{7,6},{8,9},{9,8},{10,11... | collective-permute-start | bytes 786440 | tf_op jit(solution)/shard_map/ppermute | solution.py:287
  22.4 13.1 %collective-permute-start.1 = (f32[256,256]{1,0:T(8,128)S(1)}, f32[256,256]{1,0:T(8,128)S(1)}, u32[]{:S(2)}, u32[]{:S(2)}) collective-permute-start(f32[256,256]{1,0:T(8,128)S(1)} %add.15), channel_id=1, source_target_pairs={{0,3},{1,2},{2,1},{3,0},{4,7},{5,6},{6,5},{7,4},{8,11},{9,10},{10,... | collective-permute-start | bytes 786440 | tf_op jit(solution)/shard_map/ppermute | solution.py:287
  29.5 21.3 %copy-start = (f32[8,256]{1,0:T(8,128)}, f32[8,256]{1,0:T(8,128)S(1)}, u32[]{:S(2)}) copy-start(f32[8,256]{1,0:T(8,128)S(1)} %get-tuple-element.22.like_v) | copy-start | bytes 24580
  36.7 1.2 %collective-permute-start.3 = (f32[8,128]{1,0:T(8,128)S(1)}, f32[8,128]{1,0:T(8,128)S(1)}, u32[]{:S(2)}, u32[]{:S(2)}) collective-permute-start(f32[8,128]{1,0:T(8,128)S(1)} %get-tuple-element.24), channel_id=1, source_target_pairs={{0,4},{1,5},{2,6},{3,7},{4,0},{5,1},{6,2},{7,3},{8,12},{9,13},{10,... | collective-permute-start | bytes 12296 | tf_op jit(solution)/shard_map/ppermute | solution.py:287
  37.8 3.0 %collective-permute-start.4 = (f32[8,128]{1,0:T(8,128)S(1)}, f32[8,128]{1,0:T(8,128)S(1)}, u32[]{:S(2)}, u32[]{:S(2)}) collective-permute-start(f32[8,128]{1,0:T(8,128)S(1)} %add.16), channel_id=1, source_target_pairs={{0,12},{1,13},{2,14},{3,15},{4,8},{5,9},{6,10},{7,11},{8,4},{9,5},... | collective-permute-start | bytes 12296 | tf_op jit(solution)/shard_map/ppermute | solution.py:287
  40.9 3.0 %collective-permute-start.5 = (f32[8,128]{1,0:T(8,128)S(1)}, f32[8,128]{1,0:T(8,128)S(1)}, u32[]{:S(2)}, u32[]{:S(2)}) collective-permute-start(f32[8,128]{1,0:T(8,128)S(1)} %add.17), channel_id=1, source_target_pairs={{0,20},{1,21},{2,22},{3,23},{4,16},{5,17},{6,18},{7,19},{8,28},{9,... | collective-permute-start | bytes 12296 | tf_op jit(solution)/shard_map/ppermute | solution.py:287
  43.9 7.0 %copy-start.6 = (f32[8,128]{1,0:T(8,128)}, f32[8,128]{1,0:T(8,128)S(1)}, u32[]{:S(2)}) copy-start(f32[8,128]{1,0:T(8,128)S(1)} %add.18.own_v) | copy-start | bytes 12292
  43.9 3.0 %collective-permute-start.6 = (f32[8,128]{1,0:T(8,128)S(1)}, f32[8,128]{1,0:T(8,128)S(1)}, u32[]{:S(2)}, u32[]{:S(2)}) collective-permute-start(f32[8,128]{1,0:T(8,128)S(1)} %add.18.own_v), channel_id=1, source_target_pairs={{0,5},{1,4},{2,7},{3,6},{4,1},{5,0},{6,3},{7,2},{8,13},{9,12},{10,... | collective-permute-start | bytes 12296 | tf_op jit(solution)/shard_map/ppermute | solution.py:287
  46.9 3.9 %copy-start.7 = (f32[8,128]{1,0:T(8,128)}, f32[8,128]{1,0:T(8,128)S(1)}, u32[]{:S(2)}) copy-start(f32[8,128]{1,0:T(8,128)S(1)} %add.19.half_v) | copy-start | bytes 12292
  46.9 3.9 %collective-permute-start.7 = (f32[8,128]{1,0:T(8,128)S(1)}, f32[8,128]{1,0:T(8,128)S(1)}, u32[]{:S(2)}, u32[]{:S(2)}) collective-permute-start(f32[8,128]{1,0:T(8,128)S(1)} %add.19.half_v), channel_id=1, source_target_pairs={{0,6},{1,7},{2,4},{3,5},{4,2},{5,3},{6,0},{7,1},{8,14},{9,15},{10,... | collective-permute-start | bytes 12296 | tf_op jit(solution)/shard_map/ppermute | solution.py:287
  50.9 0.6 %copy-start.8 = (f32[8,128]{1,0:T(8,128)}, f32[8,128]{1,0:T(8,128)S(1)}, u32[]{:S(2)}) copy-start(f32[8,128]{1,0:T(8,128)S(1)} %collective-permute-done.7.other_v) | copy-start | bytes 12292

commit v4 on v3

--- a/solution.py
+++ b/solution.py
@@ -217,14 +217,13 @@
     )(third, blocks, sums, directions, shifts, chol, mean.reshape(1, n))
 
 
-def finish_flows(mine, far, beside, rating, draws, likelihood, lines_total):
+def overload_sums(mine, far, beside, rating, draws, likelihood, lines_total):
     rows, lines = mine.shape
     n = draws.shape[1]
     packed_rows = -(-(rows // LANES + n // LANES + 1) // 8) * 8
 
-    def body(mine_v, far_v, beside_v, rating_v, draws_v, like_v, flows, packed):
+    def body(mine_v, far_v, beside_v, rating_v, draws_v, like_v, packed):
         value = mine_v[...] + far_v[...] + beside_v[...]
-        flows[...] = value
         limit = jnp.concatenate([rating_v[j : j + 1, :] for j in range(lines // LANES)], 1)
         over = jnp.abs(value) * (SHARP / (limit.astype(jnp.float32) * 0.01)) - SHARP
         soft = jnp.maximum(over, 0.0) + jnp.log(1.0 + jnp.exp(-jnp.abs(over)))
@@ -242,13 +241,10 @@
     return pl.pallas_call(
         body,
         in_specs=[vmem] * 6,
-        out_specs=[vmem] * 2,
-        out_shape=[
-            jax.ShapeDtypeStruct((rows, lines), jnp.float32),
-            jax.ShapeDtypeStruct((packed_rows, LANES), jnp.float32),
-        ],
+        out_specs=vmem,
+        out_shape=jax.ShapeDtypeStruct((packed_rows, LANES), jnp.float32),
         compiler_params=pltpu.CompilerParams(vmem_limit_bytes=32 * MIB),
-        name="finish_flows",
+        name="overload_sums",
     )(mine, far, beside, rating.reshape(lines // LANES, LANES), draws, likelihood)
 
 
@@ -272,6 +268,7 @@
         in_specs=[vmem] * 5,
         out_specs=[vmem] * 3,
         out_shape=[jax.ShapeDtypeStruct(s, jnp.float32) for s in shapes],
+        compiler_params=pltpu.CompilerParams(vmem_limit_bytes=8 * MIB),
         name="last_outputs",
     )(own, half, other, likelihood, mean.reshape(b, LANES))
     return [x.reshape(-1) for x in out]
@@ -324,9 +321,10 @@
         beside = exchange(third, 0, 1)
         mine, own_normals, likelihood = own_part(third, blocks, sums, *drawn, block_rows)
         far = exchange(second + from_near, 0, 3)
-        flows, packed = finish_flows(
+        packed = overload_sums(
             mine, far, beside, line_rating, own_normals, likelihood, lines_total
         )
+        flows = mine + far + beside
         packed = packed + exchange(packed, 1, 0)
         flip = 2
         while flip < lax.axis_size("line"):

time: 52.9 us -> 51.1 us (0.966)
  Pallas kernels: 20.8 us -> 19.6 us
  other arithmetic: 0.12 us -> 0.89 us
  waiting for transfers between devices: 17.1 us -> 16.4 us
  local copies, waits for them, and re-layouts: 0.62 us -> 0.03 us
    add x0 -> x1, other arithmetic: none -> 0.77 us  [per_device(): flows = mine + far + beside]
    pallas_call x1, Pallas kernels: 1.3 us -> 0.59 us  [last_outputs(): pl.pallas_call(body, in_specs=[vmem] * 5, out_specs=[vmem] * 3, out_shape...]
    ppermute x8, waiting for transfers between devices: 17.1 us -> 16.4 us  [exchange(): return lax.ppermute(value, ('line', 'bus'), pairs)]
    unnamed x18 -> x10, local copies, waits for them, and re-layouts: 0.62 us -> 0.03 us
  transfers between devices with their start and end apart: 8 -> 8, of which waited for: 7 -> 7; matrix products, arithmetic and copies ran while one was open for 0% -> 2% of each run, Pallas kernels for 12% -> 13%
where the time goes in v4:
time: 51.1 us; the launch traced here: 51 us
  Pallas kernels  19.6 us (38%)
  waiting for transfers between devices  16.4 us (32%)
  starting transfers between devices  13.4 us (26%)
  other arithmetic  0.89 us (2%)
  between operations  0.71 us (1%)
    ppermute x8, waiting for transfers between devices, exchange(): return lax.ppermute(value, ('line', 'bus'), pairs)  16.4 us
    ppermute x8, starting transfers between devices, exchange(): return lax.ppermute(value, ('line', 'bus'), pairs)  13.4 us
    pallas_call x1, Pallas kernels, head(): pl.pallas_call(body, in_specs=[pl.BlockSpec(memory_space=pltpu.SMEM)] + [...  11.8 us
    pallas_call x1, Pallas kernels, middle_parts(): pl.pallas_call(body, in_specs=[pl.BlockSpec(memory_space=pltpu.SMEM)] + [...  3.93 us
    pallas_call x1, Pallas kernels, own_part(): pl.pallas_call(body, in_specs=[pl.BlockSpec(memory_space=pl.ANY), pl.Bloc...  2.59 us
  transfers between devices with their start and end apart: 8, of which 7 were waited for; matrix products, arithmetic and copies ran while one was open for 2% of the time, Pallas kernels for 13%

profile of v4, /device:TPU:0, one launch (start us, length us, event | category | flops | bytes accessed | tf_op | source)
XLA Modules:
  0.0 51.0 jit_solution(5746976258554154392)
XLA Ops:
  0.6 0.0 copy-start.2
  0.6 0.0 copy-start.4
  0.7 0.0 copy-start.3
  0.7 0.0 copy-start
  0.7 0.1 pad_add_fusion.blocks_s
  0.8 11.8 %segment_sums.1 = (f32[528,256]{1,0:T(8,128)S(1)}, f32[256,256]{1,0:T(8,128)S(1)}) custom-call(s32[4]{0:T(128)S(1)} %pad_add_fusion.blocks_s, bf16[256,25088]{1,0:T(8,128)(2,1)} %p_h.1, f32[196,128]{1,0:T(8,128)} %bitcast.18, f32[196,128]{1,0:T(8,128)} %bitcast.19, s32[196,128]{1,0:T(8,128)} %bitcast.20, s32[30,512]{1,0:T(8,128)} %d_v.3, s32[8,512]{1,0:T(8,128)} %s_v.3, ...), custom_call_target="tpu_custom_call" | custom-call | flops 6576668672 | bytes 12845056 | tf_op jit(solution)/shard_map/segment_sums/pallas_call | solution.py:131
  12.5 3.1 %collective-permute-start = (f32[256,256]{1,0:T(8,128)S(1)}, f32[256,256]{1,0:T(8,128)S(1)}, u32[]{:S(2)}, u32[]{:S(2)}) collective-permute-start(f32[256,256]{1,0:T(8,128)S(1)} %get-tuple-element.18), channel_id=1, source_target_pairs={{0,1},{1,0},{2,3},{3,2},{4,5},{5,4},{6,7},{7,6},{8,9},{9,8},{10,11... | collective-permute-start | bytes 786440 | tf_op jit(solution)/shard_map/ppermute | solution.py:284
  15.6 0.0 copy-done.2
  15.6 0.0 copy-done.4
  15.6 0.0 copy-done.3
  15.6 0.0 copy-done
  15.6 3.9 %middle_parts.1 = (f32[256,256]{1,0:T(8,128)S(1)}, f32[256,256]{1,0:T(8,128)S(1)}) custom-call(s32[4]{0:T(128)S(1)} %pad_add_fusion.blocks_s, f32[528,256]{1,0:T(8,128)S(1)} %get-tuple-element.14.sums_v, s32[30,512]{1,0:T(8,128)S(1)} %copy-done.3, s32[8,512]{1,0:T(8,128)S(1)} %copy-done.4, f32[512,512]{1,0:T(8,128)S(1)} %copy-done.2, f32[1,512]{1,0:T(1,128)S(1)} %bitcast.14), custom_call_target="tpu_custom_call" | custom-call | flops 1207959552 | bytes 3145728 | tf_op jit(solution)/shard_map/middle_parts/pallas_call | solution.py:180
  19.6 0.1 collective-permute-start.2
  19.7 2.7 %collective-permute-done = f32[256,256]{1,0:T(8,128)S(1)} collective-permute-done((f32[256,256]{1,0:T(8,128)S(1)}, f32[256,256]{1,0:T(8,128)S(1)}, u32[]{:S(2)}, u32[]{:S(2)}) %collective-permute-start) | collective-permute-done | bytes 262176 | tf_op jit(solution)/shard_map/ppermute | solution.py:284
  22.4 4.6 %collective-permute-start.1 = (f32[256,256]{1,0:T(8,128)S(1)}, f32[256,256]{1,0:T(8,128)S(1)}, u32[]{:S(2)}, u32[]{:S(2)}) collective-permute-start(f32[256,256]{1,0:T(8,128)S(1)} %add.21), channel_id=1, source_target_pairs={{0,3},{1,2},{2,1},{3,0},{4,7},{5,6},{6,5},{7,4},{8,11},{9,10},{10,... | collective-permute-start | bytes 786440 | tf_op jit(solution)/shard_map/ppermute | solution.py:284
  27.0 2.6 %own_part.1 = (f32[256,256]{1,0:T(8,128)S(1)}, f32[256,512]{1,0:T(8,128)S(1)}, f32[8,256]{1,0:T(8,128)S(1)}) custom-call(f32[256,256]{1,0:T(8,128)S(1)} %get-tuple-element.15.third_h, s32[4]{0:T(128)S(1)} %pad_add_fusion.blocks_s, f32[528,256]{1,0:T(8,128)S(1)} %get-tuple-element.14.sums_v, s32[30,512]{1,0:T(8,128)S(1)} %copy-done.3, ...), custom_call_target="tpu_custom_call" | custom-call | flops 603979776 | bytes 2097152 | tf_op jit(solution)/shard_map/own_part/pallas_call | solution.py:207
  29.5 0.0 collective-permute-done.2.beside_v
  29.5 5.9 %collective-permute-done.1.far_v = f32[256,256]{1,0:T(8,128)S(1)} collective-permute-done((f32[256,256]{1,0:T(8,128)S(1)}, f32[256,256]{1,0:T(8,128)S(1)}, u32[]{:S(2)}, u32[]{:S(2)}) %collective-permute-start.1) | collective-permute-done | bytes 262176 | tf_op jit(solution)/shard_map/ppermute | solution.py:284
  35.5 0.0 copy-done.1
  35.5 0.7 %overload_sums.1 = f32[8,128]{1,0:T(8,128)S(1)} custom-call(f32[256,256]{1,0:T(8,128)S(1)} %get-tuple-element.16.mine_v, f32[256,256]{1,0:T(8,128)S(1)} %collective-permute-done.1.far_v, f32[256,256]{1,0:T(8,128)S(1)} %collective-permute-done.2.beside_v, s32[2,128]{1,0:T(2,128)S(1)} %bitcast.17, f32[256,512]{1,0:T(8,128)S(1)} %get-tuple-element.19.draws_v, ...), custom_call_target="tpu_custom_call" | custom-call | tf_op jit(solution)/shard_map/overload_sums/pallas_call | solution.py:241
  36.2 0.0 collective-permute-start.3
  36.2 1.2 %collective-permute-done.3 = f32[8,128]{1,0:T(8,128)S(1)} collective-permute-done((f32[8,128]{1,0:T(8,128)S(1)}, f32[8,128]{1,0:T(8,128)S(1)}, u32[]{:S(2)}, u32[]{:S(2)}) %collective-permute-start.3) | collective-permute-done | bytes 4128 | tf_op jit(solution)/shard_map/ppermute | solution.py:284
  37.4 1.2 %collective-permute-start.4 = (f32[8,128]{1,0:T(8,128)S(1)}, f32[8,128]{1,0:T(8,128)S(1)}, u32[]{:S(2)}, u32[]{:S(2)}) collective-permute-start(f32[8,128]{1,0:T(8,128)S(1)} %add.24), channel_id=1, source_target_pairs={{0,12},{1,13},{2,14},{3,15},{4,8},{5,9},{6,10},{7,11},{8,4},{9,5},... | collective-permute-start | bytes 12296 | tf_op jit(solution)/shard_map/ppermute | solution.py:284
  38.6 1.8 %collective-permute-done.4 = f32[8,128]{1,0:T(8,128)S(1)} collective-permute-done((f32[8,128]{1,0:T(8,128)S(1)}, f32[8,128]{1,0:T(8,128)S(1)}, u32[]{:S(2)}, u32[]{:S(2)}) %collective-permute-start.4) | collective-permute-done | bytes 4128 | tf_op jit(solution)/shard_map/ppermute | solution.py:284
  40.4 1.3 %collective-permute-start.5 = (f32[8,128]{1,0:T(8,128)S(1)}, f32[8,128]{1,0:T(8,128)S(1)}, u32[]{:S(2)}, u32[]{:S(2)}) collective-permute-start(f32[8,128]{1,0:T(8,128)S(1)} %add.25), channel_id=1, source_target_pairs={{0,20},{1,21},{2,22},{3,23},{4,16},{5,17},{6,18},{7,19},{8,28},{9,... | collective-permute-start | bytes 12296 | tf_op jit(solution)/shard_map/ppermute | solution.py:284
  41.7 1.7 %collective-permute-done.5 = f32[8,128]{1,0:T(8,128)S(1)} collective-permute-done((f32[8,128]{1,0:T(8,128)S(1)}, f32[8,128]{1,0:T(8,128)S(1)}, u32[]{:S(2)}, u32[]{:S(2)}) %collective-permute-start.5) | collective-permute-done | bytes 4128 | tf_op jit(solution)/shard_map/ppermute | solution.py:284
  43.4 1.2 %collective-permute-start.6 = (f32[8,128]{1,0:T(8,128)S(1)}, f32[8,128]{1,0:T(8,128)S(1)}, u32[]{:S(2)}, u32[]{:S(2)}) collective-permute-start(f32[8,128]{1,0:T(8,128)S(1)} %add.26.own_v), channel_id=1, source_target_pairs={{0,5},{1,4},{2,7},{3,6},{4,1},{5,0},{6,3},{7,2},{8,13},{9,12},{10,... | collective-permute-start | bytes 12296 | tf_op jit(solution)/shard_map/ppermute | solution.py:284
  44.6 1.8 %collective-permute-done.6 = f32[8,128]{1,0:T(8,128)S(1)} collective-permute-done((f32[8,128]{1,0:T(8,128)S(1)}, f32[8,128]{1,0:T(8,128)S(1)}, u32[]{:S(2)}, u32[]{:S(2)}) %collective-permute-start.6) | collective-permute-done | bytes 4128 | tf_op jit(solution)/shard_map/ppermute | solution.py:284
  46.5 1.9 %collective-permute-start.7 = (f32[8,128]{1,0:T(8,128)S(1)}, f32[8,128]{1,0:T(8,128)S(1)}, u32[]{:S(2)}, u32[]{:S(2)}) collective-permute-start(f32[8,128]{1,0:T(8,128)S(1)} %add.27.half_v), channel_id=1, source_target_pairs={{0,6},{1,7},{2,4},{3,5},{4,2},{5,3},{6,0},{7,1},{8,14},{9,15},{10,... | collective-permute-start | bytes 12296 | tf_op jit(solution)/shard_map/ppermute | solution.py:284
  48.4 0.8 %add_add_fusion = f32[256,256]{1,0:T(8,128)} fusion(f32[256,256]{1,0:T(8,128)S(1)} %collective-permute-done.2.beside_v, f32[256,256]{1,0:T(8,128)S(1)} %get-tuple-element.16.mine_v, f32[256,256]{1,0:T(8,128)S(1)} %collective-permute-done.1.far_v), kind=kLoop, calls=%fused_computation | loop fusion | flops 131072 | bytes 1048576 | tf_op jit(solution)/shard_map/add | solution.py:327
  49.1 1.3 %collective-permute-done.7.other_v = f32[8,128]{1,0:T(8,128)S(1)} collective-permute-done((f32[8,128]{1,0:T(8,128)S(1)}, f32[8,128]{1,0:T(8,128)S(1)}, u32[]{:S(2)}, u32[]{:S(2)}) %collective-permute-start.7) | collective-permute-done | bytes 4128 | tf_op jit(solution)/shard_map/ppermute | solution.py:284
  50.4 0.6 %last_outputs.1 = (f32[2,128]{1,0:T(2,128)}, f32[2,128]{1,0:T(2,128)}, f32[4,128]{1,0:T(4,128)}) custom-call(f32[8,128]{1,0:T(8,128)S(1)} %add.26.own_v, f32[8,128]{1,0:T(8,128)S(1)} %add.27.half_v, f32[8,128]{1,0:T(8,128)S(1)} %collective-permute-done.7.other_v, f32[8,256]{1,0:T(8,128)S(1)} %get-tuple-element.20.like_v, f32[4,128]{1,0:T(4,128)S(1)} %bitcast.16), custom_call_target="tpu_custom_call" | custom-call | tf_op jit(solution)/shard_map/last_outputs/pallas_call | solution.py:266
  (6 shorter events, 0.0 us)
Async XLA Ops:
  0.6 15.0 %copy-start.2 = (f32[512,512]{1,0:T(8,128)S(1)}, f32[512,512]{1,0:T(8,128)}, u32[]{:S(2)}) copy-start(f32[512,512]{1,0:T(8,128)} %c_v.3) | copy-start | bytes 3145732
  0.6 15.0 %copy-start.4 = (s32[8,512]{1,0:T(8,128)S(1)}, s32[8,512]{1,0:T(8,128)}, u32[]{:S(2)}) copy-start(s32[8,512]{1,0:T(8,128)} %s_v.3) | copy-start | bytes 49156
  0.7 15.0 %copy-start.3 = (s32[30,512]{1,0:T(8,128)S(1)}, s32[30,512]{1,0:T(8,128)}, u32[]{:S(2)}) copy-start(s32[30,512]{1,0:T(8,128)} %d_v.3) | copy-start | bytes 184324
  0.7 15.0 %copy-start = (f32[512]{0:T(512)S(1)}, f32[512]{0:T(512)}, u32[]{:S(2)}) copy-start(f32[512]{0:T(512)} %param.17) | copy-start | bytes 6148
  0.8 34.7 %copy-start.1 = (s32[256]{0:T(256)S(1)}, s32[256]{0:T(256)}, u32[]{:S(2)}) copy-start(s32[256]{0:T(256)} %param.13) | copy-start | bytes 3076
  12.5 9.8 %collective-permute-start = (f32[256,256]{1,0:T(8,128)S(1)}, f32[256,256]{1,0:T(8,128)S(1)}, u32[]{:S(2)}, u32[]{:S(2)}) collective-permute-start(f32[256,256]{1,0:T(8,128)S(1)} %get-tuple-element.18), channel_id=1, source_target_pairs={{0,1},{1,0},{2,3},{3,2},{4,5},{5,4},{6,7},{7,6},{8,9},{9,8},{10,11... | collective-permute-start | bytes 786440 | tf_op jit(solution)/shard_map/ppermute | solution.py:284
  19.6 10.0 %collective-permute-start.2 = (f32[256,256]{1,0:T(8,128)S(1)}, f32[256,256]{1,0:T(8,128)S(1)}, u32[]{:S(2)}, u32[]{:S(2)}) collective-permute-start(f32[256,256]{1,0:T(8,128)S(1)} %get-tuple-element.15.third_h), channel_id=1, source_target_pairs={{0,1},{1,0},{2,3},{3,2},{4,5},{5,4},{6,7},{7,6},{8,9},{9,8},{10,11... | collective-permute-start | bytes 786440 | tf_op jit(solution)/shard_map/ppermute | solution.py:284
  22.4 13.1 %collective-permute-start.1 = (f32[256,256]{1,0:T(8,128)S(1)}, f32[256,256]{1,0:T(8,128)S(1)}, u32[]{:S(2)}, u32[]{:S(2)}) collective-permute-start(f32[256,256]{1,0:T(8,128)S(1)} %add.21), channel_id=1, source_target_pairs={{0,3},{1,2},{2,1},{3,0},{4,7},{5,6},{6,5},{7,4},{8,11},{9,10},{10,... | collective-permute-start | bytes 786440 | tf_op jit(solution)/shard_map/ppermute | solution.py:284
  36.2 1.2 %collective-permute-start.3 = (f32[8,128]{1,0:T(8,128)S(1)}, f32[8,128]{1,0:T(8,128)S(1)}, u32[]{:S(2)}, u32[]{:S(2)}) collective-permute-start(f32[8,128]{1,0:T(8,128)S(1)} %overload_sums.1), channel_id=1, source_target_pairs={{0,4},{1,5},{2,6},{3,7},{4,0},{5,1},{6,2},{7,3},{8,12},{9,13},{10,... | collective-permute-start | bytes 12296 | tf_op jit(solution)/shard_map/ppermute | solution.py:284
  37.4 3.0 %collective-permute-start.4 = (f32[8,128]{1,0:T(8,128)S(1)}, f32[8,128]{1,0:T(8,128)S(1)}, u32[]{:S(2)}, u32[]{:S(2)}) collective-permute-start(f32[8,128]{1,0:T(8,128)S(1)} %add.24), channel_id=1, source_target_pairs={{0,12},{1,13},{2,14},{3,15},{4,8},{5,9},{6,10},{7,11},{8,4},{9,5},... | collective-permute-start | bytes 12296 | tf_op jit(solution)/shard_map/ppermute | solution.py:284
  40.4 3.0 %collective-permute-start.5 = (f32[8,128]{1,0:T(8,128)S(1)}, f32[8,128]{1,0:T(8,128)S(1)}, u32[]{:S(2)}, u32[]{:S(2)}) collective-permute-start(f32[8,128]{1,0:T(8,128)S(1)} %add.25), channel_id=1, source_target_pairs={{0,20},{1,21},{2,22},{3,23},{4,16},{5,17},{6,18},{7,19},{8,28},{9,... | collective-permute-start | bytes 12296 | tf_op jit(solution)/shard_map/ppermute | solution.py:284
  43.4 3.0 %collective-permute-start.6 = (f32[8,128]{1,0:T(8,128)S(1)}, f32[8,128]{1,0:T(8,128)S(1)}, u32[]{:S(2)}, u32[]{:S(2)}) collective-permute-start(f32[8,128]{1,0:T(8,128)S(1)} %add.26.own_v), channel_id=1, source_target_pairs={{0,5},{1,4},{2,7},{3,6},{4,1},{5,0},{6,3},{7,2},{8,13},{9,12},{10,... | collective-permute-start | bytes 12296 | tf_op jit(solution)/shard_map/ppermute | solution.py:284
  46.5 3.9 %collective-permute-start.7 = (f32[8,128]{1,0:T(8,128)S(1)}, f32[8,128]{1,0:T(8,128)S(1)}, u32[]{:S(2)}, u32[]{:S(2)}) collective-permute-start(f32[8,128]{1,0:T(8,128)S(1)} %add.27.half_v), channel_id=1, source_target_pairs={{0,6},{1,7},{2,4},{3,5},{4,2},{5,3},{6,0},{7,1},{8,14},{9,15},{10,... | collective-permute-start | bytes 12296 | tf_op jit(solution)/shard_map/ppermute | solution.py:284

commit v5 on v4

v5 whole, which is shorter than its diff:
```python
import math

import jax
import jax.numpy as jnp
from jax import lax
from jax.experimental import pallas as pl
from jax.experimental.pallas import tpu as pltpu
from jax.sharding import PartitionSpec as P

POINTS = 128
SHARP = 8.0
HIGH = lax.Precision.HIGH
HIGHEST = lax.Precision.HIGHEST
NT = (((1,), (1,)), ((), ()))
NN = (((1,), (0,)), ((), ()))
LANES = 128
EXTRA = 16
QUARTERS = 4
MIB = 2**20
CENTRAL = (
    2.81022636e-08, 3.43273939e-07, -3.5233877e-06, -4.39150654e-06, 0.00021858087,
    -0.00125372503, -0.00417768164, 0.246640727, 1.50140941,
)
TAIL = (
    -0.000200214257, 0.000100950558, 0.00134934322, -0.00367342844, 0.00573950773,
    -0.0076224613, 0.00943887047, 1.00167406, 2.83297682,
)


def dot(a, b, dims, precision):
    return lax.dot_general(a, b, dims, precision=precision, preferred_element_type=jnp.float32)


def normal_of(digits):
    x = (2 * (digits >> 7) + 1).astype(jnp.float32) * (2.0 / 16777216.0) - 1.0
    w = -jnp.log((1.0 - x) * (1.0 + x))
    central = w < 5.0
    w = jnp.where(central, w - 2.5, jnp.sqrt(w) - 3.0)
    p = jnp.where(central, CENTRAL[0], TAIL[0])
    for a, b in zip(CENTRAL[1:], TAIL[1:]):
        p = jnp.where(central, a, b) + p * w
    return math.sqrt(2.0) * (p * x)


def block_normals(directions, shifts, start, rows):
    group = min(rows, POINTS)
    n = directions.shape[1]
    digits = jnp.zeros((1, n), jnp.int32)
    bits = group.bit_length() - 1
    lead = min(bits, 3)
    at = lax.broadcasted_iota(jnp.int32, (2**lead, n), 0)
    digits = jnp.zeros((2**lead, n), jnp.int32)
    for b in range(lead):
        digits = digits ^ jnp.where((at >> b & 1) == 1, directions[b : b + 1, :], 0)
    for b in range(lead, bits):
        digits = jnp.concatenate([digits, digits ^ directions[b : b + 1, :]], 0)
    pieces = []
    for j in range(rows // group):
        first = start + j * group
        point = lax.rem(first, POINTS)
        flip = shifts[pl.ds(lax.div(first, POINTS), 1), :]
        for b in range(bits, POINTS.bit_length() - 1):
            flip = flip ^ (directions[b : b + 1, :] * (point >> b & 1))
        pieces.append(normal_of(digits ^ flip))
    return jnp.concatenate(pieces, 0) if len(pieces) > 1 else pieces[0]


def block_width(buses):
    for width in (6272, 3584, 1792, 896, 512, 256):
        if buses % width == 0:
            return width
    return LANES


def head(blocks, ptdf, base, gain, factor, n):
    lines, buses = ptdf.shape
    width = block_width(buses)
    steps, rows, per = buses // width, buses // LANES, width // LANES
    q, groups = lines // QUARTERS, n // LANES

    def body(
        blocks_s, p_h, b_h, g_h, f_h, out_0, out_1, out_2, out_3,
        sums, flipped, base_v, p_v, b_v, g_v, f_v, p_sem, v_sem,
    ):
        pairs = ((f_h, f_v), (g_h, g_v), (b_h, b_v))
        small = [pltpu.make_async_copy(h, v, v_sem.at[i]) for i, (h, v) in enumerate(pairs)]
        for copy in small:
            copy.start()

        def block_copy(k):
            at = pl.ds(pl.multiple_of(k * width, width), width)
            return pltpu.make_async_copy(p_h.at[:, at], p_v.at[:, at], p_sem.at[k])

        def start(k, _):
            block_copy(k).start()
            return 0

        lax.fori_loop(0, steps, start, 0)
        sums[...] = jnp.zeros_like(sums)
        for copy in small:
            copy.wait()

        def step(k, _):
            block_copy(k).wait()

            def row(v):
                return jnp.concatenate([v[pl.ds(k * per + j, 1), :] for j in range(per)], 1)

            g = row(g_v)
            p = p_v[:, pl.ds(pl.multiple_of(k * width, width), width)]
            scaled = (p.astype(jnp.float32) * g).astype(jnp.bfloat16)
            own = lax.broadcasted_iota(jnp.int16, (n, width), 0) == row(f_v).astype(jnp.int16)
            hot = jnp.where(own, jnp.bfloat16(1), jnp.bfloat16(0))
            ratio = row(b_v) / g
            high = ratio.astype(jnp.bfloat16)
            low = (ratio - high.astype(jnp.float32)).astype(jnp.bfloat16)
            rest = jnp.zeros((EXTRA - 2, width), jnp.bfloat16)
            left = jnp.concatenate([hot, high, low, rest], 0)
            sums[...] += lax.dot_general(left, scaled, NT, preferred_element_type=jnp.float32)
            return 0

        lax.fori_loop(0, steps, step, 0)
        flipped[...] = sums[:n, :].T
        base_row = sums[n : n + 1, :] + sums[n + 1 : n + 2, :]
        blank = jnp.zeros((1, LANES - q), jnp.float32)
        for d in range(QUARTERS):
            base_v[8 * d : 8 * d + 8, :] = jnp.broadcast_to(
                jnp.concatenate([base_row[:, d * q : d * q + q], blank], 1), (8, LANES)
            )
        for i, out in enumerate((out_0, out_1, out_2, out_3)):
            d = blocks_s[i]
            for j in range(groups):
                out[j * q : j * q + q, :] = flipped[
                    pl.ds(pl.multiple_of(d * q, 8), q), j * LANES : (j + 1) * LANES
                ]
            out[groups * q :, :] = base_v[pl.ds(pl.multiple_of(d * 8, 8), 8), :]

    hbm = pl.BlockSpec(memory_space=pltpu.HBM)
    vmem = pl.BlockSpec(memory_space=pltpu.VMEM)
    return pl.pallas_call(
        body,
        in_specs=[pl.BlockSpec(memory_space=pltpu.SMEM)] + [hbm] * 4,
        out_specs=[vmem] * QUARTERS,
        out_shape=[jax.ShapeDtypeStruct((groups * q + 8, LANES), jnp.float32)] * QUARTERS,
        scratch_shapes=[
            pltpu.VMEM((n + EXTRA, lines), jnp.float32),
            pltpu.VMEM((lines, n), jnp.float32),
            pltpu.VMEM((8 * QUARTERS, LANES), jnp.float32),
            pltpu.VMEM((lines, buses), jnp.bfloat16),
            pltpu.VMEM((rows, LANES), jnp.float32),
            pltpu.VMEM((rows, LANES), jnp.float32),
            pltpu.VMEM((rows, LANES), jnp.int32),
            pltpu.SemaphoreType.DMA((steps,)),
            pltpu.SemaphoreType.DMA((3,)),
        ],
        compiler_params=pltpu.CompilerParams(vmem_limit_bytes=48 * MIB),
        cost_estimate=pl.CostEstimate(
            flops=2 * lines * buses * n, bytes_accessed=2 * lines * buses, transcendentals=0
        ),
        name="segment_sums",
    )(
        blocks,
        *(
            pltpu.with_memory_space_constraint(x, pltpu.HBM)
            for x in (
                ptdf, base.reshape(rows, LANES), gain.reshape(rows, LANES), factor.reshape(rows, LANES),
            )
        ),
    )


def split(x):
    high = x.astype(jnp.bfloat16)
    return high, (x - high.astype(jnp.float32)).astype(jnp.bfloat16)


def all_factors(directions, shifts, chol, mean):
    n = directions.shape[1]
    scenarios = POINTS * shifts.shape[0]
    block = 2 * POINTS

    def body(d_v, s_v, c_v, m_v, f_high, f_low, kept, likelihood, c_high, c_low):
        c_high[...], c_low[...] = split(c_v[...])
        mean_terms = jnp.concatenate([*split(m_v[...]), jnp.zeros((14, n), jnp.bfloat16)], 0)

        def step(k, _):
            at = pl.ds(pl.multiple_of(k * block, block), block)
            draws = block_normals(d_v, s_v, k * block, block)
            kept[at, :] = draws
            high, low = split(draws + m_v[...])
            both = dot(jnp.concatenate([high, low], 0), c_high[...], NT, None)
            factors = both[:block, :] + (both[block:, :] + dot(high, c_low[...], NT, None))
            f_high[at, :], f_low[at, :] = split(factors)
            high, low = split(draws)
            tilt = dot(mean_terms, high, NT, None)
            tilt = tilt[:1, :] + (tilt[1:2, :] + dot(mean_terms, low, NT, None)[:1, :])
            for j in range(block // LANES):
                likelihood[pl.ds(k * (block // LANES) + j, 1), :] = jnp.exp(
                    -tilt[:, j * LANES : (j + 1) * LANES]
                )
            return 0

        lax.fori_loop(0, scenarios // block, step, 0)

    vmem = pl.BlockSpec(memory_space=pltpu.VMEM)
    big = jax.ShapeDtypeStruct((scenarios, n), jnp.bfloat16)
    return pl.pallas_call(
        body,
        in_specs=[vmem] * 4,
        out_specs=[vmem] * 4,
        out_shape=[
            big,
            big,
            jax.ShapeDtypeStruct((scenarios, n), jnp.float32),
            jax.ShapeDtypeStruct((scenarios // LANES, LANES), jnp.float32),
        ],
        scratch_shapes=[pltpu.VMEM((n, n), jnp.bfloat16), pltpu.VMEM((n, n), jnp.bfloat16)],
        compiler_params=pltpu.CompilerParams(vmem_limit_bytes=20 * MIB),
        cost_estimate=pl.CostEstimate(
            flops=6 * scenarios * n * n, bytes_accessed=6 * MIB, transcendentals=2 * scenarios * n
        ),
        name="all_factors",
    )(directions, shifts, chol, mean.reshape(1, n))


def pair_sum(mine, other, later):
    def body(mine_v, other_v, later_v, out, passed):
        out[...] = mine_v[...] + other_v[...]
        passed[...] = later_v[...]

    vmem = pl.BlockSpec(memory_space=pltpu.VMEM)
    return pl.pallas_call(
        body,
        in_specs=[vmem] * 3,
        out_specs=[vmem] * 2,
        out_shape=[jax.ShapeDtypeStruct(mine.shape, jnp.float32)] * 2,
        compiler_params=pltpu.CompilerParams(vmem_limit_bytes=4 * MIB),
        name="pair_sum",
    )(mine, other, later)


def quarter_flows(blocks, mine, beside, far, scale, f_high, f_low, lines_total):
    scenarios, n = f_high.shape
    q = scale.shape[0]
    block, groups = scenarios // QUARTERS, n // LANES

    def body(
        blocks_s, mine_v, beside_v, far_v, scale_v, high_v, low_v, out_0, out_1, out_2, out_3, share, flows
    ):
        total = mine_v[...] + beside_v[...] + far_v[...]
        g = jnp.concatenate([total[j * q : j * q + q, :] for j in range(groups)], 1)
        diagonal = lax.broadcasted_iota(jnp.int32, (q, LANES), 0) == lax.broadcasted_iota(
            jnp.int32, (q, LANES), 1
        )
        base = jnp.sum(
            jnp.where(diagonal, total[groups * q : groups * q + 1, :], 0.0), axis=1, keepdims=True
        )
        g_high, g_low = split(g)
        wide = dot(jnp.concatenate([g_high, g_low], 0), high_v[...], NT, None)
        value = wide[:q, :] + (wide[q:, :] + dot(g_high, low_v[...], NT, None)) + base
        flows[...] = value
        over = jnp.abs(value) * jnp.concatenate([scale_v[...]] * (scenarios // LANES), 1) - SHARP
        soft = jnp.maximum(over, 0.0) + jnp.log(1.0 + jnp.exp(-jnp.abs(over)))
        row = jnp.sum(soft, axis=0, keepdims=True) * (1.0 / SHARP / lines_total)
        share[...] = jnp.concatenate(
            [row[:, j * LANES : (j + 1) * LANES] for j in range(scenarios // LANES)], 0
        )
        for i, out in enumerate((out_0, out_1, out_2, out_3)):
            out[...] = flows[:, pl.ds(pl.multiple_of(blocks_s[i] * block, LANES), block)]

    vmem = pl.BlockSpec(memory_space=pltpu.VMEM)
    shapes = [(q, block)] * QUARTERS + [(scenarios // LANES, LANES)]
    return pl.pallas_call(
        body,
        in_specs=[pl.BlockSpec(memory_space=pltpu.SMEM)] + [vmem] * 6,
        out_specs=[vmem] * 5,
        out_shape=[jax.ShapeDtypeStruct(s, jnp.float32) for s in shapes],
        scratch_shapes=[pltpu.VMEM((q, scenarios), jnp.float32)],
        compiler_params=pltpu.CompilerParams(vmem_limit_bytes=12 * MIB),
        name="quarter_flows",
    )(blocks, mine, beside, far, scale, f_high, f_low)


def own_flows(blocks, parts):
    q, block = parts[0].shape

    def body(blocks_s, part_0, part_1, part_2, part_3, out, whole):
        for i, part in enumerate((part_0, part_1, part_2, part_3)):
            whole[pl.ds(pl.multiple_of(blocks_s[i] * q, 8), q), :] = part[...]
        out[...] = whole[...].T

    vmem = pl.BlockSpec(memory_space=pltpu.VMEM)
    return pl.pallas_call(
        body,
        in_specs=[pl.BlockSpec(memory_space=pltpu.SMEM)] + [vmem] * 4,
        out_specs=vmem,
        out_shape=pltpu.HBM((block, q * QUARTERS), jnp.float32),
        scratch_shapes=[pltpu.VMEM((q * QUARTERS, block), jnp.float32)],
        compiler_params=pltpu.CompilerParams(vmem_limit_bytes=4 * MIB),
        name="own_flows",
    )(blocks, *parts)


def last_outputs(after, blocks, half, other, likelihood, draws, mean):
    scenarios, n = draws.shape
    a, b = scenarios // QUARTERS // LANES, n // LANES

    def body(after_h, blocks_s, half_v, other_v, like_v, draws_v, mean_v, overload, weight, new_mean, kept):
        every = half_v[...] + other_v[...]
        emphasis = like_v[...] * every
        total = jnp.sum(jnp.sum(emphasis, axis=1, keepdims=True), axis=0, keepdims=True)
        columns = emphasis.T
        parts = jnp.zeros((8, n), jnp.float32)
        for g in range(scenarios // LANES):
            piece = draws_v[g * LANES : (g + 1) * LANES, :] * columns[:, g : g + 1]
            parts = parts + jnp.sum(piece.reshape(LANES // 8, 8, n), axis=0)
        moved = jnp.sum(parts, axis=0, keepdims=True)
        moved = jnp.concatenate([moved[:, j * LANES : (j + 1) * LANES] for j in range(b)], 0)
        kept[0] = every
        kept[1] = scenarios * emphasis / total
        at = pl.ds(blocks_s[3] * a, a)
        overload[...] = kept[0, at, :]
        weight[...] = kept[1, at, :]
        new_mean[...] = mean_v[...] + moved / total

    vmem = pl.BlockSpec(memory_space=pltpu.VMEM)
    shapes = [(a, LANES), (a, LANES), (b, LANES)]
    out = pl.pallas_call(
        body,
        in_specs=[pl.BlockSpec(memory_space=pl.ANY), pl.BlockSpec(memory_space=pltpu.SMEM)] + [vmem] * 5,
        out_specs=[vmem] * 3,
        out_shape=[jax.ShapeDtypeStruct(s, jnp.float32) for s in shapes],
        scratch_shapes=[pltpu.VMEM((2, scenarios // LANES, LANES), jnp.float32)],
        compiler_params=pltpu.CompilerParams(vmem_limit_bytes=8 * MIB),
        name="last_outputs",
    )(
        pltpu.with_memory_space_constraint(after, pltpu.HBM), blocks, half, other, likelihood, draws,
        mean.reshape(b, LANES),
    )
    return [x.reshape(-1) for x in out]


def exchange(value, line_flip, bus_flip):
    lines, buses = lax.axis_size("line"), lax.axis_size("bus")
    pairs = [
        (i * buses + j, (i ^ line_flip) * buses + (j ^ bus_flip))
        for i in range(lines)
        for j in range(buses)
    ]
    return lax.ppermute(value, ("line", "bus"), pairs)


def normals(directions, shifts):
    point = jnp.arange(POINTS, dtype=jnp.int32)
    digits = jnp.zeros((POINTS, directions.shape[1]), jnp.int32)
    for b in range(POINTS.bit_length() - 1):
        digits = digits ^ (point >> b & 1)[:, None] * directions[b][None, :]
    return normal_of(digits[None, :, :] ^ shifts[:, None, :]).reshape(-1, directions.shape[1])


def per_device(
    ptdf,
    base_injection,
    injection_gain,
    factor_of_bus,
    line_rating,
    directions,
    shifts,
    chol_factor,
    proposal_mean,
):
    bus_devices = lax.axis_size("bus")
    lines = ptdf.shape[0]
    lines_total = lines * lax.axis_size("line")
    n = directions.shape[1]
    scenarios = POINTS * shifts.shape[0]
    z = lax.axis_index("bus").astype(jnp.int32)
    drawn = (directions, shifts, chol_factor, proposal_mean)
    own_buses = (ptdf, base_injection, injection_gain, factor_of_bus)

    if bus_devices == QUARTERS:
        blocks = jnp.stack([z ^ 2, z ^ 3, z ^ 1, z])
        for_pair, for_far, for_near, mine = head(blocks, *own_buses, n)
        from_near = exchange(for_pair, 0, 1)
        f_high, f_low, draws, likelihood = all_factors(*drawn)
        beside = exchange(for_near, 0, 1)
        far = exchange(for_far + from_near, 0, 3)
        q, block = lines // QUARTERS, scenarios // QUARTERS
        rating = lax.dynamic_slice_in_dim(line_rating, z * q, q).astype(jnp.float32) * 0.01
        scale = jnp.broadcast_to((SHARP / rating)[:, None], (q, LANES))
        to_2, to_3, to_1, own, share = quarter_flows(
            blocks, mine, beside, far, scale, f_high, f_low, lines_total
        )
        from_2 = exchange(to_2, 0, 2)
        share = share + exchange(share, 1, 0)
        share, to_3 = lax.optimization_barrier((share, to_3))
        from_3 = exchange(to_3, 0, 3)
        share = share + exchange(share, 3, 0)
        share, to_1 = lax.optimization_barrier((share, to_1))
        from_1 = exchange(to_1, 0, 1)
        flip = 4
        while flip < lax.axis_size("line"):
            share = share + exchange(share, flip + 1, 0)
            flip *= 2
        share, from_2 = lax.optimization_barrier((share, from_2))
        half = share + exchange(share, 1, 1)
        other = exchange(half, 1, 2)
        flows = own_flows(blocks, [from_2, from_3, from_1, own])
        overload, weight, new_mean = last_outputs(
            flows, blocks, half, other, likelihood, draws, proposal_mean
        )
        return (flows, overload, weight, new_mean)

    quarters = head(jnp.arange(QUARTERS, dtype=jnp.int32), *own_buses, n)
    q, groups = lines // QUARTERS, n // LANES
    per_factor = jnp.concatenate(
        [jnp.concatenate([x[j * q : j * q + q] for j in range(groups)], 1) for x in quarters], 0
    )
    base_flow = jnp.concatenate([x[groups * q, :q] for x in quarters])
    block_rows = scenarios // bus_devices
    draws = normals(directions, shifts)
    factors = dot(draws + proposal_mean[None, :], chol_factor, NT, HIGH)
    part = dot(factors, per_factor, NT, HIGH) + base_flow[None, :]
    flows = lax.psum_scatter(part, "bus", scatter_dimension=0, tiled=True)
    rating = line_rating.astype(jnp.float32) * 0.01
    own_normals = lax.dynamic_slice_in_dim(draws, z * block_rows, block_rows, 0)
    likelihood = jnp.exp(-jnp.dot(own_normals, proposal_mean, precision=HIGHEST))
    share = jnp.sum(jax.nn.softplus(SHARP * (jnp.abs(flows) / rating[None, :] - 1.0)), axis=1)
    overload = lax.psum(share, "line") / SHARP / lines_total
    emphasis = likelihood * overload
    moved_part = jnp.dot(emphasis, own_normals, precision=HIGHEST)
    moved, total = lax.psum((moved_part, jnp.sum(emphasis)), "bus")
    return (flows, overload, scenarios * emphasis / total, proposal_mean + moved / total)


def solution(mesh):
    return jax.shard_map(
        per_device,
        mesh=mesh,
        in_specs=(P("line", "bus"), P("bus"), P("bus"), P("bus"), P("line"), P(), P(), P(), P()),
        out_specs=(P("bus", "line"), P("bus"), P("bus"), P()),
        check_vma=False,
    )
```

time: 51.1 us -> 47.2 us (0.924)
  waiting for transfers between devices: 16.4 us -> 10.9 us
  Pallas kernels: 19.6 us -> 21 us
  other arithmetic: 0.89 us -> 0.19 us
  starting transfers between devices: 13.4 us -> 14.1 us
    ppermute x8 -> x11, waiting for transfers between devices: 16.4 us -> 10.9 us  [exchange(): return lax.ppermute(value, ('line', 'bus'), pairs)]
    pallas_call x4, Pallas kernels: 7.81 us -> 10.2 us  [the longest x1 5.95 us: all_factors(): pl.pallas_call(body, in_specs=[vmem] * 4, out_specs=[vmem] * 4, out_shape...]
    pallas_call x1, Pallas kernels: 11.8 us -> 10.8 us  [head(): pl.pallas_call(body, in_specs=[pl.BlockSpec(memory_space=pltpu.SMEM)] + [...]
    add x6 -> x5, other arithmetic: 0.81 us -> 0.03 us  [the longest x1 0.02 us: per_device(): far = exchange(for_far + from_near, 0, 3)]
    ppermute x8 -> x11, starting transfers between devices: 13.4 us -> 14.1 us  [exchange(): return lax.ppermute(value, ('line', 'bus'), pairs)]
  transfers between devices with their start and end apart: 8 -> 11, of which waited for: 7 -> 6; matrix products, arithmetic and copies ran while one was open for 2% -> 0% of each run, Pallas kernels for 13% -> 16%
where the time goes in v5:
time: 47.2 us; the launch traced here: 47.1 us
  Pallas kernels  21 us (44%)
  starting transfers between devices  14.1 us (30%)
  waiting for transfers between devices  10.9 us (23%)
  between operations  0.74 us (2%)
    ppermute x11, starting transfers between devices, exchange(): return lax.ppermute(value, ('line', 'bus'), pairs)  14.1 us
    ppermute x11, waiting for transfers between devices, exchange(): return lax.ppermute(value, ('line', 'bus'), pairs)  10.9 us
    pallas_call x1, Pallas kernels, head(): pl.pallas_call(body, in_specs=[pl.BlockSpec(memory_space=pltpu.SMEM)] + [...  10.8 us
    pallas_call x1, Pallas kernels, all_factors(): pl.pallas_call(body, in_specs=[vmem] * 4, out_specs=[vmem] * 4, out_shape...  5.95 us
    pallas_call x1, Pallas kernels, last_outputs(): pl.pallas_call(body, in_specs=[pl.BlockSpec(memory_space=pl.ANY), pl.Bloc...  1.49 us
    pallas_call x1, Pallas kernels, own_flows(): pl.pallas_call(body, in_specs=[pl.BlockSpec(memory_space=pltpu.SMEM)] + [...  1.4 us
    pallas_call x1, Pallas kernels, quarter_flows(): pl.pallas_call(body, in_specs=[pl.BlockSpec(memory_space=pltpu.SMEM)] + [...  1.38 us
  transfers between devices with their start and end apart: 11, of which 6 were waited for; matrix products, arithmetic and copies ran while one was open for 0% of the time, Pallas kernels for 16%

profile of v5, /device:TPU:0, one launch (start us, length us, event | category | flops | bytes accessed | tf_op | source)
XLA Modules:
  0.0 47.1 jit_solution(13966809298559348234)
XLA Ops:
  0.6 0.0 copy-start.4
  0.6 0.0 copy-start
  0.7 0.1 pad_add_fusion.blocks_s
  0.8 10.8 %segment_sums.1 = (f32[264,128]{1,0:T(8,128)S(1)}, f32[264,128]{1,0:T(8,128)S(1)}, f32[264,128]{1,0:T(8,128)S(1)}, f32[264,128]{1,0:T(8,128)S(1)}) custom-call(s32[4]{0:T(128)S(1)} %pad_add_fusion.blocks_s, bf16[256,25088]{1,0:T(8,128)(2,1)} %p_h.1, f32[196,128]{1,0:T(8,128)} %bitcast.14, f32[196,128]{1,0:T(8,128)} %bitcast.15, s32[196,128]{1,0:T(8,128)} %bitcast.16), custom_call_target="tpu_custom_call" | custom-call | flops 6576668672 | bytes 12845056 | tf_op jit(solution)/shard_map/segment_sums/pallas_call | solution.py:140
  11.5 3.1 %collective-permute-start.1 = (f32[264,128]{1,0:T(8,128)S(1)}, f32[264,128]{1,0:T(8,128)S(1)}, u32[]{:S(2)}, u32[]{:S(2)}) collective-permute-start(f32[264,128]{1,0:T(8,128)S(1)} %get-tuple-element.29), channel_id=1, source_target_pairs={{0,1},{1,0},{2,3},{3,2},{4,5},{5,4},{6,7},{7,6},{8,9},{9,8},{10,11... | collective-permute-start | bytes 405512 | tf_op jit(solution)/shard_map/ppermute | solution.py:350
  14.6 0.1 collective-permute-start
  14.7 0.1 multiply_divide_fusion
  14.8 4.2 %collective-permute-done.1 = f32[264,128]{1,0:T(8,128)S(1)} collective-permute-done((f32[264,128]{1,0:T(8,128)S(1)}, f32[264,128]{1,0:T(8,128)S(1)}, u32[]{:S(2)}, u32[]{:S(2)}) %collective-permute-start.1) | collective-permute-done | bytes 135200 | tf_op jit(solution)/shard_map/ppermute | solution.py:350
  19.1 4.2 %collective-permute-start.2 = (f32[264,128]{1,0:T(8,128)S(1)}, f32[264,128]{1,0:T(8,128)S(1)}, u32[]{:S(2)}, u32[]{:S(2)}) collective-permute-start(f32[264,128]{1,0:T(8,128)S(1)} %add.18), channel_id=1, source_target_pairs={{0,3},{1,2},{2,1},{3,0},{4,7},{5,6},{6,5},{7,4},{8,11},{9,10},{10,... | collective-permute-start | bytes 405512 | tf_op jit(solution)/shard_map/ppermute | solution.py:350
  23.3 5.9 %all_factors.1 = (bf16[1024,512]{1,0:T(8,128)(2,1)S(1)}, bf16[1024,512]{1,0:T(8,128)(2,1)S(1)}, f32[1024,512]{1,0:T(8,128)S(1)}, f32[8,128]{1,0:T(8,128)S(1)}) custom-call(s32[30,512]{1,0:T(8,128)S(1)} %copy-done.2, s32[8,512]{1,0:T(8,128)S(1)} %copy-done.3, f32[512,512]{1,0:T(8,128)S(1)} %copy-done.1, f32[1,512]{1,0:T(1,128)S(1)} %bitcast.12), custom_call_target="tpu_custom_call" | custom-call | flops 1610612736 | bytes 6291456 | tf_op jit(solution)/shard_map/all_factors/pallas_call | solution.py:207
  29.2 0.0 collective-permute-done.beside_v
  29.2 0.0 collective-permute-done.2.far_v
  29.2 0.1 broadcast_in_dim.2.scale_v
  29.3 1.4 %quarter_flows.1 = (f32[64,256]{1,0:T(8,128)S(1)}, f32[64,256]{1,0:T(8,128)S(1)}, f32[64,256]{1,0:T(8,128)S(1)}, f32[64,256]{1,0:T(8,128)S(1)}, f32[8,128]{1,0:T(8,128)S(1)}) custom-call(s32[4]{0:T(128)S(1)} %pad_add_fusion.blocks_s, f32[264,128]{1,0:T(8,128)S(1)} %get-tuple-element.26.mine_v, f32[264,128]{1,0:T(8,128)S(1)} %collective-permute-done.beside_v, ...), custom_call_target="tpu_custom_call" | custom-call | tf_op jit(solution)/shard_map/quarter_flows/pallas_call | solution.py:273
  30.7 0.1 collective-permute-start.3
  30.8 0.1 collective-permute-start.6
  30.8 1.1 %collective-permute-done.3 = f32[8,128]{1,0:T(8,128)S(1)} collective-permute-done((f32[8,128]{1,0:T(8,128)S(1)}, f32[8,128]{1,0:T(8,128)S(1)}, u32[]{:S(2)}, u32[]{:S(2)}) %collective-permute-start.3) | collective-permute-done | bytes 4128 | tf_op jit(solution)/shard_map/ppermute | solution.py:350
  31.9 1.2 %collective-permute-start.4 = (f32[8,128]{1,0:T(8,128)S(1)}, f32[8,128]{1,0:T(8,128)S(1)}, u32[]{:S(2)}, u32[]{:S(2)}) collective-permute-start(f32[8,128]{1,0:T(8,128)S(1)} %add.20), channel_id=1, source_target_pairs={{0,12},{1,13},{2,14},{3,15},{4,8},{5,9},{6,10},{7,11},{8,4},{9,5},... | collective-permute-start | bytes 12296 | tf_op jit(solution)/shard_map/ppermute | solution.py:350
  33.2 0.8 %collective-permute-start.7 = (f32[64,256]{1,0:T(8,128)S(1)}, f32[64,256]{1,0:T(8,128)S(1)}, u32[]{:S(2)}, u32[]{:S(2)}) collective-permute-start(f32[64,256]{1,0:T(8,128)S(1)} %get-tuple-element.39), channel_id=1, source_target_pairs={{0,3},{1,2},{2,1},{3,0},{4,7},{5,6},{6,5},{7,4},{8,11},{9,10},{10,... | collective-permute-start | bytes 196616 | tf_op jit(solution)/shard_map/ppermute | solution.py:350
  34.0 1.0 %collective-permute-done.4 = f32[8,128]{1,0:T(8,128)S(1)} collective-permute-done((f32[8,128]{1,0:T(8,128)S(1)}, f32[8,128]{1,0:T(8,128)S(1)}, u32[]{:S(2)}, u32[]{:S(2)}) %collective-permute-start.4) | collective-permute-done | bytes 4128 | tf_op jit(solution)/shard_map/ppermute | solution.py:350
  35.0 0.6 %collective-permute-start.8 = (f32[64,256]{1,0:T(8,128)S(1)}, f32[64,256]{1,0:T(8,128)S(1)}, u32[]{:S(2)}, u32[]{:S(2)}) collective-permute-start(f32[64,256]{1,0:T(8,128)S(1)} %get-tuple-element.40), channel_id=1, source_target_pairs={{0,1},{1,0},{2,3},{3,2},{4,5},{5,4},{6,7},{7,6},{8,9},{9,8},{10,11... | collective-permute-start | bytes 196616 | tf_op jit(solution)/shard_map/ppermute | solution.py:350
  35.6 1.0 %collective-permute-start.5 = (f32[8,128]{1,0:T(8,128)S(1)}, f32[8,128]{1,0:T(8,128)S(1)}, u32[]{:S(2)}, u32[]{:S(2)}) collective-permute-start(f32[8,128]{1,0:T(8,128)S(1)} %add.21), channel_id=1, source_target_pairs={{0,20},{1,21},{2,22},{3,23},{4,16},{5,17},{6,18},{7,19},{8,28},{9,... | collective-permute-start | bytes 12296 | tf_op jit(solution)/shard_map/ppermute | solution.py:350
  36.6 2.0 %collective-permute-done.5 = f32[8,128]{1,0:T(8,128)S(1)} collective-permute-done((f32[8,128]{1,0:T(8,128)S(1)}, f32[8,128]{1,0:T(8,128)S(1)}, u32[]{:S(2)}, u32[]{:S(2)}) %collective-permute-start.5) | collective-permute-done | bytes 4128 | tf_op jit(solution)/shard_map/ppermute | solution.py:350
  38.6 0.0 collective-permute-done.6.part_0
  38.6 1.2 %collective-permute-start.9 = (f32[8,128]{1,0:T(8,128)S(1)}, f32[8,128]{1,0:T(8,128)S(1)}, u32[]{:S(2)}, u32[]{:S(2)}) collective-permute-start(f32[8,128]{1,0:T(8,128)S(1)} %add.22), channel_id=1, source_target_pairs={{0,5},{1,4},{2,7},{3,6},{4,1},{5,0},{6,3},{7,2},{8,13},{9,12},{10,... | collective-permute-start | bytes 12296 | tf_op jit(solution)/shard_map/ppermute | solution.py:350
  39.8 1.8 %collective-permute-done.9 = f32[8,128]{1,0:T(8,128)S(1)} collective-permute-done((f32[8,128]{1,0:T(8,128)S(1)}, f32[8,128]{1,0:T(8,128)S(1)}, u32[]{:S(2)}, u32[]{:S(2)}) %collective-permute-start.9) | collective-permute-done | bytes 4128 | tf_op jit(solution)/shard_map/ppermute | solution.py:350
  41.6 1.8 %collective-permute-start.10 = (f32[8,128]{1,0:T(8,128)S(1)}, f32[8,128]{1,0:T(8,128)S(1)}, u32[]{:S(2)}, u32[]{:S(2)}) collective-permute-start(f32[8,128]{1,0:T(8,128)S(1)} %add.23.half_v), channel_id=1, source_target_pairs={{0,6},{1,7},{2,4},{3,5},{4,2},{5,3},{6,0},{7,1},{8,14},{9,15},{10,... | collective-permute-start | bytes 12296 | tf_op jit(solution)/shard_map/ppermute | solution.py:350
  43.4 0.0 collective-permute-done.7.part_1
  43.4 0.0 collective-permute-done.8.part_2
  43.4 1.4 %own_flows.1.after_h = f32[256,256]{1,0:T(8,128)} custom-call(s32[4]{0:T(128)S(1)} %pad_add_fusion.blocks_s, f32[64,256]{1,0:T(8,128)S(1)} %collective-permute-done.6.part_0, f32[64,256]{1,0:T(8,128)S(1)} %collective-permute-done.7.part_1, f32[64,256]{1,0:T(8,128)S(1)} %collective-permute-done.8.part_2, f32[64,256]{1,0:T(8,128)S(1)} %get-tuple-element.41.part_3), custom_call_target="tpu_custom_call" | custom-call | tf_op jit(solution)/shard_map/own_flows/pallas_call | solution.py:293
  44.8 0.7 %collective-permute-done.10.other_v = f32[8,128]{1,0:T(8,128)S(1)} collective-permute-done((f32[8,128]{1,0:T(8,128)S(1)}, f32[8,128]{1,0:T(8,128)S(1)}, u32[]{:S(2)}, u32[]{:S(2)}) %collective-permute-start.10) | collective-permute-done | bytes 4128 | tf_op jit(solution)/shard_map/ppermute | solution.py:350
  45.6 1.5 %last_outputs.1 = (f32[2,128]{1,0:T(2,128)}, f32[2,128]{1,0:T(2,128)}, f32[4,128]{1,0:T(4,128)}) custom-call(f32[256,256]{1,0:T(8,128)} %own_flows.1.after_h, s32[4]{0:T(128)S(1)} %pad_add_fusion.blocks_s, f32[8,128]{1,0:T(8,128)S(1)} %add.23.half_v, f32[8,128]{1,0:T(8,128)S(1)} %collective-permute-done.10.other_v, f32[8,128]{1,0:T(8,128)S(1)} %get-tuple-element.43.like_v, ...), custom_call_target="tpu_custom_call" | custom-call | tf_op jit(solution)/shard_map/last_outputs/pallas_call | solution.py:328
  (13 shorter events, 0.1 us)
Async XLA Ops:
  0.6 14.1 %copy-start.4 = (s32[256]{0:T(256)S(1)}, s32[256]{0:T(256)}, u32[]{:S(2)}) copy-start(s32[256]{0:T(256)} %param.13) | copy-start | bytes 3076
  0.6 22.6 %copy-start = (f32[512]{0:T(512)S(1)}, f32[512]{0:T(512)}, u32[]{:S(2)}) copy-start(f32[512]{0:T(512)} %param.17) | copy-start | bytes 6148
  0.7 22.6 %copy-start.1 = (f32[512,512]{1,0:T(8,128)S(1)}, f32[512,512]{1,0:T(8,128)}, u32[]{:S(2)}) copy-start(f32[512,512]{1,0:T(8,128)} %c_v.1) | copy-start | bytes 3145732
  0.7 22.6 %copy-start.3 = (s32[8,512]{1,0:T(8,128)S(1)}, s32[8,512]{1,0:T(8,128)}, u32[]{:S(2)}) copy-start(s32[8,512]{1,0:T(8,128)} %s_v.1) | copy-start | bytes 49156
  0.7 22.6 %copy-start.2 = (s32[30,512]{1,0:T(8,128)S(1)}, s32[30,512]{1,0:T(8,128)}, u32[]{:S(2)}) copy-start(s32[30,512]{1,0:T(8,128)} %d_v.1) | copy-start | bytes 184324
  11.5 7.5 %collective-permute-start.1 = (f32[264,128]{1,0:T(8,128)S(1)}, f32[264,128]{1,0:T(8,128)S(1)}, u32[]{:S(2)}, u32[]{:S(2)}) collective-permute-start(f32[264,128]{1,0:T(8,128)S(1)} %get-tuple-element.29), channel_id=1, source_target_pairs={{0,1},{1,0},{2,3},{3,2},{4,5},{5,4},{6,7},{7,6},{8,9},{9,8},{10,11... | collective-permute-start | bytes 405512 | tf_op jit(solution)/shard_map/ppermute | solution.py:350
  14.6 14.6 %collective-permute-start = (f32[264,128]{1,0:T(8,128)S(1)}, f32[264,128]{1,0:T(8,128)S(1)}, u32[]{:S(2)}, u32[]{:S(2)}) collective-permute-start(f32[264,128]{1,0:T(8,128)S(1)} %get-tuple-element.27), channel_id=1, source_target_pairs={{0,1},{1,0},{2,3},{3,2},{4,5},{5,4},{6,7},{7,6},{8,9},{9,8},{10,11... | collective-permute-start | bytes 405512 | tf_op jit(solution)/shard_map/ppermute | solution.py:350
  19.1 10.2 %collective-permute-start.2 = (f32[264,128]{1,0:T(8,128)S(1)}, f32[264,128]{1,0:T(8,128)S(1)}, u32[]{:S(2)}, u32[]{:S(2)}) collective-permute-start(f32[264,128]{1,0:T(8,128)S(1)} %add.18), channel_id=1, source_target_pairs={{0,3},{1,2},{2,1},{3,0},{4,7},{5,6},{6,5},{7,4},{8,11},{9,10},{10,... | collective-permute-start | bytes 405512 | tf_op jit(solution)/shard_map/ppermute | solution.py:350
  30.7 1.2 %collective-permute-start.3 = (f32[8,128]{1,0:T(8,128)S(1)}, f32[8,128]{1,0:T(8,128)S(1)}, u32[]{:S(2)}, u32[]{:S(2)}) collective-permute-start(f32[8,128]{1,0:T(8,128)S(1)} %get-tuple-element.32), channel_id=1, source_target_pairs={{0,4},{1,5},{2,6},{3,7},{4,0},{5,1},{6,2},{7,3},{8,12},{9,13},{10,... | collective-permute-start | bytes 12296 | tf_op jit(solution)/shard_map/ppermute | solution.py:350
  30.8 7.8 %collective-permute-start.6 = (f32[64,256]{1,0:T(8,128)S(1)}, f32[64,256]{1,0:T(8,128)S(1)}, u32[]{:S(2)}, u32[]{:S(2)}) collective-permute-start(f32[64,256]{1,0:T(8,128)S(1)} %get-tuple-element.37), channel_id=1, source_target_pairs={{0,2},{1,3},{2,0},{3,1},{4,6},{5,7},{6,4},{7,5},{8,10},{9,11},{10,... | collective-permute-start | bytes 196616 | tf_op jit(solution)/shard_map/ppermute | solution.py:350
  31.9 3.0 %collective-permute-start.4 = (f32[8,128]{1,0:T(8,128)S(1)}, f32[8,128]{1,0:T(8,128)S(1)}, u32[]{:S(2)}, u32[]{:S(2)}) collective-permute-start(f32[8,128]{1,0:T(8,128)S(1)} %add.20), channel_id=1, source_target_pairs={{0,12},{1,13},{2,14},{3,15},{4,8},{5,9},{6,10},{7,11},{8,4},{9,5},... | collective-permute-start | bytes 12296 | tf_op jit(solution)/shard_map/ppermute | solution.py:350
  33.2 10.3 %collective-permute-start.7 = (f32[64,256]{1,0:T(8,128)S(1)}, f32[64,256]{1,0:T(8,128)S(1)}, u32[]{:S(2)}, u32[]{:S(2)}) collective-permute-start(f32[64,256]{1,0:T(8,128)S(1)} %get-tuple-element.39), channel_id=1, source_target_pairs={{0,3},{1,2},{2,1},{3,0},{4,7},{5,6},{6,5},{7,4},{8,11},{9,10},{10,... | collective-permute-start | bytes 196616 | tf_op jit(solution)/shard_map/ppermute | solution.py:350
  35.0 8.5 %collective-permute-start.8 = (f32[64,256]{1,0:T(8,128)S(1)}, f32[64,256]{1,0:T(8,128)S(1)}, u32[]{:S(2)}, u32[]{:S(2)}) collective-permute-start(f32[64,256]{1,0:T(8,128)S(1)} %get-tuple-element.40), channel_id=1, source_target_pairs={{0,1},{1,0},{2,3},{3,2},{4,5},{5,4},{6,7},{7,6},{8,9},{9,8},{10,11... | collective-permute-start | bytes 196616 | tf_op jit(solution)/shard_map/ppermute | solution.py:350
  35.6 3.0 %collective-permute-start.5 = (f32[8,128]{1,0:T(8,128)S(1)}, f32[8,128]{1,0:T(8,128)S(1)}, u32[]{:S(2)}, u32[]{:S(2)}) collective-permute-start(f32[8,128]{1,0:T(8,128)S(1)} %add.21), channel_id=1, source_target_pairs={{0,20},{1,21},{2,22},{3,23},{4,16},{5,17},{6,18},{7,19},{8,28},{9,... | collective-permute-start | bytes 12296 | tf_op jit(solution)/shard_map/ppermute | solution.py:350
  38.6 3.0 %collective-permute-start.9 = (f32[8,128]{1,0:T(8,128)S(1)}, f32[8,128]{1,0:T(8,128)S(1)}, u32[]{:S(2)}, u32[]{:S(2)}) collective-permute-start(f32[8,128]{1,0:T(8,128)S(1)} %add.22), channel_id=1, source_target_pairs={{0,5},{1,4},{2,7},{3,6},{4,1},{5,0},{6,3},{7,2},{8,13},{9,12},{10,... | collective-permute-start | bytes 12296 | tf_op jit(solution)/shard_map/ppermute | solution.py:350
  41.6 3.9 %collective-permute-start.10 = (f32[8,128]{1,0:T(8,128)S(1)}, f32[8,128]{1,0:T(8,128)S(1)}, u32[]{:S(2)}, u32[]{:S(2)}) collective-permute-start(f32[8,128]{1,0:T(8,128)S(1)} %add.23.half_v), channel_id=1, source_target_pairs={{0,6},{1,7},{2,4},{3,5},{4,2},{5,3},{6,0},{7,1},{8,14},{9,15},{10,... | collective-permute-start | bytes 12296 | tf_op jit(solution)/shard_map/ppermute | solution.py:350

commit v6 on v5

--- a/solution.py
+++ b/solution.py
@@ -65,17 +65,17 @@
     return jnp.concatenate(pieces, 0) if len(pieces) > 1 else pieces[0]
 
 
-def block_width(buses):
-    for width in (6272, 3584, 1792, 896, 512, 256):
-        if buses % width == 0:
-            return width
-    return LANES
+def block_plan(buses):
+    for first, later in ((3584, 7168), (6272, 6272), (3584, 3584), (1792, 1792), (896, 896), (256, 256)):
+        if buses >= first and (buses - first) % later == 0:
+            return first, later
+    return LANES, LANES
 
 
 def head(blocks, ptdf, base, gain, factor, n):
     lines, buses = ptdf.shape
-    width = block_width(buses)
-    steps, rows, per = buses // width, buses // LANES, width // LANES
+    first, later = block_plan(buses)
+    steps, rows = 1 + (buses - first) // later, buses // LANES
     q, groups = lines // QUARTERS, n // LANES
 
     def body(
@@ -87,27 +87,33 @@
         for copy in small:
             copy.start()
 
-        def block_copy(k):
-            at = pl.ds(pl.multiple_of(k * width, width), width)
+        def place(k):
+            return pl.multiple_of(first + (k - 1) * later, LANES)
+
+        def block_copy(k, begin, width):
+            at = pl.ds(begin, width)
             return pltpu.make_async_copy(p_h.at[:, at], p_v.at[:, at], p_sem.at[k])
 
         def start(k, _):
-            block_copy(k).start()
+            block_copy(k, place(k), later).start()
             return 0
 
-        lax.fori_loop(0, steps, start, 0)
+        block_copy(0, 0, first).start()
+        lax.fori_loop(1, steps, start, 0)
         sums[...] = jnp.zeros_like(sums)
         for copy in small:
             copy.wait()
 
-        def step(k, _):
-            block_copy(k).wait()
+        def add_block(k, begin, width):
+            block_copy(k, begin, width).wait()
 
             def row(v):
-                return jnp.concatenate([v[pl.ds(k * per + j, 1), :] for j in range(per)], 1)
+                return jnp.concatenate(
+                    [v[pl.ds(begin // LANES + j, 1), :] for j in range(width // LANES)], 1
+                )
 
             g = row(g_v)
-            p = p_v[:, pl.ds(pl.multiple_of(k * width, width), width)]
+            p = p_v[:, pl.ds(begin, width)]
             scaled = (p.astype(jnp.float32) * g).astype(jnp.bfloat16)
             own = lax.broadcasted_iota(jnp.int16, (n, width), 0) == row(f_v).astype(jnp.int16)
             hot = jnp.where(own, jnp.bfloat16(1), jnp.bfloat16(0))
@@ -117,9 +123,13 @@
             rest = jnp.zeros((EXTRA - 2, width), jnp.bfloat16)
             left = jnp.concatenate([hot, high, low, rest], 0)
             sums[...] += lax.dot_general(left, scaled, NT, preferred_element_type=jnp.float32)
+
+        def step(k, _):
+            add_block(k, place(k), later)
             return 0
 
-        lax.fori_loop(0, steps, step, 0)
+        add_block(0, 0, first)
+        lax.fori_loop(1, steps, step, 0)
         flipped[...] = sums[:n, :].T
         base_row = sums[n : n + 1, :] + sums[n + 1 : n + 2, :]
         blank = jnp.zeros((1, LANES - q), jnp.float32)

time: 47.2 us -> 46.7 us (0.989)
  Pallas kernels: 21 us -> 20.5 us
    pallas_call x1, Pallas kernels: 10.8 us -> 10.3 us  [head(): pl.pallas_call(body, in_specs=[pl.BlockSpec(memory_space=pltpu.SMEM)] + [...]
where the time goes in v6:
time: 46.7 us; the launch traced here: 46.6 us
  Pallas kernels  20.5 us (44%)
  starting transfers between devices  14.1 us (30%)
  waiting for transfers between devices  10.9 us (23%)
  between operations  0.74 us (2%)
    ppermute x11, starting transfers between devices, exchange(): return lax.ppermute(value, ('line', 'bus'), pairs)  14.1 us
    ppermute x11, waiting for transfers between devices, exchange(): return lax.ppermute(value, ('line', 'bus'), pairs)  10.9 us
    pallas_call x1, Pallas kernels, head(): pl.pallas_call(body, in_specs=[pl.BlockSpec(memory_space=pltpu.SMEM)] + [...  10.3 us
    pallas_call x1, Pallas kernels, all_factors(): pl.pallas_call(body, in_specs=[vmem] * 4, out_specs=[vmem] * 4, out_shape...  5.95 us
    pallas_call x1, Pallas kernels, last_outputs(): pl.pallas_call(body, in_specs=[pl.BlockSpec(memory_space=pl.ANY), pl.Bloc...  1.49 us
    pallas_call x1, Pallas kernels, own_flows(): pl.pallas_call(body, in_specs=[pl.BlockSpec(memory_space=pltpu.SMEM)] + [...  1.4 us
    pallas_call x1, Pallas kernels, quarter_flows(): pl.pallas_call(body, in_specs=[pl.BlockSpec(memory_space=pltpu.SMEM)] + [...  1.38 us
  transfers between devices with their start and end apart: 11, of which 6 were waited for; matrix products, arithmetic and copies ran while one was open for 0% of the time, Pallas kernels for 16%

profile of v6, /device:TPU:0, one launch (start us, length us, event | category | flops | bytes accessed | tf_op | source)
XLA Modules:
  0.0 46.6 jit_solution(4468829780480333924)
XLA Ops:
  0.6 0.0 copy-start.4
  0.6 0.0 copy-start
  0.7 0.1 pad_add_fusion.blocks_s
  0.8 10.3 %segment_sums.1 = (f32[264,128]{1,0:T(8,128)S(1)}, f32[264,128]{1,0:T(8,128)S(1)}, f32[264,128]{1,0:T(8,128)S(1)}, f32[264,128]{1,0:T(8,128)S(1)}) custom-call(s32[4]{0:T(128)S(1)} %pad_add_fusion.blocks_s, bf16[256,25088]{1,0:T(8,128)(2,1)} %p_h.1, f32[196,128]{1,0:T(8,128)} %bitcast.14, f32[196,128]{1,0:T(8,128)} %bitcast.15, s32[196,128]{1,0:T(8,128)} %bitcast.16), custom_call_target="tpu_custom_call" | custom-call | flops 6576668672 | bytes 12845056 | tf_op jit(solution)/shard_map/segment_sums/pallas_call | solution.py:150
  11.1 3.1 %collective-permute-start.1 = (f32[264,128]{1,0:T(8,128)S(1)}, f32[264,128]{1,0:T(8,128)S(1)}, u32[]{:S(2)}, u32[]{:S(2)}) collective-permute-start(f32[264,128]{1,0:T(8,128)S(1)} %get-tuple-element.29), channel_id=1, source_target_pairs={{0,1},{1,0},{2,3},{3,2},{4,5},{5,4},{6,7},{7,6},{8,9},{9,8},{10,11... | collective-permute-start | bytes 405512 | tf_op jit(solution)/shard_map/ppermute | solution.py:360
  14.1 0.1 collective-permute-start
  14.2 0.1 multiply_divide_fusion
  14.3 4.3 %collective-permute-done.1 = f32[264,128]{1,0:T(8,128)S(1)} collective-permute-done((f32[264,128]{1,0:T(8,128)S(1)}, f32[264,128]{1,0:T(8,128)S(1)}, u32[]{:S(2)}, u32[]{:S(2)}) %collective-permute-start.1) | collective-permute-done | bytes 135200 | tf_op jit(solution)/shard_map/ppermute | solution.py:360
  18.6 4.2 %collective-permute-start.2 = (f32[264,128]{1,0:T(8,128)S(1)}, f32[264,128]{1,0:T(8,128)S(1)}, u32[]{:S(2)}, u32[]{:S(2)}) collective-permute-start(f32[264,128]{1,0:T(8,128)S(1)} %add.18), channel_id=1, source_target_pairs={{0,3},{1,2},{2,1},{3,0},{4,7},{5,6},{6,5},{7,4},{8,11},{9,10},{10,... | collective-permute-start | bytes 405512 | tf_op jit(solution)/shard_map/ppermute | solution.py:360
  22.7 6.0 %all_factors.1 = (bf16[1024,512]{1,0:T(8,128)(2,1)S(1)}, bf16[1024,512]{1,0:T(8,128)(2,1)S(1)}, f32[1024,512]{1,0:T(8,128)S(1)}, f32[8,128]{1,0:T(8,128)S(1)}) custom-call(s32[30,512]{1,0:T(8,128)S(1)} %copy-done.2, s32[8,512]{1,0:T(8,128)S(1)} %copy-done.3, f32[512,512]{1,0:T(8,128)S(1)} %copy-done.1, f32[1,512]{1,0:T(1,128)S(1)} %bitcast.12), custom_call_target="tpu_custom_call" | custom-call | flops 1610612736 | bytes 6291456 | tf_op jit(solution)/shard_map/all_factors/pallas_call | solution.py:217
  28.7 0.0 collective-permute-done.beside_v
  28.7 0.0 collective-permute-done.2.far_v
  28.7 0.1 broadcast_in_dim.2.scale_v
  28.8 1.4 %quarter_flows.1 = (f32[64,256]{1,0:T(8,128)S(1)}, f32[64,256]{1,0:T(8,128)S(1)}, f32[64,256]{1,0:T(8,128)S(1)}, f32[64,256]{1,0:T(8,128)S(1)}, f32[8,128]{1,0:T(8,128)S(1)}) custom-call(s32[4]{0:T(128)S(1)} %pad_add_fusion.blocks_s, f32[264,128]{1,0:T(8,128)S(1)} %get-tuple-element.26.mine_v, f32[264,128]{1,0:T(8,128)S(1)} %collective-permute-done.beside_v, ...), custom_call_target="tpu_custom_call" | custom-call | tf_op jit(solution)/shard_map/quarter_flows/pallas_call | solution.py:283
  30.2 0.1 collective-permute-start.3
  30.2 0.1 collective-permute-start.6
  30.3 1.1 %collective-permute-done.3 = f32[8,128]{1,0:T(8,128)S(1)} collective-permute-done((f32[8,128]{1,0:T(8,128)S(1)}, f32[8,128]{1,0:T(8,128)S(1)}, u32[]{:S(2)}, u32[]{:S(2)}) %collective-permute-start.3) | collective-permute-done | bytes 4128 | tf_op jit(solution)/shard_map/ppermute | solution.py:360
  31.4 1.3 %collective-permute-start.4 = (f32[8,128]{1,0:T(8,128)S(1)}, f32[8,128]{1,0:T(8,128)S(1)}, u32[]{:S(2)}, u32[]{:S(2)}) collective-permute-start(f32[8,128]{1,0:T(8,128)S(1)} %add.20), channel_id=1, source_target_pairs={{0,12},{1,13},{2,14},{3,15},{4,8},{5,9},{6,10},{7,11},{8,4},{9,5},... | collective-permute-start | bytes 12296 | tf_op jit(solution)/shard_map/ppermute | solution.py:360
  32.7 0.8 %collective-permute-start.7 = (f32[64,256]{1,0:T(8,128)S(1)}, f32[64,256]{1,0:T(8,128)S(1)}, u32[]{:S(2)}, u32[]{:S(2)}) collective-permute-start(f32[64,256]{1,0:T(8,128)S(1)} %get-tuple-element.39), channel_id=1, source_target_pairs={{0,3},{1,2},{2,1},{3,0},{4,7},{5,6},{6,5},{7,4},{8,11},{9,10},{10,... | collective-permute-start | bytes 196616 | tf_op jit(solution)/shard_map/ppermute | solution.py:360
  33.5 0.9 %collective-permute-done.4 = f32[8,128]{1,0:T(8,128)S(1)} collective-permute-done((f32[8,128]{1,0:T(8,128)S(1)}, f32[8,128]{1,0:T(8,128)S(1)}, u32[]{:S(2)}, u32[]{:S(2)}) %collective-permute-start.4) | collective-permute-done | bytes 4128 | tf_op jit(solution)/shard_map/ppermute | solution.py:360
  34.4 0.6 %collective-permute-start.8 = (f32[64,256]{1,0:T(8,128)S(1)}, f32[64,256]{1,0:T(8,128)S(1)}, u32[]{:S(2)}, u32[]{:S(2)}) collective-permute-start(f32[64,256]{1,0:T(8,128)S(1)} %get-tuple-element.40), channel_id=1, source_target_pairs={{0,1},{1,0},{2,3},{3,2},{4,5},{5,4},{6,7},{7,6},{8,9},{9,8},{10,11... | collective-permute-start | bytes 196616 | tf_op jit(solution)/shard_map/ppermute | solution.py:360
  35.1 1.0 %collective-permute-start.5 = (f32[8,128]{1,0:T(8,128)S(1)}, f32[8,128]{1,0:T(8,128)S(1)}, u32[]{:S(2)}, u32[]{:S(2)}) collective-permute-start(f32[8,128]{1,0:T(8,128)S(1)} %add.21), channel_id=1, source_target_pairs={{0,20},{1,21},{2,22},{3,23},{4,16},{5,17},{6,18},{7,19},{8,28},{9,... | collective-permute-start | bytes 12296 | tf_op jit(solution)/shard_map/ppermute | solution.py:360
  36.1 2.0 %collective-permute-done.5 = f32[8,128]{1,0:T(8,128)S(1)} collective-permute-done((f32[8,128]{1,0:T(8,128)S(1)}, f32[8,128]{1,0:T(8,128)S(1)}, u32[]{:S(2)}, u32[]{:S(2)}) %collective-permute-start.5) | collective-permute-done | bytes 4128 | tf_op jit(solution)/shard_map/ppermute | solution.py:360
  38.1 0.0 collective-permute-done.6.part_0
  38.1 1.2 %collective-permute-start.9 = (f32[8,128]{1,0:T(8,128)S(1)}, f32[8,128]{1,0:T(8,128)S(1)}, u32[]{:S(2)}, u32[]{:S(2)}) collective-permute-start(f32[8,128]{1,0:T(8,128)S(1)} %add.22), channel_id=1, source_target_pairs={{0,5},{1,4},{2,7},{3,6},{4,1},{5,0},{6,3},{7,2},{8,13},{9,12},{10,... | collective-permute-start | bytes 12296 | tf_op jit(solution)/shard_map/ppermute | solution.py:360
  39.3 1.8 %collective-permute-done.9 = f32[8,128]{1,0:T(8,128)S(1)} collective-permute-done((f32[8,128]{1,0:T(8,128)S(1)}, f32[8,128]{1,0:T(8,128)S(1)}, u32[]{:S(2)}, u32[]{:S(2)}) %collective-permute-start.9) | collective-permute-done | bytes 4128 | tf_op jit(solution)/shard_map/ppermute | solution.py:360
  41.1 1.8 %collective-permute-start.10 = (f32[8,128]{1,0:T(8,128)S(1)}, f32[8,128]{1,0:T(8,128)S(1)}, u32[]{:S(2)}, u32[]{:S(2)}) collective-permute-start(f32[8,128]{1,0:T(8,128)S(1)} %add.23.half_v), channel_id=1, source_target_pairs={{0,6},{1,7},{2,4},{3,5},{4,2},{5,3},{6,0},{7,1},{8,14},{9,15},{10,... | collective-permute-start | bytes 12296 | tf_op jit(solution)/shard_map/ppermute | solution.py:360
  42.9 0.0 collective-permute-done.7.part_1
  42.9 0.0 collective-permute-done.8.part_2
  42.9 1.4 %own_flows.1.after_h = f32[256,256]{1,0:T(8,128)} custom-call(s32[4]{0:T(128)S(1)} %pad_add_fusion.blocks_s, f32[64,256]{1,0:T(8,128)S(1)} %collective-permute-done.6.part_0, f32[64,256]{1,0:T(8,128)S(1)} %collective-permute-done.7.part_1, f32[64,256]{1,0:T(8,128)S(1)} %collective-permute-done.8.part_2, f32[64,256]{1,0:T(8,128)S(1)} %get-tuple-element.41.part_3), custom_call_target="tpu_custom_call" | custom-call | tf_op jit(solution)/shard_map/own_flows/pallas_call | solution.py:303
  44.3 0.7 %collective-permute-done.10.other_v = f32[8,128]{1,0:T(8,128)S(1)} collective-permute-done((f32[8,128]{1,0:T(8,128)S(1)}, f32[8,128]{1,0:T(8,128)S(1)}, u32[]{:S(2)}, u32[]{:S(2)}) %collective-permute-start.10) | collective-permute-done | bytes 4128 | tf_op jit(solution)/shard_map/ppermute | solution.py:360
  45.1 1.5 %last_outputs.1 = (f32[2,128]{1,0:T(2,128)}, f32[2,128]{1,0:T(2,128)}, f32[4,128]{1,0:T(4,128)}) custom-call(f32[256,256]{1,0:T(8,128)} %own_flows.1.after_h, s32[4]{0:T(128)S(1)} %pad_add_fusion.blocks_s, f32[8,128]{1,0:T(8,128)S(1)} %add.23.half_v, f32[8,128]{1,0:T(8,128)S(1)} %collective-permute-done.10.other_v, f32[8,128]{1,0:T(8,128)S(1)} %get-tuple-element.43.like_v, ...), custom_call_target="tpu_custom_call" | custom-call | tf_op jit(solution)/shard_map/last_outputs/pallas_call | solution.py:338
  (13 shorter events, 0.1 us)
Async XLA Ops:
  0.6 13.6 %copy-start.4 = (s32[256]{0:T(256)S(1)}, s32[256]{0:T(256)}, u32[]{:S(2)}) copy-start(s32[256]{0:T(256)} %param.13) | copy-start | bytes 3076
  0.6 22.1 %copy-start = (f32[512]{0:T(512)S(1)}, f32[512]{0:T(512)}, u32[]{:S(2)}) copy-start(f32[512]{0:T(512)} %param.17) | copy-start | bytes 6148
  0.7 22.1 %copy-start.1 = (f32[512,512]{1,0:T(8,128)S(1)}, f32[512,512]{1,0:T(8,128)}, u32[]{:S(2)}) copy-start(f32[512,512]{1,0:T(8,128)} %c_v.1) | copy-start | bytes 3145732
  0.7 22.1 %copy-start.3 = (s32[8,512]{1,0:T(8,128)S(1)}, s32[8,512]{1,0:T(8,128)}, u32[]{:S(2)}) copy-start(s32[8,512]{1,0:T(8,128)} %s_v.1) | copy-start | bytes 49156
  0.7 22.1 %copy-start.2 = (s32[30,512]{1,0:T(8,128)S(1)}, s32[30,512]{1,0:T(8,128)}, u32[]{:S(2)}) copy-start(s32[30,512]{1,0:T(8,128)} %d_v.1) | copy-start | bytes 184324
  11.1 7.5 %collective-permute-start.1 = (f32[264,128]{1,0:T(8,128)S(1)}, f32[264,128]{1,0:T(8,128)S(1)}, u32[]{:S(2)}, u32[]{:S(2)}) collective-permute-start(f32[264,128]{1,0:T(8,128)S(1)} %get-tuple-element.29), channel_id=1, source_target_pairs={{0,1},{1,0},{2,3},{3,2},{4,5},{5,4},{6,7},{7,6},{8,9},{9,8},{10,11... | collective-permute-start | bytes 405512 | tf_op jit(solution)/shard_map/ppermute | solution.py:360
  14.1 14.6 %collective-permute-start = (f32[264,128]{1,0:T(8,128)S(1)}, f32[264,128]{1,0:T(8,128)S(1)}, u32[]{:S(2)}, u32[]{:S(2)}) collective-permute-start(f32[264,128]{1,0:T(8,128)S(1)} %get-tuple-element.27), channel_id=1, source_target_pairs={{0,1},{1,0},{2,3},{3,2},{4,5},{5,4},{6,7},{7,6},{8,9},{9,8},{10,11... | collective-permute-start | bytes 405512 | tf_op jit(solution)/shard_map/ppermute | solution.py:360
  18.6 10.1 %collective-permute-start.2 = (f32[264,128]{1,0:T(8,128)S(1)}, f32[264,128]{1,0:T(8,128)S(1)}, u32[]{:S(2)}, u32[]{:S(2)}) collective-permute-start(f32[264,128]{1,0:T(8,128)S(1)} %add.18), channel_id=1, source_target_pairs={{0,3},{1,2},{2,1},{3,0},{4,7},{5,6},{6,5},{7,4},{8,11},{9,10},{10,... | collective-permute-start | bytes 405512 | tf_op jit(solution)/shard_map/ppermute | solution.py:360
  30.2 1.2 %collective-permute-start.3 = (f32[8,128]{1,0:T(8,128)S(1)}, f32[8,128]{1,0:T(8,128)S(1)}, u32[]{:S(2)}, u32[]{:S(2)}) collective-permute-start(f32[8,128]{1,0:T(8,128)S(1)} %get-tuple-element.32), channel_id=1, source_target_pairs={{0,4},{1,5},{2,6},{3,7},{4,0},{5,1},{6,2},{7,3},{8,12},{9,13},{10,... | collective-permute-start | bytes 12296 | tf_op jit(solution)/shard_map/ppermute | solution.py:360
  30.2 7.9 %collective-permute-start.6 = (f32[64,256]{1,0:T(8,128)S(1)}, f32[64,256]{1,0:T(8,128)S(1)}, u32[]{:S(2)}, u32[]{:S(2)}) collective-permute-start(f32[64,256]{1,0:T(8,128)S(1)} %get-tuple-element.37), channel_id=1, source_target_pairs={{0,2},{1,3},{2,0},{3,1},{4,6},{5,7},{6,4},{7,5},{8,10},{9,11},{10,... | collective-permute-start | bytes 196616 | tf_op jit(solution)/shard_map/ppermute | solution.py:360
  31.4 3.0 %collective-permute-start.4 = (f32[8,128]{1,0:T(8,128)S(1)}, f32[8,128]{1,0:T(8,128)S(1)}, u32[]{:S(2)}, u32[]{:S(2)}) collective-permute-start(f32[8,128]{1,0:T(8,128)S(1)} %add.20), channel_id=1, source_target_pairs={{0,12},{1,13},{2,14},{3,15},{4,8},{5,9},{6,10},{7,11},{8,4},{9,5},... | collective-permute-start | bytes 12296 | tf_op jit(solution)/shard_map/ppermute | solution.py:360
  32.7 10.3 %collective-permute-start.7 = (f32[64,256]{1,0:T(8,128)S(1)}, f32[64,256]{1,0:T(8,128)S(1)}, u32[]{:S(2)}, u32[]{:S(2)}) collective-permute-start(f32[64,256]{1,0:T(8,128)S(1)} %get-tuple-element.39), channel_id=1, source_target_pairs={{0,3},{1,2},{2,1},{3,0},{4,7},{5,6},{6,5},{7,4},{8,11},{9,10},{10,... | collective-permute-start | bytes 196616 | tf_op jit(solution)/shard_map/ppermute | solution.py:360
  34.4 8.5 %collective-permute-start.8 = (f32[64,256]{1,0:T(8,128)S(1)}, f32[64,256]{1,0:T(8,128)S(1)}, u32[]{:S(2)}, u32[]{:S(2)}) collective-permute-start(f32[64,256]{1,0:T(8,128)S(1)} %get-tuple-element.40), channel_id=1, source_target_pairs={{0,1},{1,0},{2,3},{3,2},{4,5},{5,4},{6,7},{7,6},{8,9},{9,8},{10,11... | collective-permute-start | bytes 196616 | tf_op jit(solution)/shard_map/ppermute | solution.py:360
  35.1 3.0 %collective-permute-start.5 = (f32[8,128]{1,0:T(8,128)S(1)}, f32[8,128]{1,0:T(8,128)S(1)}, u32[]{:S(2)}, u32[]{:S(2)}) collective-permute-start(f32[8,128]{1,0:T(8,128)S(1)} %add.21), channel_id=1, source_target_pairs={{0,20},{1,21},{2,22},{3,23},{4,16},{5,17},{6,18},{7,19},{8,28},{9,... | collective-permute-start | bytes 12296 | tf_op jit(solution)/shard_map/ppermute | solution.py:360
  38.1 3.0 %collective-permute-start.9 = (f32[8,128]{1,0:T(8,128)S(1)}, f32[8,128]{1,0:T(8,128)S(1)}, u32[]{:S(2)}, u32[]{:S(2)}) collective-permute-start(f32[8,128]{1,0:T(8,128)S(1)} %add.22), channel_id=1, source_target_pairs={{0,5},{1,4},{2,7},{3,6},{4,1},{5,0},{6,3},{7,2},{8,13},{9,12},{10,... | collective-permute-start | bytes 12296 | tf_op jit(solution)/shard_map/ppermute | solution.py:360
  41.1 3.9 %collective-permute-start.10 = (f32[8,128]{1,0:T(8,128)S(1)}, f32[8,128]{1,0:T(8,128)S(1)}, u32[]{:S(2)}, u32[]{:S(2)}) collective-permute-start(f32[8,128]{1,0:T(8,128)S(1)} %add.23.half_v), channel_id=1, source_target_pairs={{0,6},{1,7},{2,4},{3,5},{4,2},{5,3},{6,0},{7,1},{8,14},{9,15},{10,... | collective-permute-start | bytes 12296 | tf_op jit(solution)/shard_map/ppermute | solution.py:360

commit v7 on v6

--- a/solution.py
+++ b/solution.py
@@ -84,8 +84,6 @@
     ):
         pairs = ((f_h, f_v), (g_h, g_v), (b_h, b_v))
         small = [pltpu.make_async_copy(h, v, v_sem.at[i]) for i, (h, v) in enumerate(pairs)]
-        for copy in small:
-            copy.start()
 
         def place(k):
             return pl.multiple_of(first + (k - 1) * later, LANES)
@@ -99,12 +97,13 @@
             return 0
 
         block_copy(0, 0, first).start()
+        for copy in small:
+            copy.start()
         lax.fori_loop(1, steps, start, 0)
-        sums[...] = jnp.zeros_like(sums)
         for copy in small:
             copy.wait()
 
-        def add_block(k, begin, width):
+        def block_sums(k, begin, width):
             block_copy(k, begin, width).wait()
 
             def row(v):
@@ -122,13 +121,13 @@
             low = (ratio - high.astype(jnp.float32)).astype(jnp.bfloat16)
             rest = jnp.zeros((EXTRA - 2, width), jnp.bfloat16)
             left = jnp.concatenate([hot, high, low, rest], 0)
-            sums[...] += lax.dot_general(left, scaled, NT, preferred_element_type=jnp.float32)
+            return lax.dot_general(left, scaled, NT, preferred_element_type=jnp.float32)
 
         def step(k, _):
-            add_block(k, place(k), later)
+            sums[...] += block_sums(k, place(k), later)
             return 0
 
-        add_block(0, 0, first)
+        sums[...] = block_sums(0, 0, first)
         lax.fori_loop(1, steps, step, 0)
         flipped[...] = sums[:n, :].T
         base_row = sums[n : n + 1, :] + sums[n + 1 : n + 2, :]

time: 46.7 us -> 46.8 us (level)
  no operation moved by 1% of the time
where the time goes in v7:
time: 46.8 us; the launch traced here: 46.6 us
  Pallas kernels  20.5 us (44%)
  starting transfers between devices  14.1 us (30%)
  waiting for transfers between devices  10.9 us (23%)
  between operations  0.74 us (2%)
    ppermute x11, starting transfers between devices, exchange(): return lax.ppermute(value, ('line', 'bus'), pairs)  14.1 us
    ppermute x11, waiting for transfers between devices, exchange(): return lax.ppermute(value, ('line', 'bus'), pairs)  10.9 us
    pallas_call x1, Pallas kernels, head(): pl.pallas_call(body, in_specs=[pl.BlockSpec(memory_space=pltpu.SMEM)] + [...  10.3 us
    pallas_call x1, Pallas kernels, all_factors(): pl.pallas_call(body, in_specs=[vmem] * 4, out_specs=[vmem] * 4, out_shape...  5.95 us
    pallas_call x1, Pallas kernels, last_outputs(): pl.pallas_call(body, in_specs=[pl.BlockSpec(memory_space=pl.ANY), pl.Bloc...  1.49 us
    pallas_call x1, Pallas kernels, own_flows(): pl.pallas_call(body, in_specs=[pl.BlockSpec(memory_space=pltpu.SMEM)] + [...  1.4 us
    pallas_call x1, Pallas kernels, quarter_flows(): pl.pallas_call(body, in_specs=[pl.BlockSpec(memory_space=pltpu.SMEM)] + [...  1.38 us
  transfers between devices with their start and end apart: 11, of which 6 were waited for; matrix products, arithmetic and copies ran while one was open for 0% of the time, Pallas kernels for 16%

profile of v7, /device:TPU:0, one launch (start us, length us, event | category | flops | bytes accessed | tf_op | source)
XLA Modules:
  0.0 46.6 jit_solution(2596058294994900603)
XLA Ops:
  0.6 0.0 copy-start.4
  0.6 0.0 copy-start
  0.7 0.1 pad_add_fusion.blocks_s
  0.8 10.3 %segment_sums.1 = (f32[264,128]{1,0:T(8,128)S(1)}, f32[264,128]{1,0:T(8,128)S(1)}, f32[264,128]{1,0:T(8,128)S(1)}, f32[264,128]{1,0:T(8,128)S(1)}) custom-call(s32[4]{0:T(128)S(1)} %pad_add_fusion.blocks_s, bf16[256,25088]{1,0:T(8,128)(2,1)} %p_h.1, f32[196,128]{1,0:T(8,128)} %bitcast.14, f32[196,128]{1,0:T(8,128)} %bitcast.15, s32[196,128]{1,0:T(8,128)} %bitcast.16), custom_call_target="tpu_custom_call" | custom-call | flops 6576668672 | bytes 12845056 | tf_op jit(solution)/shard_map/segment_sums/pallas_call | solution.py:149
  11.1 3.1 %collective-permute-start.1 = (f32[264,128]{1,0:T(8,128)S(1)}, f32[264,128]{1,0:T(8,128)S(1)}, u32[]{:S(2)}, u32[]{:S(2)}) collective-permute-start(f32[264,128]{1,0:T(8,128)S(1)} %get-tuple-element.29), channel_id=1, source_target_pairs={{0,1},{1,0},{2,3},{3,2},{4,5},{5,4},{6,7},{7,6},{8,9},{9,8},{10,11... | collective-permute-start | bytes 405512 | tf_op jit(solution)/shard_map/ppermute | solution.py:359
  14.2 0.1 collective-permute-start
  14.3 0.1 multiply_divide_fusion
  14.3 4.3 %collective-permute-done.1 = f32[264,128]{1,0:T(8,128)S(1)} collective-permute-done((f32[264,128]{1,0:T(8,128)S(1)}, f32[264,128]{1,0:T(8,128)S(1)}, u32[]{:S(2)}, u32[]{:S(2)}) %collective-permute-start.1) | collective-permute-done | bytes 135200 | tf_op jit(solution)/shard_map/ppermute | solution.py:359
  18.6 4.2 %collective-permute-start.2 = (f32[264,128]{1,0:T(8,128)S(1)}, f32[264,128]{1,0:T(8,128)S(1)}, u32[]{:S(2)}, u32[]{:S(2)}) collective-permute-start(f32[264,128]{1,0:T(8,128)S(1)} %add.18), channel_id=1, source_target_pairs={{0,3},{1,2},{2,1},{3,0},{4,7},{5,6},{6,5},{7,4},{8,11},{9,10},{10,... | collective-permute-start | bytes 405512 | tf_op jit(solution)/shard_map/ppermute | solution.py:359
  22.8 6.0 %all_factors.1 = (bf16[1024,512]{1,0:T(8,128)(2,1)S(1)}, bf16[1024,512]{1,0:T(8,128)(2,1)S(1)}, f32[1024,512]{1,0:T(8,128)S(1)}, f32[8,128]{1,0:T(8,128)S(1)}) custom-call(s32[30,512]{1,0:T(8,128)S(1)} %copy-done.2, s32[8,512]{1,0:T(8,128)S(1)} %copy-done.3, f32[512,512]{1,0:T(8,128)S(1)} %copy-done.1, f32[1,512]{1,0:T(1,128)S(1)} %bitcast.12), custom_call_target="tpu_custom_call" | custom-call | flops 1610612736 | bytes 6291456 | tf_op jit(solution)/shard_map/all_factors/pallas_call | solution.py:216
  28.7 0.0 collective-permute-done.beside_v
  28.8 0.0 collective-permute-done.2.far_v
  28.8 0.1 broadcast_in_dim.2.scale_v
  28.8 1.4 %quarter_flows.1 = (f32[64,256]{1,0:T(8,128)S(1)}, f32[64,256]{1,0:T(8,128)S(1)}, f32[64,256]{1,0:T(8,128)S(1)}, f32[64,256]{1,0:T(8,128)S(1)}, f32[8,128]{1,0:T(8,128)S(1)}) custom-call(s32[4]{0:T(128)S(1)} %pad_add_fusion.blocks_s, f32[264,128]{1,0:T(8,128)S(1)} %get-tuple-element.26.mine_v, f32[264,128]{1,0:T(8,128)S(1)} %collective-permute-done.beside_v, ...), custom_call_target="tpu_custom_call" | custom-call | tf_op jit(solution)/shard_map/quarter_flows/pallas_call | solution.py:282
  30.2 0.1 collective-permute-start.3
  30.3 0.1 collective-permute-start.6
  30.4 1.1 %collective-permute-done.3 = f32[8,128]{1,0:T(8,128)S(1)} collective-permute-done((f32[8,128]{1,0:T(8,128)S(1)}, f32[8,128]{1,0:T(8,128)S(1)}, u32[]{:S(2)}, u32[]{:S(2)}) %collective-permute-start.3) | collective-permute-done | bytes 4128 | tf_op jit(solution)/shard_map/ppermute | solution.py:359
  31.5 1.3 %collective-permute-start.4 = (f32[8,128]{1,0:T(8,128)S(1)}, f32[8,128]{1,0:T(8,128)S(1)}, u32[]{:S(2)}, u32[]{:S(2)}) collective-permute-start(f32[8,128]{1,0:T(8,128)S(1)} %add.20), channel_id=1, source_target_pairs={{0,12},{1,13},{2,14},{3,15},{4,8},{5,9},{6,10},{7,11},{8,4},{9,5},... | collective-permute-start | bytes 12296 | tf_op jit(solution)/shard_map/ppermute | solution.py:359
  32.7 0.8 %collective-permute-start.7 = (f32[64,256]{1,0:T(8,128)S(1)}, f32[64,256]{1,0:T(8,128)S(1)}, u32[]{:S(2)}, u32[]{:S(2)}) collective-permute-start(f32[64,256]{1,0:T(8,128)S(1)} %get-tuple-element.39), channel_id=1, source_target_pairs={{0,3},{1,2},{2,1},{3,0},{4,7},{5,6},{6,5},{7,4},{8,11},{9,10},{10,... | collective-permute-start | bytes 196616 | tf_op jit(solution)/shard_map/ppermute | solution.py:359
  33.5 0.9 %collective-permute-done.4 = f32[8,128]{1,0:T(8,128)S(1)} collective-permute-done((f32[8,128]{1,0:T(8,128)S(1)}, f32[8,128]{1,0:T(8,128)S(1)}, u32[]{:S(2)}, u32[]{:S(2)}) %collective-permute-start.4) | collective-permute-done | bytes 4128 | tf_op jit(solution)/shard_map/ppermute | solution.py:359
  34.5 0.6 %collective-permute-start.8 = (f32[64,256]{1,0:T(8,128)S(1)}, f32[64,256]{1,0:T(8,128)S(1)}, u32[]{:S(2)}, u32[]{:S(2)}) collective-permute-start(f32[64,256]{1,0:T(8,128)S(1)} %get-tuple-element.40), channel_id=1, source_target_pairs={{0,1},{1,0},{2,3},{3,2},{4,5},{5,4},{6,7},{7,6},{8,9},{9,8},{10,11... | collective-permute-start | bytes 196616 | tf_op jit(solution)/shard_map/ppermute | solution.py:359
  35.1 1.0 %collective-permute-start.5 = (f32[8,128]{1,0:T(8,128)S(1)}, f32[8,128]{1,0:T(8,128)S(1)}, u32[]{:S(2)}, u32[]{:S(2)}) collective-permute-start(f32[8,128]{1,0:T(8,128)S(1)} %add.21), channel_id=1, source_target_pairs={{0,20},{1,21},{2,22},{3,23},{4,16},{5,17},{6,18},{7,19},{8,28},{9,... | collective-permute-start | bytes 12296 | tf_op jit(solution)/shard_map/ppermute | solution.py:359
  36.1 2.1 %collective-permute-done.5 = f32[8,128]{1,0:T(8,128)S(1)} collective-permute-done((f32[8,128]{1,0:T(8,128)S(1)}, f32[8,128]{1,0:T(8,128)S(1)}, u32[]{:S(2)}, u32[]{:S(2)}) %collective-permute-start.5) | collective-permute-done | bytes 4128 | tf_op jit(solution)/shard_map/ppermute | solution.py:359
  38.2 0.0 collective-permute-done.6.part_0
  38.2 1.2 %collective-permute-start.9 = (f32[8,128]{1,0:T(8,128)S(1)}, f32[8,128]{1,0:T(8,128)S(1)}, u32[]{:S(2)}, u32[]{:S(2)}) collective-permute-start(f32[8,128]{1,0:T(8,128)S(1)} %add.22), channel_id=1, source_target_pairs={{0,5},{1,4},{2,7},{3,6},{4,1},{5,0},{6,3},{7,2},{8,13},{9,12},{10,... | collective-permute-start | bytes 12296 | tf_op jit(solution)/shard_map/ppermute | solution.py:359
  39.3 1.8 %collective-permute-done.9 = f32[8,128]{1,0:T(8,128)S(1)} collective-permute-done((f32[8,128]{1,0:T(8,128)S(1)}, f32[8,128]{1,0:T(8,128)S(1)}, u32[]{:S(2)}, u32[]{:S(2)}) %collective-permute-start.9) | collective-permute-done | bytes 4128 | tf_op jit(solution)/shard_map/ppermute | solution.py:359
  41.2 1.8 %collective-permute-start.10 = (f32[8,128]{1,0:T(8,128)S(1)}, f32[8,128]{1,0:T(8,128)S(1)}, u32[]{:S(2)}, u32[]{:S(2)}) collective-permute-start(f32[8,128]{1,0:T(8,128)S(1)} %add.23.half_v), channel_id=1, source_target_pairs={{0,6},{1,7},{2,4},{3,5},{4,2},{5,3},{6,0},{7,1},{8,14},{9,15},{10,... | collective-permute-start | bytes 12296 | tf_op jit(solution)/shard_map/ppermute | solution.py:359
  43.0 0.0 collective-permute-done.7.part_1
  43.0 0.0 collective-permute-done.8.part_2
  43.0 1.4 %own_flows.1.after_h = f32[256,256]{1,0:T(8,128)} custom-call(s32[4]{0:T(128)S(1)} %pad_add_fusion.blocks_s, f32[64,256]{1,0:T(8,128)S(1)} %collective-permute-done.6.part_0, f32[64,256]{1,0:T(8,128)S(1)} %collective-permute-done.7.part_1, f32[64,256]{1,0:T(8,128)S(1)} %collective-permute-done.8.part_2, f32[64,256]{1,0:T(8,128)S(1)} %get-tuple-element.41.part_3), custom_call_target="tpu_custom_call" | custom-call | tf_op jit(solution)/shard_map/own_flows/pallas_call | solution.py:302
  44.4 0.7 %collective-permute-done.10.other_v = f32[8,128]{1,0:T(8,128)S(1)} collective-permute-done((f32[8,128]{1,0:T(8,128)S(1)}, f32[8,128]{1,0:T(8,128)S(1)}, u32[]{:S(2)}, u32[]{:S(2)}) %collective-permute-start.10) | collective-permute-done | bytes 4128 | tf_op jit(solution)/shard_map/ppermute | solution.py:359
  45.1 1.5 %last_outputs.1 = (f32[2,128]{1,0:T(2,128)}, f32[2,128]{1,0:T(2,128)}, f32[4,128]{1,0:T(4,128)}) custom-call(f32[256,256]{1,0:T(8,128)} %own_flows.1.after_h, s32[4]{0:T(128)S(1)} %pad_add_fusion.blocks_s, f32[8,128]{1,0:T(8,128)S(1)} %add.23.half_v, f32[8,128]{1,0:T(8,128)S(1)} %collective-permute-done.10.other_v, f32[8,128]{1,0:T(8,128)S(1)} %get-tuple-element.43.like_v, ...), custom_call_target="tpu_custom_call" | custom-call | tf_op jit(solution)/shard_map/last_outputs/pallas_call | solution.py:337
  (13 shorter events, 0.1 us)
Async XLA Ops:
  0.6 13.6 %copy-start.4 = (s32[256]{0:T(256)S(1)}, s32[256]{0:T(256)}, u32[]{:S(2)}) copy-start(s32[256]{0:T(256)} %param.13) | copy-start | bytes 3076
  0.6 22.1 %copy-start = (f32[512]{0:T(512)S(1)}, f32[512]{0:T(512)}, u32[]{:S(2)}) copy-start(f32[512]{0:T(512)} %param.17) | copy-start | bytes 6148
  0.7 22.1 %copy-start.1 = (f32[512,512]{1,0:T(8,128)S(1)}, f32[512,512]{1,0:T(8,128)}, u32[]{:S(2)}) copy-start(f32[512,512]{1,0:T(8,128)} %c_v.1) | copy-start | bytes 3145732
  0.7 22.1 %copy-start.3 = (s32[8,512]{1,0:T(8,128)S(1)}, s32[8,512]{1,0:T(8,128)}, u32[]{:S(2)}) copy-start(s32[8,512]{1,0:T(8,128)} %s_v.1) | copy-start | bytes 49156
  0.7 22.1 %copy-start.2 = (s32[30,512]{1,0:T(8,128)S(1)}, s32[30,512]{1,0:T(8,128)}, u32[]{:S(2)}) copy-start(s32[30,512]{1,0:T(8,128)} %d_v.1) | copy-start | bytes 184324
  11.1 7.5 %collective-permute-start.1 = (f32[264,128]{1,0:T(8,128)S(1)}, f32[264,128]{1,0:T(8,128)S(1)}, u32[]{:S(2)}, u32[]{:S(2)}) collective-permute-start(f32[264,128]{1,0:T(8,128)S(1)} %get-tuple-element.29), channel_id=1, source_target_pairs={{0,1},{1,0},{2,3},{3,2},{4,5},{5,4},{6,7},{7,6},{8,9},{9,8},{10,11... | collective-permute-start | bytes 405512 | tf_op jit(solution)/shard_map/ppermute | solution.py:359
  14.2 14.6 %collective-permute-start = (f32[264,128]{1,0:T(8,128)S(1)}, f32[264,128]{1,0:T(8,128)S(1)}, u32[]{:S(2)}, u32[]{:S(2)}) collective-permute-start(f32[264,128]{1,0:T(8,128)S(1)} %get-tuple-element.27), channel_id=1, source_target_pairs={{0,1},{1,0},{2,3},{3,2},{4,5},{5,4},{6,7},{7,6},{8,9},{9,8},{10,11... | collective-permute-start | bytes 405512 | tf_op jit(solution)/shard_map/ppermute | solution.py:359
  18.6 10.1 %collective-permute-start.2 = (f32[264,128]{1,0:T(8,128)S(1)}, f32[264,128]{1,0:T(8,128)S(1)}, u32[]{:S(2)}, u32[]{:S(2)}) collective-permute-start(f32[264,128]{1,0:T(8,128)S(1)} %add.18), channel_id=1, source_target_pairs={{0,3},{1,2},{2,1},{3,0},{4,7},{5,6},{6,5},{7,4},{8,11},{9,10},{10,... | collective-permute-start | bytes 405512 | tf_op jit(solution)/shard_map/ppermute | solution.py:359
  30.2 1.2 %collective-permute-start.3 = (f32[8,128]{1,0:T(8,128)S(1)}, f32[8,128]{1,0:T(8,128)S(1)}, u32[]{:S(2)}, u32[]{:S(2)}) collective-permute-start(f32[8,128]{1,0:T(8,128)S(1)} %get-tuple-element.32), channel_id=1, source_target_pairs={{0,4},{1,5},{2,6},{3,7},{4,0},{5,1},{6,2},{7,3},{8,12},{9,13},{10,... | collective-permute-start | bytes 12296 | tf_op jit(solution)/shard_map/ppermute | solution.py:359
  30.3 7.9 %collective-permute-start.6 = (f32[64,256]{1,0:T(8,128)S(1)}, f32[64,256]{1,0:T(8,128)S(1)}, u32[]{:S(2)}, u32[]{:S(2)}) collective-permute-start(f32[64,256]{1,0:T(8,128)S(1)} %get-tuple-element.37), channel_id=1, source_target_pairs={{0,2},{1,3},{2,0},{3,1},{4,6},{5,7},{6,4},{7,5},{8,10},{9,11},{10,... | collective-permute-start | bytes 196616 | tf_op jit(solution)/shard_map/ppermute | solution.py:359
  31.5 3.0 %collective-permute-start.4 = (f32[8,128]{1,0:T(8,128)S(1)}, f32[8,128]{1,0:T(8,128)S(1)}, u32[]{:S(2)}, u32[]{:S(2)}) collective-permute-start(f32[8,128]{1,0:T(8,128)S(1)} %add.20), channel_id=1, source_target_pairs={{0,12},{1,13},{2,14},{3,15},{4,8},{5,9},{6,10},{7,11},{8,4},{9,5},... | collective-permute-start | bytes 12296 | tf_op jit(solution)/shard_map/ppermute | solution.py:359
  32.7 10.3 %collective-permute-start.7 = (f32[64,256]{1,0:T(8,128)S(1)}, f32[64,256]{1,0:T(8,128)S(1)}, u32[]{:S(2)}, u32[]{:S(2)}) collective-permute-start(f32[64,256]{1,0:T(8,128)S(1)} %get-tuple-element.39), channel_id=1, source_target_pairs={{0,3},{1,2},{2,1},{3,0},{4,7},{5,6},{6,5},{7,4},{8,11},{9,10},{10,... | collective-permute-start | bytes 196616 | tf_op jit(solution)/shard_map/ppermute | solution.py:359
  34.5 8.5 %collective-permute-start.8 = (f32[64,256]{1,0:T(8,128)S(1)}, f32[64,256]{1,0:T(8,128)S(1)}, u32[]{:S(2)}, u32[]{:S(2)}) collective-permute-start(f32[64,256]{1,0:T(8,128)S(1)} %get-tuple-element.40), channel_id=1, source_target_pairs={{0,1},{1,0},{2,3},{3,2},{4,5},{5,4},{6,7},{7,6},{8,9},{9,8},{10,11... | collective-permute-start | bytes 196616 | tf_op jit(solution)/shard_map/ppermute | solution.py:359
  35.1 3.0 %collective-permute-start.5 = (f32[8,128]{1,0:T(8,128)S(1)}, f32[8,128]{1,0:T(8,128)S(1)}, u32[]{:S(2)}, u32[]{:S(2)}) collective-permute-start(f32[8,128]{1,0:T(8,128)S(1)} %add.21), channel_id=1, source_target_pairs={{0,20},{1,21},{2,22},{3,23},{4,16},{5,17},{6,18},{7,19},{8,28},{9,... | collective-permute-start | bytes 12296 | tf_op jit(solution)/shard_map/ppermute | solution.py:359
  38.2 3.0 %collective-permute-start.9 = (f32[8,128]{1,0:T(8,128)S(1)}, f32[8,128]{1,0:T(8,128)S(1)}, u32[]{:S(2)}, u32[]{:S(2)}) collective-permute-start(f32[8,128]{1,0:T(8,128)S(1)} %add.22), channel_id=1, source_target_pairs={{0,5},{1,4},{2,7},{3,6},{4,1},{5,0},{6,3},{7,2},{8,13},{9,12},{10,... | collective-permute-start | bytes 12296 | tf_op jit(solution)/shard_map/ppermute | solution.py:359
  41.2 3.9 %collective-permute-start.10 = (f32[8,128]{1,0:T(8,128)S(1)}, f32[8,128]{1,0:T(8,128)S(1)}, u32[]{:S(2)}, u32[]{:S(2)}) collective-permute-start(f32[8,128]{1,0:T(8,128)S(1)} %add.23.half_v), channel_id=1, source_target_pairs={{0,6},{1,7},{2,4},{3,5},{4,2},{5,3},{6,0},{7,1},{8,14},{9,15},{10,... | collective-permute-start | bytes 12296 | tf_op jit(solution)/shard_map/ppermute | solution.py:359
